TPU v7x, 256 devices: a whole 4x4x8 slice. The times are simulated.
256 devices in a mesh: gx: 8 (over x, core), gy: 32 (over y, z).
Axes of the slice: x: 4, y: 4, z: 8, core: 2. Of those that a mesh axis runs over, the one named last changes fastest.
Arguments:
- initial: float32 [64, 256, 512], P('gx', 'gy'), may hold values from -4 to 4
- right_side: float32 [64, 256, 512], P('gx', 'gy'), may hold values from -4 to 4
- phase_map: int32 [64, 256, 512], P('gx', 'gy'), may hold values from 0 to 2
- phase_table: float32 [3], replicated, may hold values from 0.2 to 5
Outputs:
- updated: float32 [64, 256, 512], P('gx', 'gy')
All inputs are finite; a program needn't handle non-finite values.
Results may differ from a plain program's by a relative error of at most 0.0001.
Values sent between devices are 32-bit elements; how exact they have to be, the bound alone decides.
No kernel may reach another device: no remote copies, remote signals or barrier semaphores. Data moves between devices by JAX's collectives and lax.ppermute only.
A program may use at most 64 MiB of HBM per device.

v0:
```python
import functools

import jax
import jax.numpy as jnp
from jax import lax
from jax.experimental import pallas as pl
from jax.experimental.pallas import tpu as pltpu
from jax.sharding import PartitionSpec as P

F32 = jnp.float32
KEEP = 0.2
OMEGA = 0.8
VMEM = pltpu.VMEM
PARAMS = pltpu.CompilerParams(vmem_limit_bytes=48 * 1024 * 1024)


def roll(value, shift, axis):
    return pltpu.roll(value, shift % value.shape[axis], axis)


def iota(shape, dim):
    return lax.broadcasted_iota(jnp.int32, shape, dim)


def pair_sum_matrix():
    return (iota((256, 128), 0) // 2 == iota((256, 128), 1)).astype(F32)


def pair_copy_matrix():
    return (iota((128, 256), 1) // 2 == iota((128, 256), 0)).astype(F32)


def exact_dot(a, b):
    return lax.dot_general(
        a, b, (((1,), (0,)), ((), ())), precision=lax.Precision.HIGHEST, preferred_element_type=F32
    )


def lane_sum(value, matrix):
    width = value.shape[1]
    parts = [exact_dot(value[:, at : at + 256], matrix) for at in range(0, width, 256)]
    return parts[0] if len(parts) == 1 else jnp.concatenate(parts, axis=1)


def lane_copy(value, matrix):
    width = value.shape[1]
    parts = [exact_dot(value[:, at : at + 128], matrix) for at in range(0, width, 128)]
    return parts[0] if len(parts) == 1 else jnp.concatenate(parts, axis=1)


def row_sum(scratch, value):
    rows, width = value.shape
    parts = []
    for c in range(width // 128):
        scratch[c, 0:rows] = value[:, 128 * c : 128 * c + 128]
        first = scratch[c, pl.ds(0, rows // 2, stride=2)]
        parts.append(first + scratch[c, pl.ds(1, rows // 2, stride=2)])
    return parts[0] if len(parts) == 1 else jnp.concatenate(parts, axis=1)


def row_copy(scratch, value):
    rows, width = value.shape
    parts = []
    for c in range(width // 128):
        part = value[:, 128 * c : 128 * c + 128]
        scratch[c, pl.ds(0, rows, stride=2)] = part
        scratch[c, pl.ds(1, rows, stride=2)] = part
        parts.append(scratch[c, 0 : 2 * rows])
    return parts[0] if len(parts) == 1 else jnp.concatenate(parts, axis=1)


def gathered(mid, low, high, cx_low, cx, cy, cz):
    total = cx * high + cx_low * low
    total = total + cy * roll(mid, -1, 0) + roll(cy * mid, 1, 0)
    return total + cz * roll(mid, -1, 1) + roll(cz * mid, 1, 1)


def z_neighbours(mid):
    lane = iota(mid.shape, 1)
    last = mid.shape[1] - 1
    up = jnp.where(lane == last, 0.0, roll(mid, -1, 1))
    down = jnp.where(lane == 0, 0.0, roll(mid, 1, 1))
    return up, down


def diagonal(mid, low, high):
    up, down = z_neighbours(mid)
    total = low + high + roll(mid, -1, 0) + roll(mid, 1, 0) + up + down
    return 3.0 * mid + 0.5 * total


def coupling_y(mid):
    return 0.5 * (mid + roll(mid, -1, 0))


def coupling_z(mid):
    lane = iota(mid.shape, 1)
    return jnp.where(lane == mid.shape[1] - 1, 0.0, 0.5 * (mid + roll(mid, -1, 1)))


def edge_flags(at, grid):
    even = at % 2 == 0
    outside = jnp.logical_or(at == 0, at == grid - 1)
    return even, outside


def start_kernel(
    where_ref, table_hbm, phase_hbm, init_hbm, rhs_hbm,
    kap_ref, init_ref, rhs_ref, near_ref, far_ref, yeven_ref, yodd_ref,
    table_ref, phase_ref, sems,
):
    copies = [
        pltpu.make_async_copy(source, target, sems.at[i])
        for i, (source, target) in enumerate(
            ((table_hbm, table_ref), (phase_hbm, phase_ref), (init_hbm, init_ref), (rhs_hbm, rhs_ref))
        )
    ]
    for copy in copies:
        copy.start()
    for copy in copies:
        copy.wait()
    even = where_ref[0] % 2 == 0
    for x in range(8):
        phase = phase_ref[x]
        kap_ref[x] = jnp.where(
            phase == 0, table_ref[0], jnp.where(phase == 1, table_ref[1], table_ref[2])
        )
    for ref, side in ((near_ref, even), (far_ref, jnp.logical_not(even))):
        deep = jnp.where(side, 5, 0)
        shallow = jnp.where(side, 6, 0)
        for i in range(3):
            ref[i] = kap_ref[deep + i]
            ref[3 + i] = init_ref[deep + i]
        for i in range(2):
            ref[6 + i] = rhs_ref[shallow + i]

    def write(low_ref, high_ref):
        for x in range(8):
            low_ref[x, 0:3] = kap_ref[x, 0:3]
            low_ref[x, 3:6] = init_ref[x, 0:3]
            low_ref[x, 6:8] = rhs_ref[x, 0:2]
            high_ref[x, 0:3] = kap_ref[x, 5:8]
            high_ref[x, 3:6] = init_ref[x, 5:8]
            high_ref[x, 6:8] = rhs_ref[x, 6:8]

    by_parity(where_ref, yeven_ref, yodd_ref, write)


def by_parity(where_ref, even_ref, odd_ref, write):
    even = where_ref[1] % 2 == 0

    @pl.when(even)
    def _():
        write(odd_ref, even_ref)

    @pl.when(jnp.logical_not(even))
    def _():
        write(even_ref, odd_ref)


def y_tiles(where_ref, grid, even_ref, odd_ref, p):
    even, outside = edge_flags(where_ref[1], grid)
    inner = even_ref[p]
    outer = jnp.where(outside, 0.0, odd_ref[p])
    return jnp.where(even, inner, outer), jnp.where(even, outer, inner)


def corner_messages(nx, ny, yeven, yodd):
    even = lax.axis_index("gx") % 2 == 0
    high, low = both_tiles(ny, yeven, yodd)
    top = jnp.concatenate([high[7:8], high[6:7], low[7:8], low[6:7]], axis=0)
    bottom = jnp.concatenate([high[0:2], low[0:2]], axis=0)
    return jnp.where(even, top, bottom), jnp.where(even, bottom, top)


def both_tiles(ny, yeven, yodd):
    at = lax.axis_index("gy")
    even, outside = edge_flags(at, ny)
    outer = jnp.where(outside, 0.0, yodd)
    return jnp.where(even, yeven, outer), jnp.where(even, outer, yeven)


class Planes:
    def __init__(self, middle, outer, first, count):
        self.middle, self.outer, self.first, self.count = middle, outer, first, count

    def find(self, p):
        if p < self.first:
            return self.outer, p
        if p < self.first + self.count:
            return self.middle, p - self.first
        return self.outer, p - self.count

    def __getitem__(self, p):
        ref, at = self.find(p)
        return ref[at]

    def __setitem__(self, p, value):
        ref, at = self.find(p)
        ref[at] = value


def setup0(ks, cx, cy, cz, wi, planes, faces):
    for p in faces:
        cx[p] = 0.5 * (ks[p] + ks[p + 1])
    for p in planes:
        mid = ks[p]
        cy[p] = coupling_y(mid)
        cz[p] = coupling_z(mid)
        diag = diagonal(mid, ks[p - 1], ks[p + 1])
        wi[p] = jnp.where(mid > 0.0, OMEGA / jnp.where(mid > 0.0, diag, 1.0), 0.0)


def sweep0(source, target, rs, cx, cy, cz, wi, planes):
    for p in planes:
        mid = source[p]
        total = gathered(mid, source[p - 1], source[p + 1], cx[p - 1], cx[p], cy[p], cz[p])
        target[p] = KEEP * mid + wi[p] * (rs[p] + total)


def rest0(v2, rs, ks, cx, cy, cz, p):
    mid = v2[p]
    total = gathered(mid, v2[p - 1], v2[p + 1], cx[p - 1], cx[p], cy[p], cz[p])
    diag = diagonal(ks[p], ks[p - 1], ks[p + 1])
    return (rs[p] + total - diag * mid)[0:8]


def add_y_halo(ks, vs, rs, p, high, low):
    zero = jnp.zeros((8, 512), F32)
    ks[p, 8:16] = zero
    vs[p, 8:16] = zero
    rs[p, 8:16] = zero
    ks[p, 8:11] = high[0:3]
    ks[p, 13:16] = low[0:3]
    vs[p, 8:11] = high[3:6]
    vs[p, 13:16] = low[3:6]
    rs[p, 8:10] = high[6:8]
    rs[p, 14:16] = low[6:8]


def early0_kernel(
    ny, where_ref, kap_ref, init_ref, rhs_ref, even_ref, odd_ref,
    ks, vs, rs, cx, cy, cz, wi, v1, v2, rest,
):
    for x in range(8):
        ks[x, 0:8] = kap_ref[x]
        vs[x, 0:8] = init_ref[x]
        rs[x, 0:8] = rhs_ref[x]
        add_y_halo(ks, vs, rs, x, *y_tiles(where_ref, ny, even_ref, odd_ref, x))
    ks, vs, rs = (Planes(ref, None, 3, 8) for ref in (ks, vs, rs))
    cx = Planes(cx, None, 3, 7)
    cy, cz, wi, v1 = (Planes(ref, None, 4, 6) for ref in (cy, cz, wi, v1))
    v2 = Planes(v2, None, 5, 4)
    setup0(ks, cx, cy, cz, wi, range(4, 10), range(3, 10))
    sweep0(vs, v1, rs, cx, cy, cz, wi, range(4, 10))
    sweep0(v1, v2, rs, cx, cy, cz, wi, range(5, 9))
    for p in (6, 7):
        rest[p - 6] = rest0(v2, rs, ks, cx, cy, cz, p)


def down0_kernel(
    nx, ny, where_ref, near_ref, far_ref, cnear_ref, cfar_ref,
    ks_own, vs_own, rs_own, cx_own, cy_own, cz_own, wi_own, v1_own, v2_own, rest_own,
    v0_ref, rs, cx, cy, cz, wi, block_ref, mnear_ref, mfar_ref, meven_ref, modd_ref,
    ks, vs, v1, v2, pair, fine, coarse,
):
    even, outside = edge_flags(where_ref[0], nx)
    for i in range(3):
        near_at = jnp.where(even, 3 + i, i)
        far_at = jnp.where(even, i, 3 + i)
        for ref, first in ((ks, 0), (vs, 3)):
            ref[near_at, 0:8] = near_ref[first + i]
            ref[far_at, 0:8] = jnp.where(outside, 0.0, far_ref[first + i])
    for i in range(2):
        rs[jnp.where(even, 3 + i, 1 + i), 0:8] = near_ref[6 + i]
        rs[jnp.where(even, 1 + i, 3 + i), 0:8] = jnp.where(outside, 0.0, far_ref[6 + i])
    zero = jnp.zeros((8, 512), F32)
    for p in (0, 5):
        ks[p, 8:16] = zero
        vs[p, 8:16] = zero
        rs[p, 8:16] = zero
    rs[0, 0:8] = zero
    rs[5, 0:8] = zero
    for i in range(2):
        add_y_halo(ks, vs, rs, jnp.where(even, 3 + i, 2 - i), cnear_ref[i], cnear_ref[2 + i])
        add_y_halo(
            ks, vs, rs, jnp.where(even, 2 - i, 3 + i),
            jnp.where(outside, 0.0, cfar_ref[i]), jnp.where(outside, 0.0, cfar_ref[2 + i]),
        )
    ks, vs, rs = (Planes(a, b, 3, 8) for a, b in ((ks_own, ks), (vs_own, vs), (rs_own, rs)))
    cx = Planes(cx_own, cx, 3, 7)
    cy, cz, wi, v1 = (
        Planes(a, b, 4, 6) for a, b in ((cy_own, cy), (cz_own, cz), (wi_own, wi), (v1_own, v1))
    )
    v2 = Planes(v2_own, v2, 5, 4)
    setup0(ks, cx, cy, cz, wi, (1, 2, 3, 10, 11, 12), (0, 1, 2, 10, 11, 12))
    sweep0(vs, v1, rs, cx, cy, cz, wi, (1, 2, 3, 10, 11, 12))
    sweep0(v1, v2, rs, cx, cy, cz, wi, (2, 3, 4, 9, 10, 11))
    for p in range(3, 11, 2):
        both = None
        for q in (p, p + 1):
            rest = rest_own[q - 6] if q in (6, 7) else rest0(v2, rs, ks, cx, cy, cz, q)
            both = rest if both is None else both + rest
            v0_ref[q - 3] = v2[q][0:8]
        at = 2 * (p - 3)
        fine[at : at + 4] = row_sum(pair, both)
    for p in range(1, 13, 2):
        at = 12 + 4 * p
        fine[at : at + 8] = row_sum(pair, ks[p] + ks[p + 1])
    coarse[...] = lane_sum(fine[...], pair_sum_matrix())
    for x in range(4):
        half = pl.ds(256 * (x % 2), 256)
        mid = 0.125 * coarse[24 + 8 * x : 32 + 8 * x]
        low = 0.125 * coarse[16 + 8 * x : 24 + 8 * x]
        high = 0.125 * coarse[32 + 8 * x : 40 + 8 * x]
        block_ref[x // 2, 0:4, half] = 0.5 * coarse[4 * x : 4 * x + 4]
        block_ref[x // 2, 4:8, half] = mid[0:4]
        at = 4 * (x // 2)
        block_ref[2, at : at + 4, half] = (OMEGA / diagonal(mid, low, high)[0:4])
    for ref, side in ((mnear_ref, even), (mfar_ref, jnp.logical_not(even))):
        shallow = jnp.where(side, 6, 0)
        for i in range(3):
            ref[i] = block_ref[i]
        for i in range(2):
            ref[3 + i] = v0_ref[shallow + i]

    def write(low_ref, high_ref):
        for i in range(3):
            low_ref[i] = block_ref[i]
            high_ref[i] = block_ref[i]
        for x in range(8):
            at = 2 * (x % 4)
            low_ref[3 + x // 4, at : at + 2] = v0_ref[x, 0:2]
            high_ref[3 + x // 4, at : at + 2] = v0_ref[x, 6:8]

    by_parity(where_ref, meven_ref, modd_ref, write)


def corner1_message(ny, meven, modd):
    high, low = both_tiles(ny, meven, modd)
    rows = [high[4:5, 6:8], low[4:5, 6:8], high[3:4, 0:2], low[3:4, 0:2]]
    return jnp.concatenate([high[0:3], low[0:3], jnp.concatenate(rows, axis=1)], axis=0)


def down1_kernel(
    nx, ny, where_ref, block_ref, v0_ref, near_ref, far_ref, meven_ref, modd_ref,
    cnear_ref, cfar_ref,
    v0x, v1, f1, w1, cx, cy, cz, send_ref,
    k1, u1, pair, fine,
):
    even, outside = edge_flags(where_ref[0], nx)

    def inside(value):
        return jnp.where(outside, 0.0, value)

    near = [near_ref[i] for i in range(3)]
    far = [inside(far_ref[i]) for i in range(3)]
    cnear = [cnear_ref[i] for i in range(7)]
    cfar = [inside(cfar_ref[i]) for i in range(7)]
    mine = [y_tiles(where_ref, ny, meven_ref, modd_ref, i) for i in range(5)]

    def pick(a, b):
        return [jnp.where(even, p, q) for p, q in zip(a, b)]

    blocks = (
        (pick(far, near), pick(cfar[0:3], cnear[0:3]), pick(cfar[3:6], cnear[3:6])),
        ([block_ref[i] for i in range(3)], [t[0] for t in mine], [t[1] for t in mine]),
        (pick(near, far), pick(cnear[0:3], cfar[0:3]), pick(cnear[3:6], cfar[3:6])),
    )
    zero = jnp.zeros((4, 256), F32)
    for b in range(3):
        for x in range(4):
            p = 4 * b + x
            half = slice(256 * (x % 2), 256 * (x % 2) + 256)
            t = x // 2
            for ref, at, row in (
                (f1, t, slice(0, 4)), (k1, t, slice(4, 8)), (w1, 2, slice(4 * t, 4 * t + 4))
            ):
                ref[p, 0:4] = blocks[b][0][at][row, half]
                ref[p, 4:8] = blocks[b][1][at][row, half]
                ref[p, 8:12] = zero
                ref[p, 12:16] = blocks[b][2][at][row, half]
    blank = jnp.zeros((8, 512), F32)
    for p in range(12):
        v0x[p, 8:16] = blank
    for x in range(8):
        v0x[2 + x, 0:8] = v0_ref[x]
        at = 2 * (x % 4)
        v0x[2 + x, 8:10] = mine[3 + x // 4][0][at : at + 2]
        v0x[2 + x, 14:16] = mine[3 + x // 4][1][at : at + 2]
    near_at = jnp.where(even, 10, 0)
    far_at = jnp.where(even, 0, 10)
    for i in range(2):
        v0x[near_at + i, 0:8] = near_ref[3 + i]
        v0x[far_at + i, 0:8] = inside(far_ref[3 + i])
    low_tile = jnp.where(even, cfar[6], cnear[6])
    high_tile = jnp.where(even, cnear[6], cfar[6])
    for at, tile, row in ((1, low_tile, 0), (10, high_tile, 4)):
        v0x[at, 8:10] = tile[row : row + 2]
        v0x[at, 14:16] = tile[row + 2 : row + 4]
    for p in range(12):
        u1[p] = w1[p] * f1[p]
        if p < 11:
            cx[p] = 0.5 * (k1[p] + k1[p + 1])
        cy[p] = coupling_y(k1[p])
        cz[p] = coupling_z(k1[p])
    for p in range(1, 11):
        mid = u1[p]
        total = gathered(mid, u1[p - 1], u1[p + 1], cx[p - 1], cx[p], cy[p], cz[p])
        v1[p] = KEEP * mid + w1[p] * (f1[p] + total)
    for p in range(4, 8, 2):
        both = None
        for q in (p, p + 1):
            mid = v1[q]
            total = gathered(mid, v1[q - 1], v1[q + 1], cx[q - 1], cx[q], cy[q], cz[q])
            diag = diagonal(k1[q], k1[q - 1], k1[q + 1])
            rest = (f1[q] + total - diag * mid)[0:8]
            both = rest if both is None else both + rest
        at = p - 4
        fine[at : at + 2] = 0.5 * row_sum(pair, both)[0:2]
        kept = k1[p, 0:8] + k1[p + 1, 0:8]
        fine[4 + at : 6 + at] = 0.125 * row_sum(pair, kept)[0:2]
    tile = lane_sum(fine[...], pair_sum_matrix())
    for i in range(send_ref.shape[0]):
        send_ref[i] = tile


def up_kernel(
    nx, ny, where_ref, *refs
):
    half = nx // 2
    columns = (refs[:half], refs[half : 2 * half])
    own, far = refs[nx : nx + 5], refs[nx + 5 : nx + 10]
    rs = Planes(own[0], far[0], 3, 8)
    cx0 = Planes(own[1], far[1], 3, 7)
    cy0, cz0, w0 = (Planes(a, b, 4, 6) for a, b in zip(own[2:], far[2:]))
    up_levels(nx, ny, where_ref, columns, rs, cx0, cy0, cz0, w0, *refs[nx + 10 :])


def up_levels(
    nx, ny, where_ref, columns, rs, cx0, cy0, cz0, w0, v1, f1, w1, cx1, cy1, cz1, v0x, out_ref,
    f2, k2, cx2, cyi, cyo, cz2, w2, d2, u2, v2, e2, f3, k3, cx3, cy3, cz3, w3, edge3, ga, gb,
    small, wide, e1a, e1b, narrow, e0a, e0b,
):
    gx = where_ref[0]
    gy = where_ref[1]
    core = gx % 2
    n2 = 2 * nx
    zero = jnp.zeros((ny, 128), F32)
    row = iota((ny, 128), 0)
    lane = iota((ny, 128), 1)
    last_row = row == ny - 1
    for s in range(2):
        k2[0, s] = zero
        k2[n2 + 1, s] = zero
        u2[0, s] = zero
        u2[n2 + 1, s] = zero
        v2[0, s] = zero
        v2[n2 + 1, s] = zero
    for j in range(nx // 2):
        chip = (gx // 2) ^ j
        for refs, which in ((columns[0], core), (columns[1], 1 - core)):
            for i in range(2):
                p = 4 * chip + 2 * which + i + 1
                for s in range(2):
                    f2[p, s] = refs[j][2 * i + s]
                    k2[p, s] = refs[j][4 + 2 * i + s]
    for p in range(n2 + 1):
        for s in range(2):
            cx2[p, s] = 0.5 * (k2[p, s] + k2[p + 1, s])
    for p in range(1, n2 + 1):
        k_low, k_high = k2[p, 0], k2[p, 1]
        after = jnp.where(last_row, 0.0, roll(k_low, -1, 0))
        before = jnp.where(row == 0, 0.0, roll(k_high, 1, 0))
        cyi[p] = 0.5 * (k_low + k_high)
        cyo[p] = jnp.where(last_row, 0.0, 0.5 * (k_high + after))
        for s, mid, ya, yb in ((0, k_low, k_high, before), (1, k_high, k_low, after)):
            up, down = z_neighbours(mid)
            cz2[p, s] = jnp.where(lane == 127, 0.0, 0.5 * (mid + up))
            diag = 3.0 * mid + 0.5 * (k2[p - 1, s] + k2[p + 1, s] + ya + yb + up + down)
            scale = OMEGA / diag
            d2[p, s] = diag
            w2[p, s] = scale
            u2[p, s] = scale * f2[p, s]

    def gather2(ref, p):
        low, high = ref[p, 0], ref[p, 1]
        sums = []
        for s, mid in ((0, low), (1, high)):
            total = cx2[p, s] * ref[p + 1, s] + cx2[p - 1, s] * ref[p - 1, s]
            total = total + cz2[p, s] * roll(mid, -1, 1) + roll(cz2[p, s] * mid, 1, 1)
            sums.append(total)
        sums[0] = sums[0] + cyi[p] * high + roll(cyo[p] * high, 1, 0)
        sums[1] = sums[1] + cyi[p] * low + cyo[p] * roll(low, -1, 0)
        return (low, high), sums

    def sweep2(source, target):
        for p in range(1, n2 + 1):
            mids, sums = gather2(source, p)
            for s in range(2):
                target[p, s] = KEEP * mids[s] + w2[p, s] * (f2[p, s] + sums[s])

    sweep2(u2, v2)
    even_lane = lane % 2 == 0

    def pair_lanes(value):
        return value + jnp.where(even_lane, roll(value, -1, 1), roll(value, 1, 1))

    k3[0] = zero
    k3[nx + 1] = zero
    ga[0] = zero
    ga[nx + 1] = zero
    gb[0] = zero
    gb[nx + 1] = zero
    for x in range(nx):
        both = None
        kept = None
        for p in (2 * x + 1, 2 * x + 2):
            mids, sums = gather2(v2, p)
            for s in range(2):
                rest = f2[p, s] + sums[s] - d2[p, s] * mids[s]
                both = rest if both is None else both + rest
                kept = k2[p, s] if kept is None else kept + k2[p, s]
        f3[x + 1] = 0.5 * pair_lanes(both)
        k3[x + 1] = 0.125 * pair_lanes(kept)
    for p in range(nx + 1):
        cx3[p] = 0.5 * (k3[p] + k3[p + 1])
    edge_total = zero
    rest_total = zero
    outer = (
        (row == 0).astype(F32) + last_row.astype(F32)
        + (lane < 2).astype(F32) + (lane >= 126).astype(F32)
    )
    for p in range(1, nx + 1):
        mid = k3[p]
        after = jnp.where(last_row, 0.0, roll(mid, -1, 0))
        before = jnp.where(row == 0, 0.0, roll(mid, 1, 0))
        up = jnp.where(lane >= 126, 0.0, roll(mid, -2, 1))
        down = jnp.where(lane < 2, 0.0, roll(mid, 2, 1))
        cy3[p] = jnp.where(last_row, 0.0, 0.5 * (mid + after))
        cz3[p] = jnp.where(lane >= 126, 0.0, 0.5 * (mid + up))
        diag = 3.0 * mid + 0.5 * (k3[p - 1] + k3[p + 1] + after + before + up + down)
        scale = OMEGA / diag
        w3[p] = scale
        ga[p] = scale * f3[p]
        faces = outer + (1.0 if p == 1 else 0.0) + (1.0 if p == nx else 0.0)
        edge = 0.5 * mid * faces
        edge3[p] = edge
        edge_total = edge_total + edge
        rest_total = rest_total + f3[p]

    def gather3(ref, p):
        mid = ref[p]
        total = cx3[p] * ref[p + 1] + cx3[p - 1] * ref[p - 1]
        total = total + cy3[p] * roll(mid, -1, 0) + roll(cy3[p] * mid, 1, 0)
        return mid, total + cz3[p] * roll(mid, -2, 1) + roll(cz3[p] * mid, 2, 1)

    source, target = ga, gb
    for _ in range(7):
        for p in range(1, nx + 1):
            mid, total = gather3(source, p)
            target[p] = KEEP * mid + w3[p] * (f3[p] + total)
        source, target = target, source
    for p in range(1, nx + 1):
        rest_total = rest_total - edge3[p] * source[p]

    def whole(value):
        return jnp.sum(jnp.sum(value, axis=0, keepdims=True), axis=1, keepdims=True)

    shift = whole(rest_total) / whole(edge_total)
    first_row = jnp.clip(gy - 3, 0, ny - 8)
    rows = pl.ds(first_row, 8)
    no_wrap = iota((8, 128), 0) < 7
    planes = []
    for j in range(10):
        x = 2 * gx - 4 + j
        planes.append((jnp.logical_and(x >= 0, x < n2), jnp.clip(x, 0, n2 - 1)))
    level = []
    for ok, q in planes:
        e3 = source[q // 2 + 1, rows] + shift
        level.append([jnp.where(ok, v2[q + 1, s, rows] + e3, 0.0) for s in range(2)])
    for first, last in ((1, 8), (2, 7)):
        done = list(level)
        for j in range(first, last + 1):
            ok, q = planes[j]
            low, high = level[j]
            inner = cyi[q + 1, rows]
            after = jnp.where(no_wrap, cyo[q + 1, rows], 0.0)
            sums = [inner * high + roll(after * high, 1, 0), inner * low + after * roll(low, -1, 0)]
            for s in range(2):
                mid = level[j][s]
                cz = cz2[q + 1, s, rows]
                total = sums[s] + cz * roll(mid, -1, 1) + roll(cz * mid, 1, 1)
                total = total + cx2[q + 1, s, rows] * level[j + 1][s]
                total = total + cx2[q, s, rows] * level[j - 1][s]
                value = KEEP * mid + w2[q + 1, s, rows] * (f2[q + 1, s, rows] + total)
                done[j] = [jnp.where(ok, value, 0.0)] if s == 0 else done[j] + [jnp.where(ok, value, 0.0)]
        level = done
    copies = pair_copy_matrix()
    at = gy - first_row
    steps = (
        (0, at, None),
        (2, jnp.minimum(at + 1, 7), gy < ny - 1),
        (6, jnp.maximum(at - 1, 0), gy > 0),
    )
    for i in range(6):
        small[8 * i + 4 : 8 * i + 6] = jnp.zeros((2, 128), F32)
        for s in range(2):
            e2[i, s] = level[i + 2][s]
            for j, r, ok in steps:
                line = e2[i, s, pl.ds(r, 1)]
                small[8 * i + j + s : 8 * i + j + s + 1] = (
                    line if ok is None else jnp.where(ok, line, 0.0)
                )
    wide[...] = lane_copy(small[...], copies)
    for i in range(6):
        spread = row_copy(narrow, wide[8 * i : 8 * i + 8])
        for p in (2 * i, 2 * i + 1):
            if 1 <= p <= 10:
                e1a[p] = v1[p] + spread
    for source, target, first, last in ((e1a, e1b, 2, 9), (e1b, e1a, 3, 8)):
        for p in range(first, last + 1):
            mid = source[p]
            total = gathered(
                mid, source[p - 1], source[p + 1], cx1[p - 1], cx1[p], cy1[p], cz1[p]
            )
            target[p] = KEEP * mid + w1[p] * (f1[p] + total)
    row8 = iota((8, 256), 0)
    for i in range(6):
        value = e1a[i + 3]
        wide[8 * i : 8 * i + 8] = jnp.where(row8 == 7, value[8:16], value[0:8])
    doubled = lane_copy(wide[...], copies)
    for i in range(6):
        spread = row_copy(narrow, doubled[8 * i : 8 * i + 8])
        for p in (2 * i, 2 * i + 1):
            e0a[p] = v0x[p] + spread
    for p in range(1, 11):
        mid = e0a[p]
        total = gathered(
            mid, e0a[p - 1], e0a[p + 1], cx0[p], cx0[p + 1], cy0[p + 1], cz0[p + 1]
        )
        e0b[p] = KEEP * mid + w0[p + 1] * (rs[p + 1] + total)
    for p in range(2, 10):
        mid = e0b[p]
        total = gathered(
            mid, e0b[p - 1], e0b[p + 1], cx0[p], cx0[p + 1], cy0[p + 1], cz0[p + 1]
        )
        out_ref[p - 2] = (KEEP * mid + w0[p + 1] * (rs[p + 1] + total))[0:8]


def run(kernel, outs, scratch, where, *operands, space=VMEM, cost=None):
    return pl.pallas_call(
        kernel,
        out_shape=[jax.ShapeDtypeStruct(shape, F32) for shape in outs],
        in_specs=[pl.BlockSpec(memory_space=pltpu.SMEM)]
        + [pl.BlockSpec(memory_space=space)] * len(operands),
        out_specs=[pl.BlockSpec(memory_space=VMEM)] * len(outs),
        scratch_shapes=[VMEM(s, F32) if isinstance(s, tuple) else s for s in scratch],
        compiler_params=PARAMS,
        cost_estimate=cost,
    )(where, *operands)


def body(initial, right_side, phase_map, phase_table):
    nx, ny = lax.axis_size("gx"), lax.axis_size("gy")
    where = jnp.stack([lax.axis_index("gx"), lax.axis_index("gy")]).astype(jnp.int32)

    def pairs(partner):
        return [
            (x * ny + y, px * ny + py)
            for x in range(nx)
            for y in range(ny)
            for px, py in [partner(x, y)]
        ]

    def beyond(at, size):
        other = at + 1 if at % 2 else at - 1
        return other if 0 <= other < size else None

    def far_x(x, y):
        other = beyond(x, nx)
        return (x, y ^ 1) if other is None else (other, y)

    def far_y(x, y):
        other = beyond(y, ny)
        return (x ^ 1, y) if other is None else (x, other)

    both = ("gx", "gy")

    def swap_x(near, far):
        return (
            lax.ppermute(near, both, pairs(lambda x, y: (x ^ 1, y))),
            lax.ppermute(far, both, pairs(far_x)),
        )

    def swap_y(near, far):
        return (
            lax.ppermute(near, both, pairs(lambda x, y: (x, y ^ 1))),
            lax.ppermute(far, both, pairs(far_y)),
        )

    inputs = [
        pltpu.with_memory_space_constraint(value, pltpu.HBM)
        for value in (phase_table, phase_map, initial, right_side)
    ]
    early_cost = pl.CostEstimate(flops=20_000_000, bytes_accessed=4_000_000, transcendentals=0)
    tile0 = (8, 512)
    ring0 = (16, 512)
    ring1 = (16, 256)
    kappa, init, rhs, near, far, yeven, yodd = run(
        start_kernel, [(8,) + tile0] * 7,
        [pltpu.SMEM((3,), F32), VMEM((8,) + tile0, jnp.int32), pltpu.SemaphoreType.DMA((4,))],
        where, *inputs, space=pltpu.HBM,
    )
    yeven, yodd = swap_y(yeven, yodd)
    near, far = swap_x(near, far)
    yodd, yeven, far, near = lax.optimization_barrier((yodd, yeven, far, near))
    cnear, cfar = swap_x(*corner_messages(nx, ny, yeven, yodd))
    ksx, vsx, rsx, cxx, cyx, czx, wix, v1x, v2x, restx = run(
        functools.partial(early0_kernel, ny),
        [(8,) + ring0] * 3 + [(7,) + ring0] + [(6,) + ring0] * 4 + [(4,) + ring0, (2,) + tile0],
        [], where, kappa, init, rhs, yeven, yodd, cost=early_cost,
    )
    v0, rs, cx0, cy0, cz0, w0, block, mnear, mfar, meven, modd = run(
        functools.partial(down0_kernel, nx, ny),
        [(8,) + tile0]
        + [(6,) + ring0, (6,) + ring0]
        + [(8,) + ring0] * 3
        + [(3,) + tile0]
        + [(5,) + tile0] * 4,
        [(6,) + ring0] * 2 + [(8,) + ring0, (10,) + ring0, (4, 16, 128), (64, 512), (64, 256)],
        where, near, far, cnear, cfar,
        ksx, vsx, rsx, cxx, cyx, czx, wix, v1x, v2x, restx,
    )
    meven, modd = swap_y(meven, modd)
    mnear, mfar = swap_x(mnear, mfar)
    modd, meven, mfar, mnear = lax.optimization_barrier((modd, meven, mfar, mnear))
    corner = corner1_message(ny, meven, modd)
    cnear, cfar = swap_x(corner, corner)
    v0x, v1, f1, w1, cx1, cy1, cz1, send = run(
        functools.partial(down1_kernel, nx, ny),
        [(12,) + ring0] + [(12,) + ring1] * 6 + [(ny, 8, 128)],
        [(12,) + ring1, (12,) + ring1, (4, 16, 128), (8, 256)],
        where, block, v0, mnear, mfar, meven, modd, cnear, cfar,
    )
    column = jnp.transpose(lax.all_to_all(send, "gy", 0, 0), (1, 0, 2))

    def chips_apart(j):
        return pairs(lambda x, y: (((x // 2) ^ j) * 2 + x % 2, y))

    mine = [column] + [lax.ppermute(column, both, chips_apart(j)) for j in range(1, nx // 2)]
    other = [lax.ppermute(c, both, pairs(lambda x, y: (x ^ 1, y))) for c in mine]
    n2 = 2 * nx
    pair2 = (n2 + 2, 2, ny, 128)
    one2 = (n2 + 2, ny, 128)
    one3 = (nx + 2, ny, 128)
    (out,) = run(
        functools.partial(up_kernel, nx, ny), [(8,) + tile0],
        [pair2, pair2, pair2, one2, one2, pair2, pair2, pair2, pair2, pair2, (6, 2, 8, 128)]
        + [one3] * 9
        + [(48, 128), (48, 256), (12,) + ring1, (12,) + ring1, (4, 16, 128), (12,) + ring0, (12,) + ring0],
        where, *mine, *other, rsx, cxx, cyx, czx, wix, rs, cx0, cy0, cz0, w0,
        v1, f1, w1, cx1, cy1, cz1, v0x,
    )
    return out


def solution(mesh):
    return jax.shard_map(
        body,
        mesh=mesh,
        in_specs=(P("gx", "gy", None), P("gx", "gy", None), P("gx", "gy", None), P()),
        out_specs=P("gx", "gy", None),
        check_vma=False,
    )
```

profile of v0, /device:TPU:1, one launch (start us, length us, event | category | flops | bytes accessed | tf_op | source)
XLA Modules:
  0.0 67.1 jit_solution(15444787432592475030)
XLA Ops:
  0.0 0.1 pad_add_fusion.where_ref
  0.1 1.7 %shard_map.46 = (f32[8,8,512]{2,1,0:T(8,128)S(1)}, f32[8,8,512]{2,1,0:T(8,128)S(1)}, f32[8,8,512]{2,1,0:T(8,128)S(1)}, f32[8,8,512]{2,1,0:T(8,128)S(1)}, f32[8,8...) custom-call(s32[2]{0:T(128)S(1)} %pad_add_fusion.where_ref, f32[3]{0:T(128)} %table_hbm.1, ...), custom_call_target="tpu_custom_call" | custom-call | tf_op jit(solution)/shard_map/pallas_call | solution.py:652
  1.8 3.3 %collective-permute-start = (f32[8,8,512]{2,1,0:T(8,128)S(1)}, f32[8,8,512]{2,1,0:T(8,128)S(1)}, u32[]{:S(2)}, u32[]{:S(2)}) collective-permute-start(f32[8,8,512]{2,1,0:T(8,128)S(1)} %get-tuple-element.49), channel_id=1, source_target_pairs={{0,32},{1,2},{2,1},{3,4},{4,3},{5,6},{6,5},{7,8},{8,7},{9,10},{10,... | collective-permute-start | bytes 393224 | tf_op jit(solution)/shard_map/ppermute | solution.py:699
  5.1 0.9 %collective-permute-start.1 = (f32[8,8,512]{2,1,0:T(8,128)S(1)}, f32[8,8,512]{2,1,0:T(8,128)S(1)}, u32[]{:S(2)}, u32[]{:S(2)}) collective-permute-start(f32[8,8,512]{2,1,0:T(8,128)S(1)} %get-tuple-element.50), channel_id=1, source_target_pairs={{0,1},{1,0},{2,3},{3,2},{4,5},{5,4},{6,7},{7,6},{8,9},{9,8},{10,11... | collective-permute-start | bytes 393224 | tf_op jit(solution)/shard_map/ppermute | solution.py:698
  6.0 2.3 %collective-permute-start.2 = (f32[8,8,512]{2,1,0:T(8,128)S(1)}, f32[8,8,512]{2,1,0:T(8,128)S(1)}, u32[]{:S(2)}, u32[]{:S(2)}) collective-permute-start(f32[8,8,512]{2,1,0:T(8,128)S(1)} %get-tuple-element.51), channel_id=1, source_target_pairs={{0,1},{1,0},{2,3},{3,2},{4,5},{5,4},{6,7},{7,6},{8,9},{9,8},{10,11... | collective-permute-start | bytes 393224 | tf_op jit(solution)/shard_map/ppermute | solution.py:693
  8.3 0.0 collective-permute-start.3
  8.3 0.0 collective-permute-done.odd_ref
  8.3 1.9 %collective-permute-done.1.even_ref = f32[8,8,512]{2,1,0:T(8,128)S(1)} collective-permute-done((f32[8,8,512]{2,1,0:T(8,128)S(1)}, f32[8,8,512]{2,1,0:T(8,128)S(1)}, u32[]{:S(2)}, u32[]{:S(2)}) %collective-permute-start.1) | collective-permute-done | bytes 131104 | tf_op jit(solution)/shard_map/ppermute | solution.py:698
  10.2 1.1 %collective-permute-done.2.far_ref = f32[8,8,512]{2,1,0:T(8,128)S(1)} collective-permute-done((f32[8,8,512]{2,1,0:T(8,128)S(1)}, f32[8,8,512]{2,1,0:T(8,128)S(1)}, u32[]{:S(2)}, u32[]{:S(2)}) %collective-permute-start.2) | collective-permute-done | bytes 131104 | tf_op jit(solution)/shard_map/ppermute | solution.py:693
  11.3 0.0 collective-permute-done.3.near_ref
  11.4 1.5 %collective-permute-start.5 = (f32[4,8,512]{2,1,0:T(8,128)S(1)}, f32[4,8,512]{2,1,0:T(8,128)S(1)}, u32[]{:S(2)}, u32[]{:S(2)}) collective-permute-start(f32[4,8,512]{2,1,0:T(8,128)S(1)} %get-tuple-element.97), channel_id=1, source_target_pairs={{0,1},{1,0},{2,3},{3,2},{4,5},{5,4},{6,7},{7,6},{8,9},{9,8},{10,11... | collective-permute-start | bytes 196616 | tf_op jit(solution)/shard_map/ppermute | solution.py:693
  12.9 0.9 %collective-permute-start.4 = (f32[4,8,512]{2,1,0:T(8,128)S(1)}, f32[4,8,512]{2,1,0:T(8,128)S(1)}, u32[]{:S(2)}, u32[]{:S(2)}) collective-permute-start(f32[4,8,512]{2,1,0:T(8,128)S(1)} %get-tuple-element.98), channel_id=1, source_target_pairs={{0,32},{1,33},{2,34},{3,35},{4,36},{5,37},{6,38},{7,39},{8,40},{9,... | collective-permute-start | bytes 196616 | tf_op jit(solution)/shard_map/ppermute | solution.py:692
  13.8 1.2 %shard_map.47 = (f32[8,16,512]{2,1,0:T(8,128)S(1)}, f32[8,16,512]{2,1,0:T(8,128)S(1)}, f32[8,16,512]{2,1,0:T(8,128)S(1)}, f32[7,16,512]{2,1,0:T(8,128)S(1)}, f32...) custom-call(s32[2]{0:T(128)S(1)} %pad_add_fusion.where_ref, ...), custom_call_target="tpu_custom_call" | custom-call | flops 20000000 | bytes 4000000 | tf_op jit(solution)/shard_map/pallas_call | solution.py:652
  15.0 0.1 collective-permute-done.5.cfar_ref
  15.1 0.0 collective-permute-done.4.cnear_ref
  15.1 1.7 %shard_map.48 = (f32[8,8,512]{2,1,0:T(8,128)S(1)}, f32[6,16,512]{2,1,0:T(8,128)S(1)}, f32[6,16,512]{2,1,0:T(8,128)S(1)}, f32[8,16,512]{2,1,0:T(8,128)S(1)}, f32[...) custom-call(s32[2]{0:T(128)S(1)} %pad_add_fusion.where_ref, ...), custom_call_target="tpu_custom_call" | custom-call | tf_op jit(solution)/shard_map/pallas_call | solution.py:652
  16.9 1.9 %collective-permute-start.6 = (f32[5,8,512]{2,1,0:T(8,128)S(1)}, f32[5,8,512]{2,1,0:T(8,128)S(1)}, u32[]{:S(2)}, u32[]{:S(2)}) collective-permute-start(f32[5,8,512]{2,1,0:T(8,128)S(1)} %get-tuple-element.72), channel_id=1, source_target_pairs={{0,32},{1,2},{2,1},{3,4},{4,3},{5,6},{6,5},{7,8},{8,7},{9,10},{10,... | collective-permute-start | bytes 245768 | tf_op jit(solution)/shard_map/ppermute | solution.py:699
  18.7 2.7 %collective-permute-start.7 = (f32[5,8,512]{2,1,0:T(8,128)S(1)}, f32[5,8,512]{2,1,0:T(8,128)S(1)}, u32[]{:S(2)}, u32[]{:S(2)}) collective-permute-start(f32[5,8,512]{2,1,0:T(8,128)S(1)} %get-tuple-element.73), channel_id=1, source_target_pairs={{0,1},{1,0},{2,3},{3,2},{4,5},{5,4},{6,7},{7,6},{8,9},{9,8},{10,11... | collective-permute-start | bytes 245768 | tf_op jit(solution)/shard_map/ppermute | solution.py:698
  21.4 2.0 %collective-permute-start.8 = (f32[5,8,512]{2,1,0:T(8,128)S(1)}, f32[5,8,512]{2,1,0:T(8,128)S(1)}, u32[]{:S(2)}, u32[]{:S(2)}) collective-permute-start(f32[5,8,512]{2,1,0:T(8,128)S(1)} %get-tuple-element.74), channel_id=1, source_target_pairs={{0,1},{1,0},{2,3},{3,2},{4,5},{5,4},{6,7},{7,6},{8,9},{9,8},{10,11... | collective-permute-start | bytes 245768 | tf_op jit(solution)/shard_map/ppermute | solution.py:693
  23.5 0.1 collective-permute-start.9
  23.5 0.0 collective-permute-done.6.modd_ref
  23.6 0.0 collective-permute-done.7.meven_ref
  23.6 2.0 %collective-permute-done.8.far_ref = f32[5,8,512]{2,1,0:T(8,128)S(1)} collective-permute-done((f32[5,8,512]{2,1,0:T(8,128)S(1)}, f32[5,8,512]{2,1,0:T(8,128)S(1)}, u32[]{:S(2)}, u32[]{:S(2)}) %collective-permute-start.8) | collective-permute-done | bytes 81952 | tf_op jit(solution)/shard_map/ppermute | solution.py:693
  25.6 0.0 collective-permute-done.9.near_ref
  25.7 1.8 %collective-permute-start.11 = (f32[7,8,512]{2,1,0:T(8,128)S(1)}, f32[7,8,512]{2,1,0:T(8,128)S(1)}, u32[]{:S(2)}, u32[]{:S(2)}) collective-permute-start(f32[7,8,512]{2,1,0:T(8,128)S(1)} %maximum_maximum_fusion), channel_id=1, source_target_pairs={{0,1},{1,0},{2,3},{3,2},{4,5},{5,4},{6,7},{7,6},{8,9},{9,8},{10,11... | collective-permute-start | bytes 344072 | tf_op jit(solution)/shard_map/ppermute | solution.py:693
  27.5 1.5 %collective-permute-start.10 = (f32[7,8,512]{2,1,0:T(8,128)S(1)}, f32[7,8,512]{2,1,0:T(8,128)S(1)}, u32[]{:S(2)}, u32[]{:S(2)}) collective-permute-start(f32[7,8,512]{2,1,0:T(8,128)S(1)} %maximum_maximum_fusion), channel_id=1, source_target_pairs={{0,32},{1,33},{2,34},{3,35},{4,36},{5,37},{6,38},{7,39},{8,40},{9,... | collective-permute-start | bytes 344072 | tf_op jit(solution)/shard_map/ppermute | solution.py:692
  29.0 1.0 %collective-permute-done.11.cfar_ref = f32[7,8,512]{2,1,0:T(8,128)S(1)} collective-permute-done((f32[7,8,512]{2,1,0:T(8,128)S(1)}, f32[7,8,512]{2,1,0:T(8,128)S(1)}, u32[]{:S(2)}, u32[]{:S(2)}) %collective-permute-start.11) | collective-permute-done | bytes 114720 | tf_op jit(solution)/shard_map/ppermute | solution.py:693
  30.0 0.0 collective-permute-done.10.cnear_ref
  30.0 1.1 %shard_map.49 = (f32[12,16,512]{2,1,0:T(8,128)S(1)}, f32[12,16,256]{2,1,0:T(8,128)S(1)}, f32[12,16,256]{2,1,0:T(8,128)S(1)}, f32[12,16,256]{2,1,0:T(8,128)S(1)},...) custom-call(s32[2]{0:T(128)S(1)} %pad_add_fusion.where_ref, ...), custom_call_target="tpu_custom_call" | custom-call | tf_op jit(solution)/shard_map/pallas_call | solution.py:652
  31.1 17.0 %all_to_all.5 = f32[32,8,128]{2,1,0:T(8,128)S(1)} all-to-all(f32[32,8,128]{2,1,0:T(8,128)S(1)} %get-tuple-element.80), channel_id=1, replica_groups=mesh['gx'=8,'gy'=32] {'gy'}, dimensions={0} | all-to-all | bytes 262144 | tf_op jit(solution)/shard_map/all_to_all | solution.py:746
  48.2 2.4 %collective-permute-start.14 = (f32[8,32,128]{2,1,0:T(8,128)S(1)}, f32[8,32,128]{2,1,0:T(8,128)S(1)}, u32[]{:S(2)}, u32[]{:S(2)}) collective-permute-start(f32[8,32,128]{2,1,0:T(8,128)S(1)} %bitcast.5), channel_id=1, source_target_pairs={{0,192},{1,193},{2,194},{3,195},{4,196},{5,197},{6,198},{7,199},{8... | collective-permute-start | bytes 393224 | tf_op jit(solution)/shard_map/ppermute | solution.py:751
  50.6 0.7 %collective-permute-start.13 = (f32[8,32,128]{2,1,0:T(8,128)S(1)}, f32[8,32,128]{2,1,0:T(8,128)S(1)}, u32[]{:S(2)}, u32[]{:S(2)}) collective-permute-start(f32[8,32,128]{2,1,0:T(8,128)S(1)} %bitcast.6), channel_id=1, source_target_pairs={{0,128},{1,129},{2,130},{3,131},{4,132},{5,133},{6,134},{7,135},{8... | collective-permute-start | bytes 393224 | tf_op jit(solution)/shard_map/ppermute | solution.py:751
  51.4 0.2 collective-permute-start.12
  51.5 5.1 %collective-permute-start.15 = (f32[8,32,128]{2,1,0:T(8,128)S(1)}, f32[8,32,128]{2,1,0:T(8,128)S(1)}, u32[]{:S(2)}, u32[]{:S(2)}) collective-permute-start(f32[8,32,128]{2,1,0:T(8,128)S(1)} %bitcast.8), channel_id=1, source_target_pairs={{0,32},{1,33},{2,34},{3,35},{4,36},{5,37},{6,38},{7,39},{8,40},{9,... | collective-permute-start | bytes 393224 | tf_op jit(solution)/shard_map/ppermute | solution.py:752
  56.7 0.0 collective-permute-done.14.refs_3_
  56.7 2.1 %collective-permute-start.18 = (f32[8,32,128]{2,1,0:T(8,128)S(1)}, f32[8,32,128]{2,1,0:T(8,128)S(1)}, u32[]{:S(2)}, u32[]{:S(2)}) collective-permute-start(f32[8,32,128]{2,1,0:T(8,128)S(1)} %collective-permute-done.14.refs_3_), channel_id=1, source_target_pairs={{0,32},{1,33},{2,34},{3,35},{4,36},{5,37},{6,38},{7,39},{8,40},{9,... | collective-permute-start | bytes 393224 | tf_op jit(solution)/shard_map/ppermute | solution.py:752
  58.7 0.0 collective-permute-done.13.refs_2_
  58.7 1.5 %collective-permute-start.17 = (f32[8,32,128]{2,1,0:T(8,128)S(1)}, f32[8,32,128]{2,1,0:T(8,128)S(1)}, u32[]{:S(2)}, u32[]{:S(2)}) collective-permute-start(f32[8,32,128]{2,1,0:T(8,128)S(1)} %collective-permute-done.13.refs_2_), channel_id=1, source_target_pairs={{0,32},{1,33},{2,34},{3,35},{4,36},{5,37},{6,38},{7,39},{8,40},{9,... | collective-permute-start | bytes 393224 | tf_op jit(solution)/shard_map/ppermute | solution.py:752
  60.2 0.0 collective-permute-done.12.refs_1_
  60.2 0.8 %collective-permute-start.16 = (f32[8,32,128]{2,1,0:T(8,128)S(1)}, f32[8,32,128]{2,1,0:T(8,128)S(1)}, u32[]{:S(2)}, u32[]{:S(2)}) collective-permute-start(f32[8,32,128]{2,1,0:T(8,128)S(1)} %collective-permute-done.12.refs_1_), channel_id=1, source_target_pairs={{0,32},{1,33},{2,34},{3,35},{4,36},{5,37},{6,38},{7,39},{8,40},{9,... | collective-permute-start | bytes 393224 | tf_op jit(solution)/shard_map/ppermute | solution.py:752
  61.0 0.0 collective-permute-done.15.refs_4_
  61.0 0.0 collective-permute-done.18.refs_7_
  61.0 0.2 collective-permute-done.17.refs_6_
  61.2 0.8 %collective-permute-done.16.refs_5_ = f32[8,32,128]{2,1,0:T(8,128)S(1)} collective-permute-done((f32[8,32,128]{2,1,0:T(8,128)S(1)}, f32[8,32,128]{2,1,0:T(8,128)S(1)}, u32[]{:S(2)}, u32[]{:S(2)}) %collective-permute-start.16) | collective-permute-done | bytes 131104 | tf_op jit(solution)/shard_map/ppermute | solution.py:752
  62.0 5.1 %shard_map.50 = f32[8,8,512]{2,1,0:T(8,128)} custom-call(s32[2]{0:T(128)S(1)} %pad_add_fusion.where_ref, f32[8,32,128]{2,1,0:T(8,128)S(1)} %bitcast.9, f32[8,32,128]{2,1,0:T(8,128)S(1)} %collective-permute-done.12.refs_1_, f32[8,32,128]{2,1,0:T(8,128)S(1)} %collective-permute-done.13.refs_2_, f32[8,32,128]{2,1,0:T(8,128)S(1)} %collective-permute-done.14.refs_3_, ...), custom_call_target="tpu_custom_call" | custom-call | tf_op jit(solution)/shard_map/pallas_call | solution.py:652
  (12 shorter events, 0.1 us)
Async XLA Ops:
  1.8 6.5 %collective-permute-start = (f32[8,8,512]{2,1,0:T(8,128)S(1)}, f32[8,8,512]{2,1,0:T(8,128)S(1)}, u32[]{:S(2)}, u32[]{:S(2)}) collective-permute-start(f32[8,8,512]{2,1,0:T(8,128)S(1)} %get-tuple-element.49), channel_id=1, source_target_pairs={{0,32},{1,2},{2,1},{3,4},{4,3},{5,6},{6,5},{7,8},{8,7},{9,10},{10,... | collective-permute-start | bytes 393224 | tf_op jit(solution)/shard_map/ppermute | solution.py:699
  5.1 5.1 %collective-permute-start.1 = (f32[8,8,512]{2,1,0:T(8,128)S(1)}, f32[8,8,512]{2,1,0:T(8,128)S(1)}, u32[]{:S(2)}, u32[]{:S(2)}) collective-permute-start(f32[8,8,512]{2,1,0:T(8,128)S(1)} %get-tuple-element.50), channel_id=1, source_target_pairs={{0,1},{1,0},{2,3},{3,2},{4,5},{5,4},{6,7},{7,6},{8,9},{9,8},{10,11... | collective-permute-start | bytes 393224 | tf_op jit(solution)/shard_map/ppermute | solution.py:698
  6.0 5.3 %collective-permute-start.2 = (f32[8,8,512]{2,1,0:T(8,128)S(1)}, f32[8,8,512]{2,1,0:T(8,128)S(1)}, u32[]{:S(2)}, u32[]{:S(2)}) collective-permute-start(f32[8,8,512]{2,1,0:T(8,128)S(1)} %get-tuple-element.51), channel_id=1, source_target_pairs={{0,1},{1,0},{2,3},{3,2},{4,5},{5,4},{6,7},{7,6},{8,9},{9,8},{10,11... | collective-permute-start | bytes 393224 | tf_op jit(solution)/shard_map/ppermute | solution.py:693
  8.3 2.9 %collective-permute-start.3 = (f32[8,8,512]{2,1,0:T(8,128)S(1)}, f32[8,8,512]{2,1,0:T(8,128)S(1)}, u32[]{:S(2)}, u32[]{:S(2)}) collective-permute-start(f32[8,8,512]{2,1,0:T(8,128)S(1)} %get-tuple-element.52), channel_id=1, source_target_pairs={{0,32},{1,33},{2,34},{3,35},{4,36},{5,37},{6,38},{7,39},{8,40},{9,... | collective-permute-start | bytes 393224 | tf_op jit(solution)/shard_map/ppermute | solution.py:692
  11.4 3.8 %collective-permute-start.5 = (f32[4,8,512]{2,1,0:T(8,128)S(1)}, f32[4,8,512]{2,1,0:T(8,128)S(1)}, u32[]{:S(2)}, u32[]{:S(2)}) collective-permute-start(f32[4,8,512]{2,1,0:T(8,128)S(1)} %get-tuple-element.97), channel_id=1, source_target_pairs={{0,1},{1,0},{2,3},{3,2},{4,5},{5,4},{6,7},{7,6},{8,9},{9,8},{10,11... | collective-permute-start | bytes 196616 | tf_op jit(solution)/shard_map/ppermute | solution.py:693
  12.9 2.2 %collective-permute-start.4 = (f32[4,8,512]{2,1,0:T(8,128)S(1)}, f32[4,8,512]{2,1,0:T(8,128)S(1)}, u32[]{:S(2)}, u32[]{:S(2)}) collective-permute-start(f32[4,8,512]{2,1,0:T(8,128)S(1)} %get-tuple-element.98), channel_id=1, source_target_pairs={{0,32},{1,33},{2,34},{3,35},{4,36},{5,37},{6,38},{7,39},{8,40},{9,... | collective-permute-start | bytes 196616 | tf_op jit(solution)/shard_map/ppermute | solution.py:692
  16.9 6.7 %collective-permute-start.6 = (f32[5,8,512]{2,1,0:T(8,128)S(1)}, f32[5,8,512]{2,1,0:T(8,128)S(1)}, u32[]{:S(2)}, u32[]{:S(2)}) collective-permute-start(f32[5,8,512]{2,1,0:T(8,128)S(1)} %get-tuple-element.72), channel_id=1, source_target_pairs={{0,32},{1,2},{2,1},{3,4},{4,3},{5,6},{6,5},{7,8},{8,7},{9,10},{10,... | collective-permute-start | bytes 245768 | tf_op jit(solution)/shard_map/ppermute | solution.py:699
  18.7 4.8 %collective-permute-start.7 = (f32[5,8,512]{2,1,0:T(8,128)S(1)}, f32[5,8,512]{2,1,0:T(8,128)S(1)}, u32[]{:S(2)}, u32[]{:S(2)}) collective-permute-start(f32[5,8,512]{2,1,0:T(8,128)S(1)} %get-tuple-element.73), channel_id=1, source_target_pairs={{0,1},{1,0},{2,3},{3,2},{4,5},{5,4},{6,7},{7,6},{8,9},{9,8},{10,11... | collective-permute-start | bytes 245768 | tf_op jit(solution)/shard_map/ppermute | solution.py:698
  21.4 4.1 %collective-permute-start.8 = (f32[5,8,512]{2,1,0:T(8,128)S(1)}, f32[5,8,512]{2,1,0:T(8,128)S(1)}, u32[]{:S(2)}, u32[]{:S(2)}) collective-permute-start(f32[5,8,512]{2,1,0:T(8,128)S(1)} %get-tuple-element.74), channel_id=1, source_target_pairs={{0,1},{1,0},{2,3},{3,2},{4,5},{5,4},{6,7},{7,6},{8,9},{9,8},{10,11... | collective-permute-start | bytes 245768 | tf_op jit(solution)/shard_map/ppermute | solution.py:693
  23.5 2.1 %collective-permute-start.9 = (f32[5,8,512]{2,1,0:T(8,128)S(1)}, f32[5,8,512]{2,1,0:T(8,128)S(1)}, u32[]{:S(2)}, u32[]{:S(2)}) collective-permute-start(f32[5,8,512]{2,1,0:T(8,128)S(1)} %get-tuple-element.75), channel_id=1, source_target_pairs={{0,32},{1,33},{2,34},{3,35},{4,36},{5,37},{6,38},{7,39},{8,40},{9,... | collective-permute-start | bytes 245768 | tf_op jit(solution)/shard_map/ppermute | solution.py:692
  25.7 4.3 %collective-permute-start.11 = (f32[7,8,512]{2,1,0:T(8,128)S(1)}, f32[7,8,512]{2,1,0:T(8,128)S(1)}, u32[]{:S(2)}, u32[]{:S(2)}) collective-permute-start(f32[7,8,512]{2,1,0:T(8,128)S(1)} %maximum_maximum_fusion), channel_id=1, source_target_pairs={{0,1},{1,0},{2,3},{3,2},{4,5},{5,4},{6,7},{7,6},{8,9},{9,8},{10,11... | collective-permute-start | bytes 344072 | tf_op jit(solution)/shard_map/ppermute | solution.py:693
  27.5 2.5 %collective-permute-start.10 = (f32[7,8,512]{2,1,0:T(8,128)S(1)}, f32[7,8,512]{2,1,0:T(8,128)S(1)}, u32[]{:S(2)}, u32[]{:S(2)}) collective-permute-start(f32[7,8,512]{2,1,0:T(8,128)S(1)} %maximum_maximum_fusion), channel_id=1, source_target_pairs={{0,32},{1,33},{2,34},{3,35},{4,36},{5,37},{6,38},{7,39},{8,40},{9,... | collective-permute-start | bytes 344072 | tf_op jit(solution)/shard_map/ppermute | solution.py:692
  48.2 8.5 %collective-permute-start.14 = (f32[8,32,128]{2,1,0:T(8,128)S(1)}, f32[8,32,128]{2,1,0:T(8,128)S(1)}, u32[]{:S(2)}, u32[]{:S(2)}) collective-permute-start(f32[8,32,128]{2,1,0:T(8,128)S(1)} %bitcast.5), channel_id=1, source_target_pairs={{0,192},{1,193},{2,194},{3,195},{4,196},{5,197},{6,198},{7,199},{8... | collective-permute-start | bytes 393224 | tf_op jit(solution)/shard_map/ppermute | solution.py:751
  50.6 8.1 %collective-permute-start.13 = (f32[8,32,128]{2,1,0:T(8,128)S(1)}, f32[8,32,128]{2,1,0:T(8,128)S(1)}, u32[]{:S(2)}, u32[]{:S(2)}) collective-permute-start(f32[8,32,128]{2,1,0:T(8,128)S(1)} %bitcast.6), channel_id=1, source_target_pairs={{0,128},{1,129},{2,130},{3,131},{4,132},{5,133},{6,134},{7,135},{8... | collective-permute-start | bytes 393224 | tf_op jit(solution)/shard_map/ppermute | solution.py:751
  51.4 8.8 %collective-permute-start.12 = (f32[8,32,128]{2,1,0:T(8,128)S(1)}, f32[8,32,128]{2,1,0:T(8,128)S(1)}, u32[]{:S(2)}, u32[]{:S(2)}) collective-permute-start(f32[8,32,128]{2,1,0:T(8,128)S(1)} %bitcast.7), channel_id=1, source_target_pairs={{0,64},{1,65},{2,66},{3,67},{4,68},{5,69},{6,70},{7,71},{8,72},{9,... | collective-permute-start | bytes 393224 | tf_op jit(solution)/shard_map/ppermute | solution.py:751
  51.5 9.5 %collective-permute-start.15 = (f32[8,32,128]{2,1,0:T(8,128)S(1)}, f32[8,32,128]{2,1,0:T(8,128)S(1)}, u32[]{:S(2)}, u32[]{:S(2)}) collective-permute-start(f32[8,32,128]{2,1,0:T(8,128)S(1)} %bitcast.8), channel_id=1, source_target_pairs={{0,32},{1,33},{2,34},{3,35},{4,36},{5,37},{6,38},{7,39},{8,40},{9,... | collective-permute-start | bytes 393224 | tf_op jit(solution)/shard_map/ppermute | solution.py:752
  56.7 4.3 %collective-permute-start.18 = (f32[8,32,128]{2,1,0:T(8,128)S(1)}, f32[8,32,128]{2,1,0:T(8,128)S(1)}, u32[]{:S(2)}, u32[]{:S(2)}) collective-permute-start(f32[8,32,128]{2,1,0:T(8,128)S(1)} %collective-permute-done.14.refs_3_), channel_id=1, source_target_pairs={{0,32},{1,33},{2,34},{3,35},{4,36},{5,37},{6,38},{7,39},{8,40},{9,... | collective-permute-start | bytes 393224 | tf_op jit(solution)/shard_map/ppermute | solution.py:752
  58.7 2.4 %collective-permute-start.17 = (f32[8,32,128]{2,1,0:T(8,128)S(1)}, f32[8,32,128]{2,1,0:T(8,128)S(1)}, u32[]{:S(2)}, u32[]{:S(2)}) collective-permute-start(f32[8,32,128]{2,1,0:T(8,128)S(1)} %collective-permute-done.13.refs_2_), channel_id=1, source_target_pairs={{0,32},{1,33},{2,34},{3,35},{4,36},{5,37},{6,38},{7,39},{8,40},{9,... | collective-permute-start | bytes 393224 | tf_op jit(solution)/shard_map/ppermute | solution.py:752
  60.2 1.8 %collective-permute-start.16 = (f32[8,32,128]{2,1,0:T(8,128)S(1)}, f32[8,32,128]{2,1,0:T(8,128)S(1)}, u32[]{:S(2)}, u32[]{:S(2)}) collective-permute-start(f32[8,32,128]{2,1,0:T(8,128)S(1)} %collective-permute-done.12.refs_1_), channel_id=1, source_target_pairs={{0,32},{1,33},{2,34},{3,35},{4,36},{5,37},{6,38},{7,39},{8,40},{9,... | collective-permute-start | bytes 393224 | tf_op jit(solution)/shard_map/ppermute | solution.py:752
where the time goes:
time: 67.2 us; the launch traced here: 67.1 us
  starting transfers between devices  31.7 us (47%)
  blocking collectives  17 us (25%)
  Pallas kernels  10.8 us (16%)
  waiting for transfers between devices  7.1 us (11%)
    all_to_all x1, blocking collectives, body(): column = jnp.transpose(lax.all_to_all(send, 'gy', 0, 0), (1, 0, 2))  17 us
    pallas_call x5, Pallas kernels, run(): pl.pallas_call(kernel, out_shape=[jax.ShapeDtypeStruct(shape, F32) for sh...  10.8 us
    ppermute x4, starting transfers between devices, body(): lax.ppermute(c, both, pairs(lambda x, y: (x ^ 1, y)))  9.46 us
    ppermute x4, starting transfers between devices, swap_x(): lax.ppermute(far, both, pairs(far_x))  7.71 us
    ppermute x2, starting transfers between devices, swap_y(): lax.ppermute(far, both, pairs(far_y))  5.19 us
    ppermute x4, waiting for transfers between devices, swap_x(): lax.ppermute(far, both, pairs(far_x))  4.23 us
    ppermute x2, starting transfers between devices, swap_y(): lax.ppermute(near, both, pairs(lambda x, y: (x, y ^ 1)))  3.58 us
    ppermute x3, starting transfers between devices, body(): lax.ppermute(column, both, chips_apart(j))  3.34 us
  transfers between devices with their start and end apart: 19, of which 7 were waited for; matrix products, arithmetic and copies ran while one was open for 0% of the time, Pallas kernels for 2%

commit v1 on v0

--- a/solution.py
+++ b/solution.py
@@ -240,7 +240,8 @@
 
 def early0_kernel(
     ny, where_ref, kap_ref, init_ref, rhs_ref, even_ref, odd_ref,
-    ks, vs, rs, cx, cy, cz, wi, v1, v2, rest,
+    ks, vs, rs, cx, cy, cz, wi, v1, v2, rest, kc,
+    pair, fine,
 ):
     for x in range(8):
         ks[x, 0:8] = kap_ref[x]
@@ -256,11 +257,14 @@
     sweep0(v1, v2, rs, cx, cy, cz, wi, range(5, 9))
     for p in (6, 7):
         rest[p - 6] = rest0(v2, rs, ks, cx, cy, cz, p)
+    for x in range(4):
+        fine[8 * x : 8 * x + 8] = row_sum(pair, ks[2 * x + 3] + ks[2 * x + 4])
+    kc[...] = 0.125 * lane_sum(fine[...], pair_sum_matrix())
 
 
 def down0_kernel(
     nx, ny, where_ref, near_ref, far_ref, cnear_ref, cfar_ref,
-    ks_own, vs_own, rs_own, cx_own, cy_own, cz_own, wi_own, v1_own, v2_own, rest_own,
+    ks_own, vs_own, rs_own, cx_own, cy_own, cz_own, wi_own, v1_own, v2_own, rest_own, kc,
     v0_ref, rs, cx, cy, cz, wi, block_ref, mnear_ref, mfar_ref, meven_ref, modd_ref,
     ks, vs, v1, v2, pair, fine, coarse,
 ):
@@ -304,19 +308,18 @@
             v0_ref[q - 3] = v2[q][0:8]
         at = 2 * (p - 3)
         fine[at : at + 4] = row_sum(pair, both)
-    for p in range(1, 13, 2):
-        at = 12 + 4 * p
-        fine[at : at + 8] = row_sum(pair, ks[p] + ks[p + 1])
+    fine[16:24] = row_sum(pair, ks[1] + ks[2])
+    fine[24:32] = row_sum(pair, ks[11] + ks[12])
     coarse[...] = lane_sum(fine[...], pair_sum_matrix())
+    kept = [0.125 * coarse[16:24]] + [kc[8 * x : 8 * x + 8] for x in range(4)]
+    kept.append(0.125 * coarse[24:32])
     for x in range(4):
         half = pl.ds(256 * (x % 2), 256)
-        mid = 0.125 * coarse[24 + 8 * x : 32 + 8 * x]
-        low = 0.125 * coarse[16 + 8 * x : 24 + 8 * x]
-        high = 0.125 * coarse[32 + 8 * x : 40 + 8 * x]
+        mid = kept[x + 1]
         block_ref[x // 2, 0:4, half] = 0.5 * coarse[4 * x : 4 * x + 4]
         block_ref[x // 2, 4:8, half] = mid[0:4]
         at = 4 * (x // 2)
-        block_ref[2, at : at + 4, half] = (OMEGA / diagonal(mid, low, high)[0:4])
+        block_ref[2, at : at + 4, half] = (OMEGA / diagonal(mid, kept[x], kept[x + 2])[0:4])
     for ref, side in ((mnear_ref, even), (mfar_ref, jnp.logical_not(even))):
         shallow = jnp.where(side, 6, 0)
         for i in range(3):
@@ -716,10 +719,12 @@
     near, far = swap_x(near, far)
     yodd, yeven, far, near = lax.optimization_barrier((yodd, yeven, far, near))
     cnear, cfar = swap_x(*corner_messages(nx, ny, yeven, yodd))
-    ksx, vsx, rsx, cxx, cyx, czx, wix, v1x, v2x, restx = run(
+    ksx, vsx, rsx, cxx, cyx, czx, wix, v1x, v2x, restx, kcx = run(
         functools.partial(early0_kernel, ny),
-        [(8,) + ring0] * 3 + [(7,) + ring0] + [(6,) + ring0] * 4 + [(4,) + ring0, (2,) + tile0],
-        [], where, kappa, init, rhs, yeven, yodd, cost=early_cost,
+        [(8,) + ring0] * 3 + [(7,) + ring0] + [(6,) + ring0] * 4
+        + [(4,) + ring0, (2,) + tile0, (32, 256)],
+        [(4, 16, 128), (32, 512)],
+        where, kappa, init, rhs, yeven, yodd, cost=early_cost,
     )
     v0, rs, cx0, cy0, cz0, w0, block, mnear, mfar, meven, modd = run(
         functools.partial(down0_kernel, nx, ny),
@@ -728,9 +733,9 @@
         + [(8,) + ring0] * 3
         + [(3,) + tile0]
         + [(5,) + tile0] * 4,
-        [(6,) + ring0] * 2 + [(8,) + ring0, (10,) + ring0, (4, 16, 128), (64, 512), (64, 256)],
+        [(6,) + ring0] * 2 + [(8,) + ring0, (10,) + ring0, (4, 16, 128), (32, 512), (32, 256)],
         where, near, far, cnear, cfar,
-        ksx, vsx, rsx, cxx, cyx, czx, wix, v1x, v2x, restx,
+        ksx, vsx, rsx, cxx, cyx, czx, wix, v1x, v2x, restx, kcx,
     )
     meven, modd = swap_y(meven, modd)
     mnear, mfar = swap_x(mnear, mfar)
@@ -748,7 +753,10 @@
     def chips_apart(j):
         return pairs(lambda x, y: (((x // 2) ^ j) * 2 + x % 2, y))
 
-    mine = [column] + [lax.ppermute(column, both, chips_apart(j)) for j in range(1, nx // 2)]
+    mine = {0: column}
+    for j in sorted(range(1, nx // 2), key=lambda j: j != 2):
+        mine[j] = lax.ppermute(column, both, chips_apart(j))
+    mine = [mine[j] for j in range(nx // 2)]
     other = [lax.ppermute(c, both, pairs(lambda x, y: (x ^ 1, y))) for c in mine]
     n2 = 2 * nx
     pair2 = (n2 + 2, 2, ny, 128)

time: 67.2 us -> 67.1 us (level)
  transfers between devices with their start and end apart: 19 -> 19, of which waited for: 7 -> 6; matrix products, arithmetic and copies ran while one was open for 0% -> 0% of each run, Pallas kernels for 2% -> 2%
where the time goes in v1:
time: 67.1 us; the launch traced here: 67 us
  starting transfers between devices  31.7 us (47%)
  blocking collectives  17.1 us (25%)
  Pallas kernels  10.9 us (16%)
  waiting for transfers between devices  6.97 us (10%)
    all_to_all x1, blocking collectives, body(): column = jnp.transpose(lax.all_to_all(send, 'gy', 0, 0), (1, 0, 2))  17.1 us
    pallas_call x5, Pallas kernels, run(): pl.pallas_call(kernel, out_shape=[jax.ShapeDtypeStruct(shape, F32) for sh...  10.9 us
    ppermute x4, starting transfers between devices, body(): lax.ppermute(c, both, pairs(lambda x, y: (x ^ 1, y)))  9.44 us
    ppermute x4, starting transfers between devices, swap_x(): lax.ppermute(far, both, pairs(far_x))  7.68 us
    ppermute x2, starting transfers between devices, swap_y(): lax.ppermute(far, both, pairs(far_y))  5.16 us
    ppermute x4, waiting for transfers between devices, swap_x(): lax.ppermute(far, both, pairs(far_x))  4.1 us
    ppermute x2, starting transfers between devices, swap_y(): lax.ppermute(near, both, pairs(lambda x, y: (x, y ^ 1)))  3.6 us
    ppermute x3, starting transfers between devices, body(): mine[j] = lax.ppermute(column, both, chips_apart(j))  3.34 us
  transfers between devices with their start and end apart: 19, of which 6 were waited for; matrix products, arithmetic and copies ran while one was open for 0% of the time, Pallas kernels for 2%

profile of v1, /device:TPU:1, one launch (start us, length us, event | category | flops | bytes accessed | tf_op | source)
XLA Modules:
  0.0 67.0 jit_solution(13549077576484295050)
XLA Ops:
  0.0 0.1 pad_add_fusion.where_ref
  0.1 1.7 %shard_map.46 = (f32[8,8,512]{2,1,0:T(8,128)S(1)}, f32[8,8,512]{2,1,0:T(8,128)S(1)}, f32[8,8,512]{2,1,0:T(8,128)S(1)}, f32[8,8,512]{2,1,0:T(8,128)S(1)}, f32[8,8...) custom-call(s32[2]{0:T(128)S(1)} %pad_add_fusion.where_ref, f32[3]{0:T(128)} %table_hbm.1, ...), custom_call_target="tpu_custom_call" | custom-call | tf_op jit(solution)/shard_map/pallas_call | solution.py:655
  1.8 3.3 %collective-permute-start = (f32[8,8,512]{2,1,0:T(8,128)S(1)}, f32[8,8,512]{2,1,0:T(8,128)S(1)}, u32[]{:S(2)}, u32[]{:S(2)}) collective-permute-start(f32[8,8,512]{2,1,0:T(8,128)S(1)} %get-tuple-element.50), channel_id=1, source_target_pairs={{0,32},{1,2},{2,1},{3,4},{4,3},{5,6},{6,5},{7,8},{8,7},{9,10},{10,... | collective-permute-start | bytes 393224 | tf_op jit(solution)/shard_map/ppermute | solution.py:702
  5.1 0.9 %collective-permute-start.1 = (f32[8,8,512]{2,1,0:T(8,128)S(1)}, f32[8,8,512]{2,1,0:T(8,128)S(1)}, u32[]{:S(2)}, u32[]{:S(2)}) collective-permute-start(f32[8,8,512]{2,1,0:T(8,128)S(1)} %get-tuple-element.51), channel_id=1, source_target_pairs={{0,1},{1,0},{2,3},{3,2},{4,5},{5,4},{6,7},{7,6},{8,9},{9,8},{10,11... | collective-permute-start | bytes 393224 | tf_op jit(solution)/shard_map/ppermute | solution.py:701
  6.0 2.3 %collective-permute-start.2 = (f32[8,8,512]{2,1,0:T(8,128)S(1)}, f32[8,8,512]{2,1,0:T(8,128)S(1)}, u32[]{:S(2)}, u32[]{:S(2)}) collective-permute-start(f32[8,8,512]{2,1,0:T(8,128)S(1)} %get-tuple-element.52), channel_id=1, source_target_pairs={{0,1},{1,0},{2,3},{3,2},{4,5},{5,4},{6,7},{7,6},{8,9},{9,8},{10,11... | collective-permute-start | bytes 393224 | tf_op jit(solution)/shard_map/ppermute | solution.py:696
  8.3 0.0 collective-permute-start.3
  8.3 0.0 collective-permute-done.odd_ref
  8.3 1.9 %collective-permute-done.1.even_ref = f32[8,8,512]{2,1,0:T(8,128)S(1)} collective-permute-done((f32[8,8,512]{2,1,0:T(8,128)S(1)}, f32[8,8,512]{2,1,0:T(8,128)S(1)}, u32[]{:S(2)}, u32[]{:S(2)}) %collective-permute-start.1) | collective-permute-done | bytes 131104 | tf_op jit(solution)/shard_map/ppermute | solution.py:701
  10.2 1.1 %collective-permute-done.2.far_ref = f32[8,8,512]{2,1,0:T(8,128)S(1)} collective-permute-done((f32[8,8,512]{2,1,0:T(8,128)S(1)}, f32[8,8,512]{2,1,0:T(8,128)S(1)}, u32[]{:S(2)}, u32[]{:S(2)}) %collective-permute-start.2) | collective-permute-done | bytes 131104 | tf_op jit(solution)/shard_map/ppermute | solution.py:696
  11.3 0.0 collective-permute-done.3.near_ref
  11.4 1.5 %collective-permute-start.5 = (f32[4,8,512]{2,1,0:T(8,128)S(1)}, f32[4,8,512]{2,1,0:T(8,128)S(1)}, u32[]{:S(2)}, u32[]{:S(2)}) collective-permute-start(f32[4,8,512]{2,1,0:T(8,128)S(1)} %get-tuple-element.99), channel_id=1, source_target_pairs={{0,1},{1,0},{2,3},{3,2},{4,5},{5,4},{6,7},{7,6},{8,9},{9,8},{10,11... | collective-permute-start | bytes 196616 | tf_op jit(solution)/shard_map/ppermute | solution.py:696
  12.9 0.9 %collective-permute-start.4 = (f32[4,8,512]{2,1,0:T(8,128)S(1)}, f32[4,8,512]{2,1,0:T(8,128)S(1)}, u32[]{:S(2)}, u32[]{:S(2)}) collective-permute-start(f32[4,8,512]{2,1,0:T(8,128)S(1)} %get-tuple-element.100), channel_id=1, source_target_pairs={{0,32},{1,33},{2,34},{3,35},{4,36},{5,37},{6,38},{7,39},{8,40},{9,... | collective-permute-start | bytes 196616 | tf_op jit(solution)/shard_map/ppermute | solution.py:695
  13.8 1.3 %shard_map.47 = (f32[8,16,512]{2,1,0:T(8,128)S(1)}, f32[8,16,512]{2,1,0:T(8,128)S(1)}, f32[8,16,512]{2,1,0:T(8,128)S(1)}, f32[7,16,512]{2,1,0:T(8,128)S(1)}, f32...) custom-call(s32[2]{0:T(128)S(1)} %pad_add_fusion.where_ref, ...), custom_call_target="tpu_custom_call" | custom-call | flops 20000000 | bytes 4000000 | tf_op jit(solution)/shard_map/pallas_call | solution.py:655
  15.1 0.0 collective-permute-done.5.cfar_ref
  15.1 0.0 collective-permute-done.4.cnear_ref
  15.2 1.6 %shard_map.48 = (f32[8,8,512]{2,1,0:T(8,128)S(1)}, f32[6,16,512]{2,1,0:T(8,128)S(1)}, f32[6,16,512]{2,1,0:T(8,128)S(1)}, f32[8,16,512]{2,1,0:T(8,128)S(1)}, f32[...) custom-call(s32[2]{0:T(128)S(1)} %pad_add_fusion.where_ref, ...), custom_call_target="tpu_custom_call" | custom-call | tf_op jit(solution)/shard_map/pallas_call | solution.py:655
  16.8 1.8 %collective-permute-start.6 = (f32[5,8,512]{2,1,0:T(8,128)S(1)}, f32[5,8,512]{2,1,0:T(8,128)S(1)}, u32[]{:S(2)}, u32[]{:S(2)}) collective-permute-start(f32[5,8,512]{2,1,0:T(8,128)S(1)} %get-tuple-element.74), channel_id=1, source_target_pairs={{0,32},{1,2},{2,1},{3,4},{4,3},{5,6},{6,5},{7,8},{8,7},{9,10},{10,... | collective-permute-start | bytes 245768 | tf_op jit(solution)/shard_map/ppermute | solution.py:702
  18.6 2.7 %collective-permute-start.7 = (f32[5,8,512]{2,1,0:T(8,128)S(1)}, f32[5,8,512]{2,1,0:T(8,128)S(1)}, u32[]{:S(2)}, u32[]{:S(2)}) collective-permute-start(f32[5,8,512]{2,1,0:T(8,128)S(1)} %get-tuple-element.75), channel_id=1, source_target_pairs={{0,1},{1,0},{2,3},{3,2},{4,5},{5,4},{6,7},{7,6},{8,9},{9,8},{10,11... | collective-permute-start | bytes 245768 | tf_op jit(solution)/shard_map/ppermute | solution.py:701
  21.4 2.0 %collective-permute-start.8 = (f32[5,8,512]{2,1,0:T(8,128)S(1)}, f32[5,8,512]{2,1,0:T(8,128)S(1)}, u32[]{:S(2)}, u32[]{:S(2)}) collective-permute-start(f32[5,8,512]{2,1,0:T(8,128)S(1)} %get-tuple-element.76), channel_id=1, source_target_pairs={{0,1},{1,0},{2,3},{3,2},{4,5},{5,4},{6,7},{7,6},{8,9},{9,8},{10,11... | collective-permute-start | bytes 245768 | tf_op jit(solution)/shard_map/ppermute | solution.py:696
  23.4 0.1 collective-permute-start.9
  23.4 0.0 collective-permute-done.6.modd_ref
  23.4 0.0 collective-permute-done.7.meven_ref
  23.4 2.0 %collective-permute-done.8.far_ref = f32[5,8,512]{2,1,0:T(8,128)S(1)} collective-permute-done((f32[5,8,512]{2,1,0:T(8,128)S(1)}, f32[5,8,512]{2,1,0:T(8,128)S(1)}, u32[]{:S(2)}, u32[]{:S(2)}) %collective-permute-start.8) | collective-permute-done | bytes 81952 | tf_op jit(solution)/shard_map/ppermute | solution.py:696
  25.5 0.0 collective-permute-done.9.near_ref
  25.6 1.8 %collective-permute-start.11 = (f32[7,8,512]{2,1,0:T(8,128)S(1)}, f32[7,8,512]{2,1,0:T(8,128)S(1)}, u32[]{:S(2)}, u32[]{:S(2)}) collective-permute-start(f32[7,8,512]{2,1,0:T(8,128)S(1)} %maximum_maximum_fusion), channel_id=1, source_target_pairs={{0,1},{1,0},{2,3},{3,2},{4,5},{5,4},{6,7},{7,6},{8,9},{9,8},{10,11... | collective-permute-start | bytes 344072 | tf_op jit(solution)/shard_map/ppermute | solution.py:696
  27.4 1.5 %collective-permute-start.10 = (f32[7,8,512]{2,1,0:T(8,128)S(1)}, f32[7,8,512]{2,1,0:T(8,128)S(1)}, u32[]{:S(2)}, u32[]{:S(2)}) collective-permute-start(f32[7,8,512]{2,1,0:T(8,128)S(1)} %maximum_maximum_fusion), channel_id=1, source_target_pairs={{0,32},{1,33},{2,34},{3,35},{4,36},{5,37},{6,38},{7,39},{8,40},{9,... | collective-permute-start | bytes 344072 | tf_op jit(solution)/shard_map/ppermute | solution.py:695
  28.9 1.0 %collective-permute-done.11.cfar_ref = f32[7,8,512]{2,1,0:T(8,128)S(1)} collective-permute-done((f32[7,8,512]{2,1,0:T(8,128)S(1)}, f32[7,8,512]{2,1,0:T(8,128)S(1)}, u32[]{:S(2)}, u32[]{:S(2)}) %collective-permute-start.11) | collective-permute-done | bytes 114720 | tf_op jit(solution)/shard_map/ppermute | solution.py:696
  29.9 0.0 collective-permute-done.10.cnear_ref
  29.9 1.1 %shard_map.49 = (f32[12,16,512]{2,1,0:T(8,128)S(1)}, f32[12,16,256]{2,1,0:T(8,128)S(1)}, f32[12,16,256]{2,1,0:T(8,128)S(1)}, f32[12,16,256]{2,1,0:T(8,128)S(1)},...) custom-call(s32[2]{0:T(128)S(1)} %pad_add_fusion.where_ref, ...), custom_call_target="tpu_custom_call" | custom-call | tf_op jit(solution)/shard_map/pallas_call | solution.py:655
  31.0 17.1 %all_to_all.5 = f32[32,8,128]{2,1,0:T(8,128)S(1)} all-to-all(f32[32,8,128]{2,1,0:T(8,128)S(1)} %get-tuple-element.82), channel_id=1, replica_groups=mesh['gx'=8,'gy'=32] {'gy'}, dimensions={0} | all-to-all | bytes 262144 | tf_op jit(solution)/shard_map/all_to_all | solution.py:751
  48.1 2.4 %collective-permute-start.14 = (f32[8,32,128]{2,1,0:T(8,128)S(1)}, f32[8,32,128]{2,1,0:T(8,128)S(1)}, u32[]{:S(2)}, u32[]{:S(2)}) collective-permute-start(f32[8,32,128]{2,1,0:T(8,128)S(1)} %bitcast.5), channel_id=1, source_target_pairs={{0,192},{1,193},{2,194},{3,195},{4,196},{5,197},{6,198},{7,199},{8... | collective-permute-start | bytes 393224 | tf_op jit(solution)/shard_map/ppermute | solution.py:758
  50.5 0.7 %collective-permute-start.13 = (f32[8,32,128]{2,1,0:T(8,128)S(1)}, f32[8,32,128]{2,1,0:T(8,128)S(1)}, u32[]{:S(2)}, u32[]{:S(2)}) collective-permute-start(f32[8,32,128]{2,1,0:T(8,128)S(1)} %bitcast.6), channel_id=1, source_target_pairs={{0,128},{1,129},{2,130},{3,131},{4,132},{5,133},{6,134},{7,135},{8... | collective-permute-start | bytes 393224 | tf_op jit(solution)/shard_map/ppermute | solution.py:758
  51.2 0.2 collective-permute-start.12
  51.4 5.1 %collective-permute-start.15 = (f32[8,32,128]{2,1,0:T(8,128)S(1)}, f32[8,32,128]{2,1,0:T(8,128)S(1)}, u32[]{:S(2)}, u32[]{:S(2)}) collective-permute-start(f32[8,32,128]{2,1,0:T(8,128)S(1)} %bitcast.8), channel_id=1, source_target_pairs={{0,32},{1,33},{2,34},{3,35},{4,36},{5,37},{6,38},{7,39},{8,40},{9,... | collective-permute-start | bytes 393224 | tf_op jit(solution)/shard_map/ppermute | solution.py:760
  56.6 0.0 collective-permute-done.14.refs_3_
  56.6 2.1 %collective-permute-start.18 = (f32[8,32,128]{2,1,0:T(8,128)S(1)}, f32[8,32,128]{2,1,0:T(8,128)S(1)}, u32[]{:S(2)}, u32[]{:S(2)}) collective-permute-start(f32[8,32,128]{2,1,0:T(8,128)S(1)} %collective-permute-done.14.refs_3_), channel_id=1, source_target_pairs={{0,32},{1,33},{2,34},{3,35},{4,36},{5,37},{6,38},{7,39},{8,40},{9,... | collective-permute-start | bytes 393224 | tf_op jit(solution)/shard_map/ppermute | solution.py:760
  58.6 0.0 collective-permute-done.13.refs_2_
  58.6 1.5 %collective-permute-start.17 = (f32[8,32,128]{2,1,0:T(8,128)S(1)}, f32[8,32,128]{2,1,0:T(8,128)S(1)}, u32[]{:S(2)}, u32[]{:S(2)}) collective-permute-start(f32[8,32,128]{2,1,0:T(8,128)S(1)} %collective-permute-done.13.refs_2_), channel_id=1, source_target_pairs={{0,32},{1,33},{2,34},{3,35},{4,36},{5,37},{6,38},{7,39},{8,40},{9,... | collective-permute-start | bytes 393224 | tf_op jit(solution)/shard_map/ppermute | solution.py:760
  60.1 0.0 collective-permute-done.12.refs_1_
  60.1 0.8 %collective-permute-start.16 = (f32[8,32,128]{2,1,0:T(8,128)S(1)}, f32[8,32,128]{2,1,0:T(8,128)S(1)}, u32[]{:S(2)}, u32[]{:S(2)}) collective-permute-start(f32[8,32,128]{2,1,0:T(8,128)S(1)} %collective-permute-done.12.refs_1_), channel_id=1, source_target_pairs={{0,32},{1,33},{2,34},{3,35},{4,36},{5,37},{6,38},{7,39},{8,40},{9,... | collective-permute-start | bytes 393224 | tf_op jit(solution)/shard_map/ppermute | solution.py:760
  60.9 0.0 collective-permute-done.15.refs_4_
  60.9 0.0 collective-permute-done.18.refs_7_
  60.9 0.2 collective-permute-done.17.refs_6_
  61.1 0.8 %collective-permute-done.16.refs_5_ = f32[8,32,128]{2,1,0:T(8,128)S(1)} collective-permute-done((f32[8,32,128]{2,1,0:T(8,128)S(1)}, f32[8,32,128]{2,1,0:T(8,128)S(1)}, u32[]{:S(2)}, u32[]{:S(2)}) %collective-permute-start.16) | collective-permute-done | bytes 131104 | tf_op jit(solution)/shard_map/ppermute | solution.py:760
  61.9 5.1 %shard_map.50 = f32[8,8,512]{2,1,0:T(8,128)} custom-call(s32[2]{0:T(128)S(1)} %pad_add_fusion.where_ref, f32[8,32,128]{2,1,0:T(8,128)S(1)} %bitcast.9, f32[8,32,128]{2,1,0:T(8,128)S(1)} %collective-permute-done.12.refs_1_, f32[8,32,128]{2,1,0:T(8,128)S(1)} %collective-permute-done.13.refs_2_, f32[8,32,128]{2,1,0:T(8,128)S(1)} %collective-permute-done.14.refs_3_, ...), custom_call_target="tpu_custom_call" | custom-call | tf_op jit(solution)/shard_map/pallas_call | solution.py:655
  (12 shorter events, 0.1 us)
Async XLA Ops:
  1.8 6.5 %collective-permute-start = (f32[8,8,512]{2,1,0:T(8,128)S(1)}, f32[8,8,512]{2,1,0:T(8,128)S(1)}, u32[]{:S(2)}, u32[]{:S(2)}) collective-permute-start(f32[8,8,512]{2,1,0:T(8,128)S(1)} %get-tuple-element.50), channel_id=1, source_target_pairs={{0,32},{1,2},{2,1},{3,4},{4,3},{5,6},{6,5},{7,8},{8,7},{9,10},{10,... | collective-permute-start | bytes 393224 | tf_op jit(solution)/shard_map/ppermute | solution.py:702
  5.1 5.1 %collective-permute-start.1 = (f32[8,8,512]{2,1,0:T(8,128)S(1)}, f32[8,8,512]{2,1,0:T(8,128)S(1)}, u32[]{:S(2)}, u32[]{:S(2)}) collective-permute-start(f32[8,8,512]{2,1,0:T(8,128)S(1)} %get-tuple-element.51), channel_id=1, source_target_pairs={{0,1},{1,0},{2,3},{3,2},{4,5},{5,4},{6,7},{7,6},{8,9},{9,8},{10,11... | collective-permute-start | bytes 393224 | tf_op jit(solution)/shard_map/ppermute | solution.py:701
  6.0 5.3 %collective-permute-start.2 = (f32[8,8,512]{2,1,0:T(8,128)S(1)}, f32[8,8,512]{2,1,0:T(8,128)S(1)}, u32[]{:S(2)}, u32[]{:S(2)}) collective-permute-start(f32[8,8,512]{2,1,0:T(8,128)S(1)} %get-tuple-element.52), channel_id=1, source_target_pairs={{0,1},{1,0},{2,3},{3,2},{4,5},{5,4},{6,7},{7,6},{8,9},{9,8},{10,11... | collective-permute-start | bytes 393224 | tf_op jit(solution)/shard_map/ppermute | solution.py:696
  8.3 2.9 %collective-permute-start.3 = (f32[8,8,512]{2,1,0:T(8,128)S(1)}, f32[8,8,512]{2,1,0:T(8,128)S(1)}, u32[]{:S(2)}, u32[]{:S(2)}) collective-permute-start(f32[8,8,512]{2,1,0:T(8,128)S(1)} %get-tuple-element.53), channel_id=1, source_target_pairs={{0,32},{1,33},{2,34},{3,35},{4,36},{5,37},{6,38},{7,39},{8,40},{9,... | collective-permute-start | bytes 393224 | tf_op jit(solution)/shard_map/ppermute | solution.py:695
  11.4 3.8 %collective-permute-start.5 = (f32[4,8,512]{2,1,0:T(8,128)S(1)}, f32[4,8,512]{2,1,0:T(8,128)S(1)}, u32[]{:S(2)}, u32[]{:S(2)}) collective-permute-start(f32[4,8,512]{2,1,0:T(8,128)S(1)} %get-tuple-element.99), channel_id=1, source_target_pairs={{0,1},{1,0},{2,3},{3,2},{4,5},{5,4},{6,7},{7,6},{8,9},{9,8},{10,11... | collective-permute-start | bytes 196616 | tf_op jit(solution)/shard_map/ppermute | solution.py:696
  12.9 2.2 %collective-permute-start.4 = (f32[4,8,512]{2,1,0:T(8,128)S(1)}, f32[4,8,512]{2,1,0:T(8,128)S(1)}, u32[]{:S(2)}, u32[]{:S(2)}) collective-permute-start(f32[4,8,512]{2,1,0:T(8,128)S(1)} %get-tuple-element.100), channel_id=1, source_target_pairs={{0,32},{1,33},{2,34},{3,35},{4,36},{5,37},{6,38},{7,39},{8,40},{9,... | collective-permute-start | bytes 196616 | tf_op jit(solution)/shard_map/ppermute | solution.py:695
  16.8 6.6 %collective-permute-start.6 = (f32[5,8,512]{2,1,0:T(8,128)S(1)}, f32[5,8,512]{2,1,0:T(8,128)S(1)}, u32[]{:S(2)}, u32[]{:S(2)}) collective-permute-start(f32[5,8,512]{2,1,0:T(8,128)S(1)} %get-tuple-element.74), channel_id=1, source_target_pairs={{0,32},{1,2},{2,1},{3,4},{4,3},{5,6},{6,5},{7,8},{8,7},{9,10},{10,... | collective-permute-start | bytes 245768 | tf_op jit(solution)/shard_map/ppermute | solution.py:702
  18.6 4.8 %collective-permute-start.7 = (f32[5,8,512]{2,1,0:T(8,128)S(1)}, f32[5,8,512]{2,1,0:T(8,128)S(1)}, u32[]{:S(2)}, u32[]{:S(2)}) collective-permute-start(f32[5,8,512]{2,1,0:T(8,128)S(1)} %get-tuple-element.75), channel_id=1, source_target_pairs={{0,1},{1,0},{2,3},{3,2},{4,5},{5,4},{6,7},{7,6},{8,9},{9,8},{10,11... | collective-permute-start | bytes 245768 | tf_op jit(solution)/shard_map/ppermute | solution.py:701
  21.4 4.1 %collective-permute-start.8 = (f32[5,8,512]{2,1,0:T(8,128)S(1)}, f32[5,8,512]{2,1,0:T(8,128)S(1)}, u32[]{:S(2)}, u32[]{:S(2)}) collective-permute-start(f32[5,8,512]{2,1,0:T(8,128)S(1)} %get-tuple-element.76), channel_id=1, source_target_pairs={{0,1},{1,0},{2,3},{3,2},{4,5},{5,4},{6,7},{7,6},{8,9},{9,8},{10,11... | collective-permute-start | bytes 245768 | tf_op jit(solution)/shard_map/ppermute | solution.py:696
  23.4 2.1 %collective-permute-start.9 = (f32[5,8,512]{2,1,0:T(8,128)S(1)}, f32[5,8,512]{2,1,0:T(8,128)S(1)}, u32[]{:S(2)}, u32[]{:S(2)}) collective-permute-start(f32[5,8,512]{2,1,0:T(8,128)S(1)} %get-tuple-element.77), channel_id=1, source_target_pairs={{0,32},{1,33},{2,34},{3,35},{4,36},{5,37},{6,38},{7,39},{8,40},{9,... | collective-permute-start | bytes 245768 | tf_op jit(solution)/shard_map/ppermute | solution.py:695
  25.6 4.3 %collective-permute-start.11 = (f32[7,8,512]{2,1,0:T(8,128)S(1)}, f32[7,8,512]{2,1,0:T(8,128)S(1)}, u32[]{:S(2)}, u32[]{:S(2)}) collective-permute-start(f32[7,8,512]{2,1,0:T(8,128)S(1)} %maximum_maximum_fusion), channel_id=1, source_target_pairs={{0,1},{1,0},{2,3},{3,2},{4,5},{5,4},{6,7},{7,6},{8,9},{9,8},{10,11... | collective-permute-start | bytes 344072 | tf_op jit(solution)/shard_map/ppermute | solution.py:696
  27.4 2.5 %collective-permute-start.10 = (f32[7,8,512]{2,1,0:T(8,128)S(1)}, f32[7,8,512]{2,1,0:T(8,128)S(1)}, u32[]{:S(2)}, u32[]{:S(2)}) collective-permute-start(f32[7,8,512]{2,1,0:T(8,128)S(1)} %maximum_maximum_fusion), channel_id=1, source_target_pairs={{0,32},{1,33},{2,34},{3,35},{4,36},{5,37},{6,38},{7,39},{8,40},{9,... | collective-permute-start | bytes 344072 | tf_op jit(solution)/shard_map/ppermute | solution.py:695
  48.1 8.5 %collective-permute-start.14 = (f32[8,32,128]{2,1,0:T(8,128)S(1)}, f32[8,32,128]{2,1,0:T(8,128)S(1)}, u32[]{:S(2)}, u32[]{:S(2)}) collective-permute-start(f32[8,32,128]{2,1,0:T(8,128)S(1)} %bitcast.5), channel_id=1, source_target_pairs={{0,192},{1,193},{2,194},{3,195},{4,196},{5,197},{6,198},{7,199},{8... | collective-permute-start | bytes 393224 | tf_op jit(solution)/shard_map/ppermute | solution.py:758
  50.5 8.1 %collective-permute-start.13 = (f32[8,32,128]{2,1,0:T(8,128)S(1)}, f32[8,32,128]{2,1,0:T(8,128)S(1)}, u32[]{:S(2)}, u32[]{:S(2)}) collective-permute-start(f32[8,32,128]{2,1,0:T(8,128)S(1)} %bitcast.6), channel_id=1, source_target_pairs={{0,128},{1,129},{2,130},{3,131},{4,132},{5,133},{6,134},{7,135},{8... | collective-permute-start | bytes 393224 | tf_op jit(solution)/shard_map/ppermute | solution.py:758
  51.2 8.9 %collective-permute-start.12 = (f32[8,32,128]{2,1,0:T(8,128)S(1)}, f32[8,32,128]{2,1,0:T(8,128)S(1)}, u32[]{:S(2)}, u32[]{:S(2)}) collective-permute-start(f32[8,32,128]{2,1,0:T(8,128)S(1)} %bitcast.7), channel_id=1, source_target_pairs={{0,64},{1,65},{2,66},{3,67},{4,68},{5,69},{6,70},{7,71},{8,72},{9,... | collective-permute-start | bytes 393224 | tf_op jit(solution)/shard_map/ppermute | solution.py:758
  51.4 9.5 %collective-permute-start.15 = (f32[8,32,128]{2,1,0:T(8,128)S(1)}, f32[8,32,128]{2,1,0:T(8,128)S(1)}, u32[]{:S(2)}, u32[]{:S(2)}) collective-permute-start(f32[8,32,128]{2,1,0:T(8,128)S(1)} %bitcast.8), channel_id=1, source_target_pairs={{0,32},{1,33},{2,34},{3,35},{4,36},{5,37},{6,38},{7,39},{8,40},{9,... | collective-permute-start | bytes 393224 | tf_op jit(solution)/shard_map/ppermute | solution.py:760
  56.6 4.3 %collective-permute-start.18 = (f32[8,32,128]{2,1,0:T(8,128)S(1)}, f32[8,32,128]{2,1,0:T(8,128)S(1)}, u32[]{:S(2)}, u32[]{:S(2)}) collective-permute-start(f32[8,32,128]{2,1,0:T(8,128)S(1)} %collective-permute-done.14.refs_3_), channel_id=1, source_target_pairs={{0,32},{1,33},{2,34},{3,35},{4,36},{5,37},{6,38},{7,39},{8,40},{9,... | collective-permute-start | bytes 393224 | tf_op jit(solution)/shard_map/ppermute | solution.py:760
  58.6 2.4 %collective-permute-start.17 = (f32[8,32,128]{2,1,0:T(8,128)S(1)}, f32[8,32,128]{2,1,0:T(8,128)S(1)}, u32[]{:S(2)}, u32[]{:S(2)}) collective-permute-start(f32[8,32,128]{2,1,0:T(8,128)S(1)} %collective-permute-done.13.refs_2_), channel_id=1, source_target_pairs={{0,32},{1,33},{2,34},{3,35},{4,36},{5,37},{6,38},{7,39},{8,40},{9,... | collective-permute-start | bytes 393224 | tf_op jit(solution)/shard_map/ppermute | solution.py:760
  60.1 1.8 %collective-permute-start.16 = (f32[8,32,128]{2,1,0:T(8,128)S(1)}, f32[8,32,128]{2,1,0:T(8,128)S(1)}, u32[]{:S(2)}, u32[]{:S(2)}) collective-permute-start(f32[8,32,128]{2,1,0:T(8,128)S(1)} %collective-permute-done.12.refs_1_), channel_id=1, source_target_pairs={{0,32},{1,33},{2,34},{3,35},{4,36},{5,37},{6,38},{7,39},{8,40},{9,... | collective-permute-start | bytes 393224 | tf_op jit(solution)/shard_map/ppermute | solution.py:760

commit v2 on v1

--- a/solution.py
+++ b/solution.py
@@ -345,11 +345,87 @@
     return jnp.concatenate([high[0:3], low[0:3], jnp.concatenate(rows, axis=1)], axis=0)
 
 
+def nearest_messages(ny, meven, modd):
+    high, low = both_tiles(ny, meven, modd)
+
+    def message(t, r):
+        rows = [high[t, 0:1], high[t, 4:5], high[2, r : r + 1]]
+        rows += [low[t, 3:4], low[t, 7:8], low[2, r + 3 : r + 4], high[t, 0:2]]
+        return jnp.concatenate(rows, axis=0)
+
+    top, bottom = message(1, 4), message(0, 0)
+    even = lax.axis_index("gx") % 2 == 0
+    return jnp.where(even, top, bottom), jnp.where(even, bottom, top)
+
+
+def coarse_kernel(
+    nx, ny, where_ref, block_ref, near_ref, far_ref, meven_ref, modd_ref, cnear_ref, cfar_ref,
+    send_ref, f1, k1, w1, u1, v1, cx, cy, cz, pair, fine,
+):
+    even, outside = edge_flags(where_ref[0], nx)
+    lanes = (slice(0, 256), slice(256, 512))
+    zero = jnp.zeros((12, 256), F32)
+    near = [near_ref[i] for i in range(3)]
+    far = [jnp.where(outside, 0.0, far_ref[i]) for i in range(3)]
+    cnear = cnear_ref[...]
+    cfar = jnp.where(outside, 0.0, cfar_ref[...])
+    mine = [y_tiles(where_ref, ny, meven_ref, modd_ref, i) for i in range(3)]
+
+    def pick(a, b):
+        return [jnp.where(even, p, q) for p, q in zip(a, b)]
+
+    low, high = pick(far, near), pick(near, far)
+    corners = {1: (jnp.where(even, cfar, cnear), lanes[1]), 6: (jnp.where(even, cnear, cfar), lanes[0])}
+    for p, tiles, x in (
+        [(0, low, 2), (1, low, 3)]
+        + [(x + 2, [block_ref[i] for i in range(3)], x) for x in range(4)]
+        + [(6, high, 0), (7, high, 1)]
+    ):
+        half, t = lanes[x % 2], x // 2
+        for i, (ref, at, row) in enumerate(
+            ((f1, t, slice(0, 4)), (k1, t, slice(4, 8)), (w1, 2, slice(4 * t, 4 * t + 4)))
+        ):
+            ref[p, 4:16] = zero
+            ref[p, 0:4] = tiles[at][row, half]
+            if 2 <= p <= 5:
+                ref[p, 4:8] = mine[at][0][row, half]
+                ref[p, 12:16] = mine[at][1][row, half]
+            if p in corners:
+                rows, side = corners[p]
+                ref[p, 4:5] = rows[i : i + 1, side]
+                ref[p, 15:16] = rows[3 + i : 4 + i, side]
+    for p in range(8):
+        u1[p] = w1[p] * f1[p]
+        if p < 7:
+            cx[p] = 0.5 * (k1[p] + k1[p + 1])
+    for p in range(1, 7):
+        cy[p] = coupling_y(k1[p])
+        cz[p] = coupling_z(k1[p])
+        mid = u1[p]
+        total = gathered(mid, u1[p - 1], u1[p + 1], cx[p - 1], cx[p], cy[p], cz[p])
+        v1[p] = KEEP * mid + w1[p] * (f1[p] + total)
+    for p in range(2, 6, 2):
+        both = None
+        for q in (p, p + 1):
+            mid = v1[q]
+            total = gathered(mid, v1[q - 1], v1[q + 1], cx[q - 1], cx[q], cy[q], cz[q])
+            diag = diagonal(k1[q], k1[q - 1], k1[q + 1])
+            rest = (f1[q] + total - diag * mid)[0:8]
+            both = rest if both is None else both + rest
+        at = p - 2
+        fine[at : at + 2] = 0.5 * row_sum(pair, both)[0:2]
+        kept = k1[p, 0:8] + k1[p + 1, 0:8]
+        fine[4 + at : 6 + at] = 0.125 * row_sum(pair, kept)[0:2]
+    tile = lane_sum(fine[...], pair_sum_matrix())
+    for i in range(send_ref.shape[0]):
+        send_ref[i] = tile
+
+
 def down1_kernel(
     nx, ny, where_ref, block_ref, v0_ref, near_ref, far_ref, meven_ref, modd_ref,
     cnear_ref, cfar_ref,
-    v0x, v1, f1, w1, cx, cy, cz, send_ref,
-    k1, u1, pair, fine,
+    v0x, v1, f1, w1, cx, cy, cz,
+    k1, u1,
 ):
     even, outside = edge_flags(where_ref[0], nx)
 
@@ -411,21 +487,6 @@
         mid = u1[p]
         total = gathered(mid, u1[p - 1], u1[p + 1], cx[p - 1], cx[p], cy[p], cz[p])
         v1[p] = KEEP * mid + w1[p] * (f1[p] + total)
-    for p in range(4, 8, 2):
-        both = None
-        for q in (p, p + 1):
-            mid = v1[q]
-            total = gathered(mid, v1[q - 1], v1[q + 1], cx[q - 1], cx[q], cy[q], cz[q])
-            diag = diagonal(k1[q], k1[q - 1], k1[q + 1])
-            rest = (f1[q] + total - diag * mid)[0:8]
-            both = rest if both is None else both + rest
-        at = p - 4
-        fine[at : at + 2] = 0.5 * row_sum(pair, both)[0:2]
-        kept = k1[p, 0:8] + k1[p + 1, 0:8]
-        fine[4 + at : 6 + at] = 0.125 * row_sum(pair, kept)[0:2]
-    tile = lane_sum(fine[...], pair_sum_matrix())
-    for i in range(send_ref.shape[0]):
-        send_ref[i] = tile
 
 
 def up_kernel(
@@ -740,15 +801,22 @@
     meven, modd = swap_y(meven, modd)
     mnear, mfar = swap_x(mnear, mfar)
     modd, meven, mfar, mnear = lax.optimization_barrier((modd, meven, mfar, mnear))
+    nnear, nfar = swap_x(*nearest_messages(ny, meven, modd))
     corner = corner1_message(ny, meven, modd)
     cnear, cfar = swap_x(corner, corner)
-    v0x, v1, f1, w1, cx1, cy1, cz1, send = run(
+    (send,) = run(
+        functools.partial(coarse_kernel, nx, ny), [(ny, 8, 128)],
+        [(8,) + ring1] * 8 + [(4, 16, 128), (8, 256)],
+        where, block, mnear, mfar, meven, modd, nnear, nfar,
+    )
+    column = jnp.transpose(lax.all_to_all(send, "gy", 0, 0), (1, 0, 2))
+    column, cnear, cfar, v0 = lax.optimization_barrier((column, cnear, cfar, v0))
+    v0x, v1, f1, w1, cx1, cy1, cz1 = run(
         functools.partial(down1_kernel, nx, ny),
-        [(12,) + ring0] + [(12,) + ring1] * 6 + [(ny, 8, 128)],
-        [(12,) + ring1, (12,) + ring1, (4, 16, 128), (8, 256)],
-        where, block, v0, mnear, mfar, meven, modd, cnear, cfar,
-    )
-    column = jnp.transpose(lax.all_to_all(send, "gy", 0, 0), (1, 0, 2))
+        [(12,) + ring0] + [(12,) + ring1] * 6,
+        [(12,) + ring1, (12,) + ring1],
+        where, block, v0, mnear, mfar, meven, modd, cnear, cfar, cost=early_cost,
+    )
 
     def chips_apart(j):
         return pairs(lambda x, y: (((x // 2) ^ j) * 2 + x % 2, y))

time: 67.1 us -> 68.2 us (1.016)
  blocking collectives: 17.1 us -> 0 us
  waiting for transfers between devices: 6.97 us -> 20.2 us
  starting transfers between devices: 31.7 us -> 35.1 us
  Pallas kernels: 10.9 us -> 12.2 us
    all_to_all x1 -> x0, blocking collectives: 17.1 us -> none  [body(): column = jnp.transpose(lax.all_to_all(send, 'gy', 0, 0), (1, 0, 2))]
    all_to_all x0 -> x1, waiting for transfers between devices: none -> 8.32 us  [body(): column = jnp.transpose(lax.all_to_all(send, 'gy', 0, 0), (1, 0, 2))]
    all_to_all x0 -> x1, starting transfers between devices: none -> 8 us  [body(): column = jnp.transpose(lax.all_to_all(send, 'gy', 0, 0), (1, 0, 2))]
    ppermute x4 -> x5, starting transfers between devices: 7.68 us -> 3.66 us  [swap_x(): lax.ppermute(far, both, pairs(far_x))]
    ppermute x4 -> x5, waiting for transfers between devices: 4.1 us -> 7.94 us  [swap_x(): lax.ppermute(far, both, pairs(far_x))]
    ppermute x4, starting transfers between devices: 9.44 us -> 7.57 us  [body(): lax.ppermute(c, both, pairs(lambda x, y: (x ^ 1, y)))]
    pallas_call x5 -> x6, Pallas kernels: 10.9 us -> 12.2 us  [run(): pl.pallas_call(kernel, out_shape=[jax.ShapeDtypeStruct(shape, F32) for sh...]
    ppermute x2, starting transfers between devices: 5.16 us -> 3.81 us  [swap_y(): lax.ppermute(far, both, pairs(far_y))]
  transfers between devices with their start and end apart: 19 -> 22, of which waited for: 6 -> 9; matrix products, arithmetic and copies ran while one was open for 0% -> 0% of each run, Pallas kernels for 2% -> 3%
where the time goes in v2:
time: 68.2 us; the launch traced here: 68.1 us
  starting transfers between devices  35.1 us (51%)
  waiting for transfers between devices  20.2 us (30%)
  Pallas kernels  12.2 us (18%)
    pallas_call x6, Pallas kernels, run(): pl.pallas_call(kernel, out_shape=[jax.ShapeDtypeStruct(shape, F32) for sh...  12.2 us
    all_to_all x1, waiting for transfers between devices, body(): column = jnp.transpose(lax.all_to_all(send, 'gy', 0, 0), (1, 0, 2))  8.32 us
    all_to_all x1, starting transfers between devices, body(): column = jnp.transpose(lax.all_to_all(send, 'gy', 0, 0), (1, 0, 2))  8 us
    ppermute x5, waiting for transfers between devices, swap_x(): lax.ppermute(far, both, pairs(far_x))  7.94 us
    ppermute x4, starting transfers between devices, body(): lax.ppermute(c, both, pairs(lambda x, y: (x ^ 1, y)))  7.57 us
    ppermute x2, starting transfers between devices, swap_y(): lax.ppermute(near, both, pairs(lambda x, y: (x, y ^ 1)))  4.68 us
    ppermute x3, starting transfers between devices, body(): mine[j] = lax.ppermute(column, both, chips_apart(j))  3.94 us
    ppermute x2, starting transfers between devices, swap_y(): lax.ppermute(far, both, pairs(far_y))  3.81 us
  transfers between devices with their start and end apart: 22, of which 9 were waited for; matrix products, arithmetic and copies ran while one was open for 0% of the time, Pallas kernels for 3%

profile of v2, /device:TPU:1, one launch (start us, length us, event | category | flops | bytes accessed | tf_op | source)
XLA Modules:
  0.0 68.1 jit_solution(10961250668306567632)
XLA Ops:
  0.0 0.1 pad_add_fusion.where_ref
  0.1 1.7 %shard_map.46 = (f32[8,8,512]{2,1,0:T(8,128)S(1)}, f32[8,8,512]{2,1,0:T(8,128)S(1)}, f32[8,8,512]{2,1,0:T(8,128)S(1)}, f32[8,8,512]{2,1,0:T(8,128)S(1)}, f32[8,8...) custom-call(s32[2]{0:T(128)S(1)} %pad_add_fusion.where_ref, f32[3]{0:T(128)} %table_hbm.1, ...), custom_call_target="tpu_custom_call" | custom-call | tf_op jit(solution)/shard_map/pallas_call | solution.py:716
  1.8 3.3 %collective-permute-start = (f32[8,8,512]{2,1,0:T(8,128)S(1)}, f32[8,8,512]{2,1,0:T(8,128)S(1)}, u32[]{:S(2)}, u32[]{:S(2)}) collective-permute-start(f32[8,8,512]{2,1,0:T(8,128)S(1)} %get-tuple-element.53), channel_id=1, source_target_pairs={{0,32},{1,2},{2,1},{3,4},{4,3},{5,6},{6,5},{7,8},{8,7},{9,10},{10,... | collective-permute-start | bytes 393224 | tf_op jit(solution)/shard_map/ppermute | solution.py:763
  5.1 0.9 %collective-permute-start.1 = (f32[8,8,512]{2,1,0:T(8,128)S(1)}, f32[8,8,512]{2,1,0:T(8,128)S(1)}, u32[]{:S(2)}, u32[]{:S(2)}) collective-permute-start(f32[8,8,512]{2,1,0:T(8,128)S(1)} %get-tuple-element.54), channel_id=1, source_target_pairs={{0,1},{1,0},{2,3},{3,2},{4,5},{5,4},{6,7},{7,6},{8,9},{9,8},{10,11... | collective-permute-start | bytes 393224 | tf_op jit(solution)/shard_map/ppermute | solution.py:762
  6.0 2.3 %collective-permute-start.2 = (f32[8,8,512]{2,1,0:T(8,128)S(1)}, f32[8,8,512]{2,1,0:T(8,128)S(1)}, u32[]{:S(2)}, u32[]{:S(2)}) collective-permute-start(f32[8,8,512]{2,1,0:T(8,128)S(1)} %get-tuple-element.55), channel_id=1, source_target_pairs={{0,1},{1,0},{2,3},{3,2},{4,5},{5,4},{6,7},{7,6},{8,9},{9,8},{10,11... | collective-permute-start | bytes 393224 | tf_op jit(solution)/shard_map/ppermute | solution.py:757
  8.3 0.0 collective-permute-start.3
  8.3 0.0 collective-permute-done.odd_ref
  8.3 1.9 %collective-permute-done.1.even_ref = f32[8,8,512]{2,1,0:T(8,128)S(1)} collective-permute-done((f32[8,8,512]{2,1,0:T(8,128)S(1)}, f32[8,8,512]{2,1,0:T(8,128)S(1)}, u32[]{:S(2)}, u32[]{:S(2)}) %collective-permute-start.1) | collective-permute-done | bytes 131104 | tf_op jit(solution)/shard_map/ppermute | solution.py:762
  10.2 1.1 %collective-permute-done.2.far_ref = f32[8,8,512]{2,1,0:T(8,128)S(1)} collective-permute-done((f32[8,8,512]{2,1,0:T(8,128)S(1)}, f32[8,8,512]{2,1,0:T(8,128)S(1)}, u32[]{:S(2)}, u32[]{:S(2)}) %collective-permute-start.2) | collective-permute-done | bytes 131104 | tf_op jit(solution)/shard_map/ppermute | solution.py:757
  11.3 0.0 collective-permute-done.3.near_ref
  11.4 1.3 %collective-permute-start.4 = (f32[4,8,512]{2,1,0:T(8,128)S(1)}, f32[4,8,512]{2,1,0:T(8,128)S(1)}, u32[]{:S(2)}, u32[]{:S(2)}) collective-permute-start(f32[4,8,512]{2,1,0:T(8,128)S(1)} %get-tuple-element.106), channel_id=1, source_target_pairs={{0,32},{1,33},{2,34},{3,35},{4,36},{5,37},{6,38},{7,39},{8,40},{9,... | collective-permute-start | bytes 196616 | tf_op jit(solution)/shard_map/ppermute | solution.py:756
  12.6 0.4 collective-permute-start.5
  13.0 1.3 %shard_map.47 = (f32[8,16,512]{2,1,0:T(8,128)S(1)}, f32[8,16,512]{2,1,0:T(8,128)S(1)}, f32[8,16,512]{2,1,0:T(8,128)S(1)}, f32[7,16,512]{2,1,0:T(8,128)S(1)}, f32...) custom-call(s32[2]{0:T(128)S(1)} %pad_add_fusion.where_ref, ...), custom_call_target="tpu_custom_call" | custom-call | flops 20000000 | bytes 4000000 | tf_op jit(solution)/shard_map/pallas_call | solution.py:716
  14.4 0.0 collective-permute-done.4.cnear_ref
  14.4 2.2 %collective-permute-done.5.cfar_ref = f32[4,8,512]{2,1,0:T(8,128)S(1)} collective-permute-done((f32[4,8,512]{2,1,0:T(8,128)S(1)}, f32[4,8,512]{2,1,0:T(8,128)S(1)}, u32[]{:S(2)}, u32[]{:S(2)}) %collective-permute-start.5) | collective-permute-done | bytes 65568 | tf_op jit(solution)/shard_map/ppermute | solution.py:757
  16.6 1.6 %shard_map.48 = (f32[8,8,512]{2,1,0:T(8,128)S(1)}, f32[6,16,512]{2,1,0:T(8,128)S(1)}, f32[6,16,512]{2,1,0:T(8,128)S(1)}, f32[8,16,512]{2,1,0:T(8,128)S(1)}, f32[...) custom-call(s32[2]{0:T(128)S(1)} %pad_add_fusion.where_ref, ...), custom_call_target="tpu_custom_call" | custom-call | tf_op jit(solution)/shard_map/pallas_call | solution.py:716
  18.2 0.5 collective-permute-start.6
  18.7 3.8 %collective-permute-start.7 = (f32[5,8,512]{2,1,0:T(8,128)S(1)}, f32[5,8,512]{2,1,0:T(8,128)S(1)}, u32[]{:S(2)}, u32[]{:S(2)}) collective-permute-start(f32[5,8,512]{2,1,0:T(8,128)S(1)} %get-tuple-element.77), channel_id=1, source_target_pairs={{0,1},{1,0},{2,3},{3,2},{4,5},{5,4},{6,7},{7,6},{8,9},{9,8},{10,11... | collective-permute-start | bytes 245768 | tf_op jit(solution)/shard_map/ppermute | solution.py:762
  22.5 1.0 %collective-permute-start.8 = (f32[5,8,512]{2,1,0:T(8,128)S(1)}, f32[5,8,512]{2,1,0:T(8,128)S(1)}, u32[]{:S(2)}, u32[]{:S(2)}) collective-permute-start(f32[5,8,512]{2,1,0:T(8,128)S(1)} %get-tuple-element.78), channel_id=1, source_target_pairs={{0,1},{1,0},{2,3},{3,2},{4,5},{5,4},{6,7},{7,6},{8,9},{9,8},{10,11... | collective-permute-start | bytes 245768 | tf_op jit(solution)/shard_map/ppermute | solution.py:757
  23.5 0.0 collective-permute-start.9
  23.5 0.0 collective-permute-done.6.modd_ref
  23.5 1.2 %collective-permute-done.7.meven_ref = f32[5,8,512]{2,1,0:T(8,128)S(1)} collective-permute-done((f32[5,8,512]{2,1,0:T(8,128)S(1)}, f32[5,8,512]{2,1,0:T(8,128)S(1)}, u32[]{:S(2)}, u32[]{:S(2)}) %collective-permute-start.7) | collective-permute-done | bytes 81952 | tf_op jit(solution)/shard_map/ppermute | solution.py:762
  24.7 2.0 %collective-permute-done.8.far_ref = f32[5,8,512]{2,1,0:T(8,128)S(1)} collective-permute-done((f32[5,8,512]{2,1,0:T(8,128)S(1)}, f32[5,8,512]{2,1,0:T(8,128)S(1)}, u32[]{:S(2)}, u32[]{:S(2)}) %collective-permute-start.8) | collective-permute-done | bytes 81952 | tf_op jit(solution)/shard_map/ppermute | solution.py:757
  26.7 0.0 collective-permute-done.9.near_ref
  26.8 1.3 %collective-permute-start.10 = (f32[8,512]{1,0:T(8,128)S(1)}, f32[8,512]{1,0:T(8,128)S(1)}, u32[]{:S(2)}, u32[]{:S(2)}) collective-permute-start(f32[8,512]{1,0:T(8,128)S(1)} %get-tuple-element.130), channel_id=1, source_target_pairs={{0,32},{1,33},{2,34},{3,35},{4,36},{5,37},{6,38},{7,39},{8,40},{9,... | collective-permute-start | bytes 49160 | tf_op jit(solution)/shard_map/ppermute | solution.py:756
  28.2 0.0 collective-permute-start.11
  28.2 0.8 %collective-permute-done.10.cnear_ref = f32[8,512]{1,0:T(8,128)S(1)} collective-permute-done((f32[8,512]{1,0:T(8,128)S(1)}, f32[8,512]{1,0:T(8,128)S(1)}, u32[]{:S(2)}, u32[]{:S(2)}) %collective-permute-start.10) | collective-permute-done | bytes 16416 | tf_op jit(solution)/shard_map/ppermute | solution.py:756
  29.0 2.6 %collective-permute-done.11.cfar_ref = f32[8,512]{1,0:T(8,128)S(1)} collective-permute-done((f32[8,512]{1,0:T(8,128)S(1)}, f32[8,512]{1,0:T(8,128)S(1)}, u32[]{:S(2)}, u32[]{:S(2)}) %collective-permute-start.11) | collective-permute-done | bytes 16416 | tf_op jit(solution)/shard_map/ppermute | solution.py:757
  31.6 1.7 %shard_map.49 = f32[32,8,128]{2,1,0:T(8,128)} custom-call(s32[2]{0:T(128)S(1)} %pad_add_fusion.where_ref, f32[3,8,512]{2,1,0:T(8,128)S(1)} %get-tuple-element.75.block_ref, f32[5,8,512]{2,1,0:T(8,128)S(1)} %collective-permute-done.9.near_ref, f32[5,8,512]{2,1,0:T(8,128)S(1)} %collective-permute-done.8.far_ref, ...), custom_call_target="tpu_custom_call" | custom-call | tf_op jit(solution)/shard_map/pallas_call | solution.py:716
  33.3 8.0 %all-to-all-start = ((f32[32,8,128]{2,1,0:T(8,128)}), f32[32,8,128]{2,1,0:T(8,128)S(1)}, u32[]{:S(2)}, u32[]{:S(2)}) async-start(f32[32,8,128]{2,1,0:T(8,128)} %shard_map.49), calls=%async_computation | async-start | bytes 262144 | tf_op jit(solution)/shard_map/all_to_all | solution.py:812
  41.4 0.8 %collective-permute-start.12 = (f32[7,8,512]{2,1,0:T(8,128)S(1)}, f32[7,8,512]{2,1,0:T(8,128)S(1)}, u32[]{:S(2)}, u32[]{:S(2)}) collective-permute-start(f32[7,8,512]{2,1,0:T(8,128)S(1)} %maximum_maximum_fusion), channel_id=1, source_target_pairs={{0,32},{1,33},{2,34},{3,35},{4,36},{5,37},{6,38},{7,39},{8,40},{9,... | collective-permute-start | bytes 344072 | tf_op jit(solution)/shard_map/ppermute | solution.py:756
  42.1 0.0 collective-permute-start.13
  42.1 8.3 %all-to-all-done = f32[32,8,128]{2,1,0:T(8,128)S(1)} async-done(((f32[32,8,128]{2,1,0:T(8,128)}), f32[32,8,128]{2,1,0:T(8,128)S(1)}, u32[]{:S(2)}, u32[]{:S(2)}) %all-to-all-start) | async-done | bytes 131104 | tf_op jit(solution)/shard_map/all_to_all | solution.py:812
  50.5 0.0 collective-permute-done.12.cnear_ref
  50.5 0.0 collective-permute-done.13.cfar_ref
  50.5 0.1 collective-permute-start.14
  50.6 2.1 %collective-permute-start.15 = (f32[8,32,128]{2,1,0:T(8,128)S(1)}, f32[8,32,128]{2,1,0:T(8,128)S(1)}, u32[]{:S(2)}, u32[]{:S(2)}) collective-permute-start(f32[8,32,128]{2,1,0:T(8,128)S(1)} %bitcast.34), channel_id=1, source_target_pairs={{0,128},{1,129},{2,130},{3,131},{4,132},{5,133},{6,134},{7,135},{8... | collective-permute-start | bytes 393224 | tf_op jit(solution)/shard_map/ppermute | solution.py:826
  52.7 1.7 %collective-permute-start.16 = (f32[8,32,128]{2,1,0:T(8,128)S(1)}, f32[8,32,128]{2,1,0:T(8,128)S(1)}, u32[]{:S(2)}, u32[]{:S(2)}) collective-permute-start(f32[8,32,128]{2,1,0:T(8,128)S(1)} %bitcast.35), channel_id=1, source_target_pairs={{0,192},{1,193},{2,194},{3,195},{4,196},{5,197},{6,198},{7,199},{8... | collective-permute-start | bytes 393224 | tf_op jit(solution)/shard_map/ppermute | solution.py:826
  54.4 2.9 %collective-permute-start.17 = (f32[8,32,128]{2,1,0:T(8,128)S(1)}, f32[8,32,128]{2,1,0:T(8,128)S(1)}, u32[]{:S(2)}, u32[]{:S(2)}) collective-permute-start(f32[8,32,128]{2,1,0:T(8,128)S(1)} %bitcast.36), channel_id=1, source_target_pairs={{0,32},{1,33},{2,34},{3,35},{4,36},{5,37},{6,38},{7,39},{8,40},{9,... | collective-permute-start | bytes 393224 | tf_op jit(solution)/shard_map/ppermute | solution.py:828
  57.4 0.0 collective-permute-done.14.refs_1_
  57.4 0.5 collective-permute-start.18
  57.9 0.0 collective-permute-done.15.refs_2_
  57.9 2.3 %collective-permute-start.19 = (f32[8,32,128]{2,1,0:T(8,128)S(1)}, f32[8,32,128]{2,1,0:T(8,128)S(1)}, u32[]{:S(2)}, u32[]{:S(2)}) collective-permute-start(f32[8,32,128]{2,1,0:T(8,128)S(1)} %collective-permute-done.15.refs_2_), channel_id=1, source_target_pairs={{0,32},{1,33},{2,34},{3,35},{4,36},{5,37},{6,38},{7,39},{8,40},{9,... | collective-permute-start | bytes 393224 | tf_op jit(solution)/shard_map/ppermute | solution.py:828
  60.2 0.0 collective-permute-done.16.refs_3_
  60.2 1.8 %collective-permute-start.20 = (f32[8,32,128]{2,1,0:T(8,128)S(1)}, f32[8,32,128]{2,1,0:T(8,128)S(1)}, u32[]{:S(2)}, u32[]{:S(2)}) collective-permute-start(f32[8,32,128]{2,1,0:T(8,128)S(1)} %collective-permute-done.16.refs_3_), channel_id=1, source_target_pairs={{0,32},{1,33},{2,34},{3,35},{4,36},{5,37},{6,38},{7,39},{8,40},{9,... | collective-permute-start | bytes 393224 | tf_op jit(solution)/shard_map/ppermute | solution.py:828
  62.0 0.9 %shard_map.50 = (f32[12,16,512]{2,1,0:T(8,128)S(1)}, f32[12,16,256]{2,1,0:T(8,128)S(1)}, f32[12,16,256]{2,1,0:T(8,128)S(1)}, f32[12,16,256]{2,1,0:T(8,128)S(1)},...) custom-call(s32[2]{0:T(128)S(1)} %pad_add_fusion.where_ref, ...), custom_call_target="tpu_custom_call" | custom-call | flops 20000000 | bytes 4000000 | tf_op jit(solution)/shard_map/pallas_call | solution.py:716
  62.9 0.0 collective-permute-done.17.refs_4_
  62.9 0.0 collective-permute-done.18.refs_5_
  62.9 0.0 collective-permute-done.19.refs_6_
  63.0 0.1 collective-permute-done.20.refs_7_
  63.0 5.0 %shard_map.51 = f32[8,8,512]{2,1,0:T(8,128)} custom-call(s32[2]{0:T(128)S(1)} %pad_add_fusion.where_ref, f32[8,32,128]{2,1,0:T(8,128)S(1)} %bitcast.37, f32[8,32,128]{2,1,0:T(8,128)S(1)} %collective-permute-done.14.refs_1_, f32[8,32,128]{2,1,0:T(8,128)S(1)} %collective-permute-done.15.refs_2_, f32[8,32,128]{2,1,0:T(8,128)S(1)} %collective-permute-done.16.refs_3_, ...), custom_call_target="tpu_custom_call" | custom-call | tf_op jit(solution)/shard_map/pallas_call | solution.py:716
  (17 shorter events, 0.2 us)
Async XLA Ops:
  1.8 6.5 %collective-permute-start = (f32[8,8,512]{2,1,0:T(8,128)S(1)}, f32[8,8,512]{2,1,0:T(8,128)S(1)}, u32[]{:S(2)}, u32[]{:S(2)}) collective-permute-start(f32[8,8,512]{2,1,0:T(8,128)S(1)} %get-tuple-element.53), channel_id=1, source_target_pairs={{0,32},{1,2},{2,1},{3,4},{4,3},{5,6},{6,5},{7,8},{8,7},{9,10},{10,... | collective-permute-start | bytes 393224 | tf_op jit(solution)/shard_map/ppermute | solution.py:763
  5.1 5.1 %collective-permute-start.1 = (f32[8,8,512]{2,1,0:T(8,128)S(1)}, f32[8,8,512]{2,1,0:T(8,128)S(1)}, u32[]{:S(2)}, u32[]{:S(2)}) collective-permute-start(f32[8,8,512]{2,1,0:T(8,128)S(1)} %get-tuple-element.54), channel_id=1, source_target_pairs={{0,1},{1,0},{2,3},{3,2},{4,5},{5,4},{6,7},{7,6},{8,9},{9,8},{10,11... | collective-permute-start | bytes 393224 | tf_op jit(solution)/shard_map/ppermute | solution.py:762
  6.0 5.3 %collective-permute-start.2 = (f32[8,8,512]{2,1,0:T(8,128)S(1)}, f32[8,8,512]{2,1,0:T(8,128)S(1)}, u32[]{:S(2)}, u32[]{:S(2)}) collective-permute-start(f32[8,8,512]{2,1,0:T(8,128)S(1)} %get-tuple-element.55), channel_id=1, source_target_pairs={{0,1},{1,0},{2,3},{3,2},{4,5},{5,4},{6,7},{7,6},{8,9},{9,8},{10,11... | collective-permute-start | bytes 393224 | tf_op jit(solution)/shard_map/ppermute | solution.py:757
  8.3 2.9 %collective-permute-start.3 = (f32[8,8,512]{2,1,0:T(8,128)S(1)}, f32[8,8,512]{2,1,0:T(8,128)S(1)}, u32[]{:S(2)}, u32[]{:S(2)}) collective-permute-start(f32[8,8,512]{2,1,0:T(8,128)S(1)} %get-tuple-element.56), channel_id=1, source_target_pairs={{0,32},{1,33},{2,34},{3,35},{4,36},{5,37},{6,38},{7,39},{8,40},{9,... | collective-permute-start | bytes 393224 | tf_op jit(solution)/shard_map/ppermute | solution.py:756
  11.4 3.0 %collective-permute-start.4 = (f32[4,8,512]{2,1,0:T(8,128)S(1)}, f32[4,8,512]{2,1,0:T(8,128)S(1)}, u32[]{:S(2)}, u32[]{:S(2)}) collective-permute-start(f32[4,8,512]{2,1,0:T(8,128)S(1)} %get-tuple-element.106), channel_id=1, source_target_pairs={{0,32},{1,33},{2,34},{3,35},{4,36},{5,37},{6,38},{7,39},{8,40},{9,... | collective-permute-start | bytes 196616 | tf_op jit(solution)/shard_map/ppermute | solution.py:756
  12.6 4.0 %collective-permute-start.5 = (f32[4,8,512]{2,1,0:T(8,128)S(1)}, f32[4,8,512]{2,1,0:T(8,128)S(1)}, u32[]{:S(2)}, u32[]{:S(2)}) collective-permute-start(f32[4,8,512]{2,1,0:T(8,128)S(1)} %get-tuple-element.105), channel_id=1, source_target_pairs={{0,1},{1,0},{2,3},{3,2},{4,5},{5,4},{6,7},{7,6},{8,9},{9,8},{10,11... | collective-permute-start | bytes 196616 | tf_op jit(solution)/shard_map/ppermute | solution.py:757
  18.2 5.3 %collective-permute-start.6 = (f32[5,8,512]{2,1,0:T(8,128)S(1)}, f32[5,8,512]{2,1,0:T(8,128)S(1)}, u32[]{:S(2)}, u32[]{:S(2)}) collective-permute-start(f32[5,8,512]{2,1,0:T(8,128)S(1)} %get-tuple-element.76), channel_id=1, source_target_pairs={{0,32},{1,2},{2,1},{3,4},{4,3},{5,6},{6,5},{7,8},{8,7},{9,10},{10,... | collective-permute-start | bytes 245768 | tf_op jit(solution)/shard_map/ppermute | solution.py:763
  18.7 6.0 %collective-permute-start.7 = (f32[5,8,512]{2,1,0:T(8,128)S(1)}, f32[5,8,512]{2,1,0:T(8,128)S(1)}, u32[]{:S(2)}, u32[]{:S(2)}) collective-permute-start(f32[5,8,512]{2,1,0:T(8,128)S(1)} %get-tuple-element.77), channel_id=1, source_target_pairs={{0,1},{1,0},{2,3},{3,2},{4,5},{5,4},{6,7},{7,6},{8,9},{9,8},{10,11... | collective-permute-start | bytes 245768 | tf_op jit(solution)/shard_map/ppermute | solution.py:762
  22.5 4.2 %collective-permute-start.8 = (f32[5,8,512]{2,1,0:T(8,128)S(1)}, f32[5,8,512]{2,1,0:T(8,128)S(1)}, u32[]{:S(2)}, u32[]{:S(2)}) collective-permute-start(f32[5,8,512]{2,1,0:T(8,128)S(1)} %get-tuple-element.78), channel_id=1, source_target_pairs={{0,1},{1,0},{2,3},{3,2},{4,5},{5,4},{6,7},{7,6},{8,9},{9,8},{10,11... | collective-permute-start | bytes 245768 | tf_op jit(solution)/shard_map/ppermute | solution.py:757
  23.5 3.2 %collective-permute-start.9 = (f32[5,8,512]{2,1,0:T(8,128)S(1)}, f32[5,8,512]{2,1,0:T(8,128)S(1)}, u32[]{:S(2)}, u32[]{:S(2)}) collective-permute-start(f32[5,8,512]{2,1,0:T(8,128)S(1)} %get-tuple-element.79), channel_id=1, source_target_pairs={{0,32},{1,33},{2,34},{3,35},{4,36},{5,37},{6,38},{7,39},{8,40},{9,... | collective-permute-start | bytes 245768 | tf_op jit(solution)/shard_map/ppermute | solution.py:756
  26.8 2.2 %collective-permute-start.10 = (f32[8,512]{1,0:T(8,128)S(1)}, f32[8,512]{1,0:T(8,128)S(1)}, u32[]{:S(2)}, u32[]{:S(2)}) collective-permute-start(f32[8,512]{1,0:T(8,128)S(1)} %get-tuple-element.130), channel_id=1, source_target_pairs={{0,32},{1,33},{2,34},{3,35},{4,36},{5,37},{6,38},{7,39},{8,40},{9,... | collective-permute-start | bytes 49160 | tf_op jit(solution)/shard_map/ppermute | solution.py:756
  28.2 3.4 %collective-permute-start.11 = (f32[8,512]{1,0:T(8,128)S(1)}, f32[8,512]{1,0:T(8,128)S(1)}, u32[]{:S(2)}, u32[]{:S(2)}) collective-permute-start(f32[8,512]{1,0:T(8,128)S(1)} %get-tuple-element.129), channel_id=1, source_target_pairs={{0,1},{1,0},{2,3},{3,2},{4,5},{5,4},{6,7},{7,6},{8,9},{9,8},{10,11... | collective-permute-start | bytes 49160 | tf_op jit(solution)/shard_map/ppermute | solution.py:757
  33.3 17.2 %all-to-all-start = ((f32[32,8,128]{2,1,0:T(8,128)}), f32[32,8,128]{2,1,0:T(8,128)S(1)}, u32[]{:S(2)}, u32[]{:S(2)}) async-start(f32[32,8,128]{2,1,0:T(8,128)} %shard_map.49), calls=%async_computation | async-start | bytes 262144 | tf_op jit(solution)/shard_map/all_to_all | solution.py:812
  41.4 9.1 %collective-permute-start.12 = (f32[7,8,512]{2,1,0:T(8,128)S(1)}, f32[7,8,512]{2,1,0:T(8,128)S(1)}, u32[]{:S(2)}, u32[]{:S(2)}) collective-permute-start(f32[7,8,512]{2,1,0:T(8,128)S(1)} %maximum_maximum_fusion), channel_id=1, source_target_pairs={{0,32},{1,33},{2,34},{3,35},{4,36},{5,37},{6,38},{7,39},{8,40},{9,... | collective-permute-start | bytes 344072 | tf_op jit(solution)/shard_map/ppermute | solution.py:756
  42.1 8.4 %collective-permute-start.13 = (f32[7,8,512]{2,1,0:T(8,128)S(1)}, f32[7,8,512]{2,1,0:T(8,128)S(1)}, u32[]{:S(2)}, u32[]{:S(2)}) collective-permute-start(f32[7,8,512]{2,1,0:T(8,128)S(1)} %maximum_maximum_fusion), channel_id=1, source_target_pairs={{0,1},{1,0},{2,3},{3,2},{4,5},{5,4},{6,7},{7,6},{8,9},{9,8},{10,11... | collective-permute-start | bytes 344072 | tf_op jit(solution)/shard_map/ppermute | solution.py:757
  50.5 6.9 %collective-permute-start.14 = (f32[8,32,128]{2,1,0:T(8,128)S(1)}, f32[8,32,128]{2,1,0:T(8,128)S(1)}, u32[]{:S(2)}, u32[]{:S(2)}) collective-permute-start(f32[8,32,128]{2,1,0:T(8,128)S(1)} %bitcast.33), channel_id=1, source_target_pairs={{0,64},{1,65},{2,66},{3,67},{4,68},{5,69},{6,70},{7,71},{8,72},{9,... | collective-permute-start | bytes 393224 | tf_op jit(solution)/shard_map/ppermute | solution.py:826
  50.6 7.3 %collective-permute-start.15 = (f32[8,32,128]{2,1,0:T(8,128)S(1)}, f32[8,32,128]{2,1,0:T(8,128)S(1)}, u32[]{:S(2)}, u32[]{:S(2)}) collective-permute-start(f32[8,32,128]{2,1,0:T(8,128)S(1)} %bitcast.34), channel_id=1, source_target_pairs={{0,128},{1,129},{2,130},{3,131},{4,132},{5,133},{6,134},{7,135},{8... | collective-permute-start | bytes 393224 | tf_op jit(solution)/shard_map/ppermute | solution.py:826
  52.7 7.5 %collective-permute-start.16 = (f32[8,32,128]{2,1,0:T(8,128)S(1)}, f32[8,32,128]{2,1,0:T(8,128)S(1)}, u32[]{:S(2)}, u32[]{:S(2)}) collective-permute-start(f32[8,32,128]{2,1,0:T(8,128)S(1)} %bitcast.35), channel_id=1, source_target_pairs={{0,192},{1,193},{2,194},{3,195},{4,196},{5,197},{6,198},{7,199},{8... | collective-permute-start | bytes 393224 | tf_op jit(solution)/shard_map/ppermute | solution.py:826
  54.4 8.5 %collective-permute-start.17 = (f32[8,32,128]{2,1,0:T(8,128)S(1)}, f32[8,32,128]{2,1,0:T(8,128)S(1)}, u32[]{:S(2)}, u32[]{:S(2)}) collective-permute-start(f32[8,32,128]{2,1,0:T(8,128)S(1)} %bitcast.36), channel_id=1, source_target_pairs={{0,32},{1,33},{2,34},{3,35},{4,36},{5,37},{6,38},{7,39},{8,40},{9,... | collective-permute-start | bytes 393224 | tf_op jit(solution)/shard_map/ppermute | solution.py:828
  57.4 5.5 %collective-permute-start.18 = (f32[8,32,128]{2,1,0:T(8,128)S(1)}, f32[8,32,128]{2,1,0:T(8,128)S(1)}, u32[]{:S(2)}, u32[]{:S(2)}) collective-permute-start(f32[8,32,128]{2,1,0:T(8,128)S(1)} %collective-permute-done.14.refs_1_), channel_id=1, source_target_pairs={{0,32},{1,33},{2,34},{3,35},{4,36},{5,37},{6,38},{7,39},{8,40},{9,... | collective-permute-start | bytes 393224 | tf_op jit(solution)/shard_map/ppermute | solution.py:828
  57.9 5.0 %collective-permute-start.19 = (f32[8,32,128]{2,1,0:T(8,128)S(1)}, f32[8,32,128]{2,1,0:T(8,128)S(1)}, u32[]{:S(2)}, u32[]{:S(2)}) collective-permute-start(f32[8,32,128]{2,1,0:T(8,128)S(1)} %collective-permute-done.15.refs_2_), channel_id=1, source_target_pairs={{0,32},{1,33},{2,34},{3,35},{4,36},{5,37},{6,38},{7,39},{8,40},{9,... | collective-permute-start | bytes 393224 | tf_op jit(solution)/shard_map/ppermute | solution.py:828
  60.2 2.8 %collective-permute-start.20 = (f32[8,32,128]{2,1,0:T(8,128)S(1)}, f32[8,32,128]{2,1,0:T(8,128)S(1)}, u32[]{:S(2)}, u32[]{:S(2)}) collective-permute-start(f32[8,32,128]{2,1,0:T(8,128)S(1)} %collective-permute-done.16.refs_3_), channel_id=1, source_target_pairs={{0,32},{1,33},{2,34},{3,35},{4,36},{5,37},{6,38},{7,39},{8,40},{9,... | collective-permute-start | bytes 393224 | tf_op jit(solution)/shard_map/ppermute | solution.py:828

commit v3 on v1

--- a/solution.py
+++ b/solution.py
@@ -717,7 +717,7 @@
     )
     yeven, yodd = swap_y(yeven, yodd)
     near, far = swap_x(near, far)
-    yodd, yeven, far, near = lax.optimization_barrier((yodd, yeven, far, near))
+    yodd, far, yeven, near = lax.optimization_barrier((yodd, far, yeven, near))
     cnear, cfar = swap_x(*corner_messages(nx, ny, yeven, yodd))
     ksx, vsx, rsx, cxx, cyx, czx, wix, v1x, v2x, restx, kcx = run(
         functools.partial(early0_kernel, ny),
@@ -739,7 +739,7 @@
     )
     meven, modd = swap_y(meven, modd)
     mnear, mfar = swap_x(mnear, mfar)
-    modd, meven, mfar, mnear = lax.optimization_barrier((modd, meven, mfar, mnear))
+    modd, mfar, meven, mnear = lax.optimization_barrier((modd, mfar, meven, mnear))
     corner = corner1_message(ny, meven, modd)
     cnear, cfar = swap_x(corner, corner)
     v0x, v1, f1, w1, cx1, cy1, cz1, send = run(

time: 67.1 us -> 68.5 us (1.021)
  starting transfers between devices: 31.7 us -> 32.6 us
    ppermute x4, starting transfers between devices: 7.68 us -> 3.15 us  [swap_x(): lax.ppermute(far, both, pairs(far_x))]
    ppermute x4, starting transfers between devices: 2.47 us -> 5.85 us  [swap_x(): lax.ppermute(near, both, pairs(lambda x, y: (x ^ 1, y)))]
    ppermute x2, starting transfers between devices: 3.6 us -> 6.52 us  [swap_y(): lax.ppermute(near, both, pairs(lambda x, y: (x, y ^ 1)))]
    ppermute x4, waiting for transfers between devices: 4.1 us -> 1.95 us  [swap_x(): lax.ppermute(far, both, pairs(far_x))]
    ppermute x4, waiting for transfers between devices: 0.01 us -> 1.33 us  [swap_x(): lax.ppermute(near, both, pairs(lambda x, y: (x ^ 1, y)))]
    ppermute x2, starting transfers between devices: 5.16 us -> 4.3 us  [swap_y(): lax.ppermute(far, both, pairs(far_y))]
    ppermute x2, waiting for transfers between devices: 1.86 us -> 2.56 us  [swap_y(): lax.ppermute(near, both, pairs(lambda x, y: (x, y ^ 1)))]
  transfers between devices with their start and end apart: 19 -> 19, of which waited for: 6 -> 9; matrix products, arithmetic and copies ran while one was open for 0% -> 0% of each run, Pallas kernels for 2% -> 2%
where the time goes in v3:
time: 68.5 us; the launch traced here: 68.4 us
  starting transfers between devices  32.6 us (48%)
  blocking collectives  17.7 us (26%)
  Pallas kernels  10.9 us (16%)
  waiting for transfers between devices  6.84 us (10%)
    all_to_all x1, blocking collectives, body(): column = jnp.transpose(lax.all_to_all(send, 'gy', 0, 0), (1, 0, 2))  17.7 us
    pallas_call x5, Pallas kernels, run(): pl.pallas_call(kernel, out_shape=[jax.ShapeDtypeStruct(shape, F32) for sh...  10.9 us
    ppermute x4, starting transfers between devices, body(): lax.ppermute(c, both, pairs(lambda x, y: (x ^ 1, y)))  9.44 us
    ppermute x2, starting transfers between devices, swap_y(): lax.ppermute(near, both, pairs(lambda x, y: (x, y ^ 1)))  6.52 us
    ppermute x4, starting transfers between devices, swap_x(): lax.ppermute(near, both, pairs(lambda x, y: (x ^ 1, y)))  5.85 us
    ppermute x2, starting transfers between devices, swap_y(): lax.ppermute(far, both, pairs(far_y))  4.3 us
    ppermute x3, starting transfers between devices, body(): mine[j] = lax.ppermute(column, both, chips_apart(j))  3.34 us
    ppermute x4, starting transfers between devices, swap_x(): lax.ppermute(far, both, pairs(far_x))  3.15 us
  transfers between devices with their start and end apart: 19, of which 9 were waited for; matrix products, arithmetic and copies ran while one was open for 0% of the time, Pallas kernels for 2%

profile of v3, /device:TPU:1, one launch (start us, length us, event | category | flops | bytes accessed | tf_op | source)
XLA Modules:
  0.0 68.4 jit_solution(16182618963476096510)
XLA Ops:
  0.0 0.1 pad_add_fusion.where_ref
  0.1 1.7 %shard_map.46 = (f32[8,8,512]{2,1,0:T(8,128)S(1)}, f32[8,8,512]{2,1,0:T(8,128)S(1)}, f32[8,8,512]{2,1,0:T(8,128)S(1)}, f32[8,8,512]{2,1,0:T(8,128)S(1)}, f32[8,8...) custom-call(s32[2]{0:T(128)S(1)} %pad_add_fusion.where_ref, f32[3]{0:T(128)} %table_hbm.1, ...), custom_call_target="tpu_custom_call" | custom-call | tf_op jit(solution)/shard_map/pallas_call | solution.py:655
  1.8 3.3 %collective-permute-start = (f32[8,8,512]{2,1,0:T(8,128)S(1)}, f32[8,8,512]{2,1,0:T(8,128)S(1)}, u32[]{:S(2)}, u32[]{:S(2)}) collective-permute-start(f32[8,8,512]{2,1,0:T(8,128)S(1)} %get-tuple-element.50), channel_id=1, source_target_pairs={{0,32},{1,2},{2,1},{3,4},{4,3},{5,6},{6,5},{7,8},{8,7},{9,10},{10,... | collective-permute-start | bytes 393224 | tf_op jit(solution)/shard_map/ppermute | solution.py:702
  5.1 0.0 collective-permute-start.1
  5.1 2.9 %collective-permute-start.2 = (f32[8,8,512]{2,1,0:T(8,128)S(1)}, f32[8,8,512]{2,1,0:T(8,128)S(1)}, u32[]{:S(2)}, u32[]{:S(2)}) collective-permute-start(f32[8,8,512]{2,1,0:T(8,128)S(1)} %get-tuple-element.52), channel_id=1, source_target_pairs={{0,1},{1,0},{2,3},{3,2},{4,5},{5,4},{6,7},{7,6},{8,9},{9,8},{10,11... | collective-permute-start | bytes 393224 | tf_op jit(solution)/shard_map/ppermute | solution.py:701
  8.0 0.0 collective-permute-start.3
  8.0 0.0 collective-permute-done.odd_ref
  8.0 1.8 %collective-permute-done.1.far_ref = f32[8,8,512]{2,1,0:T(8,128)S(1)} collective-permute-done((f32[8,8,512]{2,1,0:T(8,128)S(1)}, f32[8,8,512]{2,1,0:T(8,128)S(1)}, u32[]{:S(2)}, u32[]{:S(2)}) %collective-permute-start.1) | collective-permute-done | bytes 131104 | tf_op jit(solution)/shard_map/ppermute | solution.py:696
  9.8 2.2 %collective-permute-done.2.even_ref = f32[8,8,512]{2,1,0:T(8,128)S(1)} collective-permute-done((f32[8,8,512]{2,1,0:T(8,128)S(1)}, f32[8,8,512]{2,1,0:T(8,128)S(1)}, u32[]{:S(2)}, u32[]{:S(2)}) %collective-permute-start.2) | collective-permute-done | bytes 131104 | tf_op jit(solution)/shard_map/ppermute | solution.py:701
  12.0 0.0 collective-permute-done.3.near_ref
  12.1 1.0 %collective-permute-start.5 = (f32[4,8,512]{2,1,0:T(8,128)S(1)}, f32[4,8,512]{2,1,0:T(8,128)S(1)}, u32[]{:S(2)}, u32[]{:S(2)}) collective-permute-start(f32[4,8,512]{2,1,0:T(8,128)S(1)} %get-tuple-element.99), channel_id=1, source_target_pairs={{0,1},{1,0},{2,3},{3,2},{4,5},{5,4},{6,7},{7,6},{8,9},{9,8},{10,11... | collective-permute-start | bytes 196616 | tf_op jit(solution)/shard_map/ppermute | solution.py:696
  13.1 2.1 %collective-permute-start.4 = (f32[4,8,512]{2,1,0:T(8,128)S(1)}, f32[4,8,512]{2,1,0:T(8,128)S(1)}, u32[]{:S(2)}, u32[]{:S(2)}) collective-permute-start(f32[4,8,512]{2,1,0:T(8,128)S(1)} %get-tuple-element.100), channel_id=1, source_target_pairs={{0,32},{1,33},{2,34},{3,35},{4,36},{5,37},{6,38},{7,39},{8,40},{9,... | collective-permute-start | bytes 196616 | tf_op jit(solution)/shard_map/ppermute | solution.py:695
  15.2 1.3 %shard_map.47 = (f32[8,16,512]{2,1,0:T(8,128)S(1)}, f32[8,16,512]{2,1,0:T(8,128)S(1)}, f32[8,16,512]{2,1,0:T(8,128)S(1)}, f32[7,16,512]{2,1,0:T(8,128)S(1)}, f32...) custom-call(s32[2]{0:T(128)S(1)} %pad_add_fusion.where_ref, ...), custom_call_target="tpu_custom_call" | custom-call | flops 20000000 | bytes 4000000 | tf_op jit(solution)/shard_map/pallas_call | solution.py:655
  16.5 0.0 collective-permute-done.5.cfar_ref
  16.5 0.0 collective-permute-done.4.cnear_ref
  16.6 1.6 %shard_map.48 = (f32[8,8,512]{2,1,0:T(8,128)S(1)}, f32[6,16,512]{2,1,0:T(8,128)S(1)}, f32[6,16,512]{2,1,0:T(8,128)S(1)}, f32[8,16,512]{2,1,0:T(8,128)S(1)}, f32[...) custom-call(s32[2]{0:T(128)S(1)} %pad_add_fusion.where_ref, ...), custom_call_target="tpu_custom_call" | custom-call | tf_op jit(solution)/shard_map/pallas_call | solution.py:655
  18.2 1.0 %collective-permute-start.6 = (f32[5,8,512]{2,1,0:T(8,128)S(1)}, f32[5,8,512]{2,1,0:T(8,128)S(1)}, u32[]{:S(2)}, u32[]{:S(2)}) collective-permute-start(f32[5,8,512]{2,1,0:T(8,128)S(1)} %get-tuple-element.74), channel_id=1, source_target_pairs={{0,32},{1,2},{2,1},{3,4},{4,3},{5,6},{6,5},{7,8},{8,7},{9,10},{10,... | collective-permute-start | bytes 245768 | tf_op jit(solution)/shard_map/ppermute | solution.py:702
  19.2 0.0 collective-permute-start.7
  19.2 3.6 %collective-permute-start.8 = (f32[5,8,512]{2,1,0:T(8,128)S(1)}, f32[5,8,512]{2,1,0:T(8,128)S(1)}, u32[]{:S(2)}, u32[]{:S(2)}) collective-permute-start(f32[5,8,512]{2,1,0:T(8,128)S(1)} %get-tuple-element.76), channel_id=1, source_target_pairs={{0,1},{1,0},{2,3},{3,2},{4,5},{5,4},{6,7},{7,6},{8,9},{9,8},{10,11... | collective-permute-start | bytes 245768 | tf_op jit(solution)/shard_map/ppermute | solution.py:701
  22.8 1.5 %collective-permute-start.9 = (f32[5,8,512]{2,1,0:T(8,128)S(1)}, f32[5,8,512]{2,1,0:T(8,128)S(1)}, u32[]{:S(2)}, u32[]{:S(2)}) collective-permute-start(f32[5,8,512]{2,1,0:T(8,128)S(1)} %get-tuple-element.77), channel_id=1, source_target_pairs={{0,32},{1,33},{2,34},{3,35},{4,36},{5,37},{6,38},{7,39},{8,40},{9,... | collective-permute-start | bytes 245768 | tf_op jit(solution)/shard_map/ppermute | solution.py:695
  24.2 0.0 collective-permute-done.6.modd_ref
  24.2 0.0 collective-permute-done.7.far_ref
  24.2 0.4 collective-permute-done.8.meven_ref
  24.6 0.5 collective-permute-done.9.near_ref
  25.2 2.2 %collective-permute-start.11 = (f32[7,8,512]{2,1,0:T(8,128)S(1)}, f32[7,8,512]{2,1,0:T(8,128)S(1)}, u32[]{:S(2)}, u32[]{:S(2)}) collective-permute-start(f32[7,8,512]{2,1,0:T(8,128)S(1)} %maximum_maximum_fusion), channel_id=1, source_target_pairs={{0,1},{1,0},{2,3},{3,2},{4,5},{5,4},{6,7},{7,6},{8,9},{9,8},{10,11... | collective-permute-start | bytes 344072 | tf_op jit(solution)/shard_map/ppermute | solution.py:696
  27.4 2.3 %collective-permute-start.10 = (f32[7,8,512]{2,1,0:T(8,128)S(1)}, f32[7,8,512]{2,1,0:T(8,128)S(1)}, u32[]{:S(2)}, u32[]{:S(2)}) collective-permute-start(f32[7,8,512]{2,1,0:T(8,128)S(1)} %maximum_maximum_fusion), channel_id=1, source_target_pairs={{0,32},{1,33},{2,34},{3,35},{4,36},{5,37},{6,38},{7,39},{8,40},{9,... | collective-permute-start | bytes 344072 | tf_op jit(solution)/shard_map/ppermute | solution.py:695
  29.7 0.2 collective-permute-done.11.cfar_ref
  29.9 0.8 %collective-permute-done.10.cnear_ref = f32[7,8,512]{2,1,0:T(8,128)S(1)} collective-permute-done((f32[7,8,512]{2,1,0:T(8,128)S(1)}, f32[7,8,512]{2,1,0:T(8,128)S(1)}, u32[]{:S(2)}, u32[]{:S(2)}) %collective-permute-start.10) | collective-permute-done | bytes 114720 | tf_op jit(solution)/shard_map/ppermute | solution.py:695
  30.7 1.1 %shard_map.49 = (f32[12,16,512]{2,1,0:T(8,128)S(1)}, f32[12,16,256]{2,1,0:T(8,128)S(1)}, f32[12,16,256]{2,1,0:T(8,128)S(1)}, f32[12,16,256]{2,1,0:T(8,128)S(1)},...) custom-call(s32[2]{0:T(128)S(1)} %pad_add_fusion.where_ref, ...), custom_call_target="tpu_custom_call" | custom-call | tf_op jit(solution)/shard_map/pallas_call | solution.py:655
  31.8 17.7 %all_to_all.5 = f32[32,8,128]{2,1,0:T(8,128)S(1)} all-to-all(f32[32,8,128]{2,1,0:T(8,128)S(1)} %get-tuple-element.82), channel_id=1, replica_groups=mesh['gx'=8,'gy'=32] {'gy'}, dimensions={0} | all-to-all | bytes 262144 | tf_op jit(solution)/shard_map/all_to_all | solution.py:751
  49.5 0.8 %collective-permute-start.14 = (f32[8,32,128]{2,1,0:T(8,128)S(1)}, f32[8,32,128]{2,1,0:T(8,128)S(1)}, u32[]{:S(2)}, u32[]{:S(2)}) collective-permute-start(f32[8,32,128]{2,1,0:T(8,128)S(1)} %bitcast.5), channel_id=1, source_target_pairs={{0,192},{1,193},{2,194},{3,195},{4,196},{5,197},{6,198},{7,199},{8... | collective-permute-start | bytes 393224 | tf_op jit(solution)/shard_map/ppermute | solution.py:758
  50.3 2.4 %collective-permute-start.13 = (f32[8,32,128]{2,1,0:T(8,128)S(1)}, f32[8,32,128]{2,1,0:T(8,128)S(1)}, u32[]{:S(2)}, u32[]{:S(2)}) collective-permute-start(f32[8,32,128]{2,1,0:T(8,128)S(1)} %bitcast.6), channel_id=1, source_target_pairs={{0,128},{1,129},{2,130},{3,131},{4,132},{5,133},{6,134},{7,135},{8... | collective-permute-start | bytes 393224 | tf_op jit(solution)/shard_map/ppermute | solution.py:758
  52.6 0.2 collective-permute-start.12
  52.8 5.1 %collective-permute-start.15 = (f32[8,32,128]{2,1,0:T(8,128)S(1)}, f32[8,32,128]{2,1,0:T(8,128)S(1)}, u32[]{:S(2)}, u32[]{:S(2)}) collective-permute-start(f32[8,32,128]{2,1,0:T(8,128)S(1)} %bitcast.8), channel_id=1, source_target_pairs={{0,32},{1,33},{2,34},{3,35},{4,36},{5,37},{6,38},{7,39},{8,40},{9,... | collective-permute-start | bytes 393224 | tf_op jit(solution)/shard_map/ppermute | solution.py:760
  58.0 0.0 collective-permute-done.14.refs_3_
  58.0 3.5 %collective-permute-start.18 = (f32[8,32,128]{2,1,0:T(8,128)S(1)}, f32[8,32,128]{2,1,0:T(8,128)S(1)}, u32[]{:S(2)}, u32[]{:S(2)}) collective-permute-start(f32[8,32,128]{2,1,0:T(8,128)S(1)} %collective-permute-done.14.refs_3_), channel_id=1, source_target_pairs={{0,32},{1,33},{2,34},{3,35},{4,36},{5,37},{6,38},{7,39},{8,40},{9,... | collective-permute-start | bytes 393224 | tf_op jit(solution)/shard_map/ppermute | solution.py:760
  61.4 0.0 collective-permute-done.13.refs_2_
  61.4 0.0 collective-permute-start.17
  61.5 0.0 collective-permute-done.12.refs_1_
  61.5 0.8 %collective-permute-start.16 = (f32[8,32,128]{2,1,0:T(8,128)S(1)}, f32[8,32,128]{2,1,0:T(8,128)S(1)}, u32[]{:S(2)}, u32[]{:S(2)}) collective-permute-start(f32[8,32,128]{2,1,0:T(8,128)S(1)} %collective-permute-done.12.refs_1_), channel_id=1, source_target_pairs={{0,32},{1,33},{2,34},{3,35},{4,36},{5,37},{6,38},{7,39},{8,40},{9,... | collective-permute-start | bytes 393224 | tf_op jit(solution)/shard_map/ppermute | solution.py:760
  62.3 0.0 collective-permute-done.15.refs_4_
  62.3 0.1 collective-permute-done.18.refs_7_
  62.4 0.4 collective-permute-done.17.refs_6_
  62.8 0.5 collective-permute-done.16.refs_5_
  63.3 5.1 %shard_map.50 = f32[8,8,512]{2,1,0:T(8,128)} custom-call(s32[2]{0:T(128)S(1)} %pad_add_fusion.where_ref, f32[8,32,128]{2,1,0:T(8,128)S(1)} %bitcast.9, f32[8,32,128]{2,1,0:T(8,128)S(1)} %collective-permute-done.12.refs_1_, f32[8,32,128]{2,1,0:T(8,128)S(1)} %collective-permute-done.13.refs_2_, f32[8,32,128]{2,1,0:T(8,128)S(1)} %collective-permute-done.14.refs_3_, ...), custom_call_target="tpu_custom_call" | custom-call | tf_op jit(solution)/shard_map/pallas_call | solution.py:655
  (12 shorter events, 0.1 us)
Async XLA Ops:
  1.8 6.2 %collective-permute-start = (f32[8,8,512]{2,1,0:T(8,128)S(1)}, f32[8,8,512]{2,1,0:T(8,128)S(1)}, u32[]{:S(2)}, u32[]{:S(2)}) collective-permute-start(f32[8,8,512]{2,1,0:T(8,128)S(1)} %get-tuple-element.50), channel_id=1, source_target_pairs={{0,32},{1,2},{2,1},{3,4},{4,3},{5,6},{6,5},{7,8},{8,7},{9,10},{10,... | collective-permute-start | bytes 393224 | tf_op jit(solution)/shard_map/ppermute | solution.py:702
  5.1 4.7 %collective-permute-start.1 = (f32[8,8,512]{2,1,0:T(8,128)S(1)}, f32[8,8,512]{2,1,0:T(8,128)S(1)}, u32[]{:S(2)}, u32[]{:S(2)}) collective-permute-start(f32[8,8,512]{2,1,0:T(8,128)S(1)} %get-tuple-element.51), channel_id=1, source_target_pairs={{0,1},{1,0},{2,3},{3,2},{4,5},{5,4},{6,7},{7,6},{8,9},{9,8},{10,11... | collective-permute-start | bytes 393224 | tf_op jit(solution)/shard_map/ppermute | solution.py:696
  5.1 6.9 %collective-permute-start.2 = (f32[8,8,512]{2,1,0:T(8,128)S(1)}, f32[8,8,512]{2,1,0:T(8,128)S(1)}, u32[]{:S(2)}, u32[]{:S(2)}) collective-permute-start(f32[8,8,512]{2,1,0:T(8,128)S(1)} %get-tuple-element.52), channel_id=1, source_target_pairs={{0,1},{1,0},{2,3},{3,2},{4,5},{5,4},{6,7},{7,6},{8,9},{9,8},{10,11... | collective-permute-start | bytes 393224 | tf_op jit(solution)/shard_map/ppermute | solution.py:701
  8.0 4.0 %collective-permute-start.3 = (f32[8,8,512]{2,1,0:T(8,128)S(1)}, f32[8,8,512]{2,1,0:T(8,128)S(1)}, u32[]{:S(2)}, u32[]{:S(2)}) collective-permute-start(f32[8,8,512]{2,1,0:T(8,128)S(1)} %get-tuple-element.53), channel_id=1, source_target_pairs={{0,32},{1,33},{2,34},{3,35},{4,36},{5,37},{6,38},{7,39},{8,40},{9,... | collective-permute-start | bytes 393224 | tf_op jit(solution)/shard_map/ppermute | solution.py:695
  12.1 4.4 %collective-permute-start.5 = (f32[4,8,512]{2,1,0:T(8,128)S(1)}, f32[4,8,512]{2,1,0:T(8,128)S(1)}, u32[]{:S(2)}, u32[]{:S(2)}) collective-permute-start(f32[4,8,512]{2,1,0:T(8,128)S(1)} %get-tuple-element.99), channel_id=1, source_target_pairs={{0,1},{1,0},{2,3},{3,2},{4,5},{5,4},{6,7},{7,6},{8,9},{9,8},{10,11... | collective-permute-start | bytes 196616 | tf_op jit(solution)/shard_map/ppermute | solution.py:696
  13.1 3.5 %collective-permute-start.4 = (f32[4,8,512]{2,1,0:T(8,128)S(1)}, f32[4,8,512]{2,1,0:T(8,128)S(1)}, u32[]{:S(2)}, u32[]{:S(2)}) collective-permute-start(f32[4,8,512]{2,1,0:T(8,128)S(1)} %get-tuple-element.100), channel_id=1, source_target_pairs={{0,32},{1,33},{2,34},{3,35},{4,36},{5,37},{6,38},{7,39},{8,40},{9,... | collective-permute-start | bytes 196616 | tf_op jit(solution)/shard_map/ppermute | solution.py:695
  18.2 6.0 %collective-permute-start.6 = (f32[5,8,512]{2,1,0:T(8,128)S(1)}, f32[5,8,512]{2,1,0:T(8,128)S(1)}, u32[]{:S(2)}, u32[]{:S(2)}) collective-permute-start(f32[5,8,512]{2,1,0:T(8,128)S(1)} %get-tuple-element.74), channel_id=1, source_target_pairs={{0,32},{1,2},{2,1},{3,4},{4,3},{5,6},{6,5},{7,8},{8,7},{9,10},{10,... | collective-permute-start | bytes 245768 | tf_op jit(solution)/shard_map/ppermute | solution.py:702
  19.2 5.1 %collective-permute-start.7 = (f32[5,8,512]{2,1,0:T(8,128)S(1)}, f32[5,8,512]{2,1,0:T(8,128)S(1)}, u32[]{:S(2)}, u32[]{:S(2)}) collective-permute-start(f32[5,8,512]{2,1,0:T(8,128)S(1)} %get-tuple-element.75), channel_id=1, source_target_pairs={{0,1},{1,0},{2,3},{3,2},{4,5},{5,4},{6,7},{7,6},{8,9},{9,8},{10,11... | collective-permute-start | bytes 245768 | tf_op jit(solution)/shard_map/ppermute | solution.py:696
  19.2 5.4 %collective-permute-start.8 = (f32[5,8,512]{2,1,0:T(8,128)S(1)}, f32[5,8,512]{2,1,0:T(8,128)S(1)}, u32[]{:S(2)}, u32[]{:S(2)}) collective-permute-start(f32[5,8,512]{2,1,0:T(8,128)S(1)} %get-tuple-element.76), channel_id=1, source_target_pairs={{0,1},{1,0},{2,3},{3,2},{4,5},{5,4},{6,7},{7,6},{8,9},{9,8},{10,11... | collective-permute-start | bytes 245768 | tf_op jit(solution)/shard_map/ppermute | solution.py:701
  22.8 2.4 %collective-permute-start.9 = (f32[5,8,512]{2,1,0:T(8,128)S(1)}, f32[5,8,512]{2,1,0:T(8,128)S(1)}, u32[]{:S(2)}, u32[]{:S(2)}) collective-permute-start(f32[5,8,512]{2,1,0:T(8,128)S(1)} %get-tuple-element.77), channel_id=1, source_target_pairs={{0,32},{1,33},{2,34},{3,35},{4,36},{5,37},{6,38},{7,39},{8,40},{9,... | collective-permute-start | bytes 245768 | tf_op jit(solution)/shard_map/ppermute | solution.py:695
  25.2 4.6 %collective-permute-start.11 = (f32[7,8,512]{2,1,0:T(8,128)S(1)}, f32[7,8,512]{2,1,0:T(8,128)S(1)}, u32[]{:S(2)}, u32[]{:S(2)}) collective-permute-start(f32[7,8,512]{2,1,0:T(8,128)S(1)} %maximum_maximum_fusion), channel_id=1, source_target_pairs={{0,1},{1,0},{2,3},{3,2},{4,5},{5,4},{6,7},{7,6},{8,9},{9,8},{10,11... | collective-permute-start | bytes 344072 | tf_op jit(solution)/shard_map/ppermute | solution.py:696
  27.4 3.3 %collective-permute-start.10 = (f32[7,8,512]{2,1,0:T(8,128)S(1)}, f32[7,8,512]{2,1,0:T(8,128)S(1)}, u32[]{:S(2)}, u32[]{:S(2)}) collective-permute-start(f32[7,8,512]{2,1,0:T(8,128)S(1)} %maximum_maximum_fusion), channel_id=1, source_target_pairs={{0,32},{1,33},{2,34},{3,35},{4,36},{5,37},{6,38},{7,39},{8,40},{9,... | collective-permute-start | bytes 344072 | tf_op jit(solution)/shard_map/ppermute | solution.py:695
  49.5 8.5 %collective-permute-start.14 = (f32[8,32,128]{2,1,0:T(8,128)S(1)}, f32[8,32,128]{2,1,0:T(8,128)S(1)}, u32[]{:S(2)}, u32[]{:S(2)}) collective-permute-start(f32[8,32,128]{2,1,0:T(8,128)S(1)} %bitcast.5), channel_id=1, source_target_pairs={{0,192},{1,193},{2,194},{3,195},{4,196},{5,197},{6,198},{7,199},{8... | collective-permute-start | bytes 393224 | tf_op jit(solution)/shard_map/ppermute | solution.py:758
  50.3 11.2 %collective-permute-start.13 = (f32[8,32,128]{2,1,0:T(8,128)S(1)}, f32[8,32,128]{2,1,0:T(8,128)S(1)}, u32[]{:S(2)}, u32[]{:S(2)}) collective-permute-start(f32[8,32,128]{2,1,0:T(8,128)S(1)} %bitcast.6), channel_id=1, source_target_pairs={{0,128},{1,129},{2,130},{3,131},{4,132},{5,133},{6,134},{7,135},{8... | collective-permute-start | bytes 393224 | tf_op jit(solution)/shard_map/ppermute | solution.py:758
  52.6 8.8 %collective-permute-start.12 = (f32[8,32,128]{2,1,0:T(8,128)S(1)}, f32[8,32,128]{2,1,0:T(8,128)S(1)}, u32[]{:S(2)}, u32[]{:S(2)}) collective-permute-start(f32[8,32,128]{2,1,0:T(8,128)S(1)} %bitcast.7), channel_id=1, source_target_pairs={{0,64},{1,65},{2,66},{3,67},{4,68},{5,69},{6,70},{7,71},{8,72},{9,... | collective-permute-start | bytes 393224 | tf_op jit(solution)/shard_map/ppermute | solution.py:758
  52.8 9.5 %collective-permute-start.15 = (f32[8,32,128]{2,1,0:T(8,128)S(1)}, f32[8,32,128]{2,1,0:T(8,128)S(1)}, u32[]{:S(2)}, u32[]{:S(2)}) collective-permute-start(f32[8,32,128]{2,1,0:T(8,128)S(1)} %bitcast.8), channel_id=1, source_target_pairs={{0,32},{1,33},{2,34},{3,35},{4,36},{5,37},{6,38},{7,39},{8,40},{9,... | collective-permute-start | bytes 393224 | tf_op jit(solution)/shard_map/ppermute | solution.py:760
  58.0 4.5 %collective-permute-start.18 = (f32[8,32,128]{2,1,0:T(8,128)S(1)}, f32[8,32,128]{2,1,0:T(8,128)S(1)}, u32[]{:S(2)}, u32[]{:S(2)}) collective-permute-start(f32[8,32,128]{2,1,0:T(8,128)S(1)} %collective-permute-done.14.refs_3_), channel_id=1, source_target_pairs={{0,32},{1,33},{2,34},{3,35},{4,36},{5,37},{6,38},{7,39},{8,40},{9,... | collective-permute-start | bytes 393224 | tf_op jit(solution)/shard_map/ppermute | solution.py:760
  61.4 1.3 %collective-permute-start.17 = (f32[8,32,128]{2,1,0:T(8,128)S(1)}, f32[8,32,128]{2,1,0:T(8,128)S(1)}, u32[]{:S(2)}, u32[]{:S(2)}) collective-permute-start(f32[8,32,128]{2,1,0:T(8,128)S(1)} %collective-permute-done.13.refs_2_), channel_id=1, source_target_pairs={{0,32},{1,33},{2,34},{3,35},{4,36},{5,37},{6,38},{7,39},{8,40},{9,... | collective-permute-start | bytes 393224 | tf_op jit(solution)/shard_map/ppermute | solution.py:760
  61.5 1.8 %collective-permute-start.16 = (f32[8,32,128]{2,1,0:T(8,128)S(1)}, f32[8,32,128]{2,1,0:T(8,128)S(1)}, u32[]{:S(2)}, u32[]{:S(2)}) collective-permute-start(f32[8,32,128]{2,1,0:T(8,128)S(1)} %collective-permute-done.12.refs_1_), channel_id=1, source_target_pairs={{0,32},{1,33},{2,34},{3,35},{4,36},{5,37},{6,38},{7,39},{8,40},{9,... | collective-permute-start | bytes 393224 | tf_op jit(solution)/shard_map/ppermute | solution.py:760

commit v4 on v1

--- a/solution.py
+++ b/solution.py
@@ -265,7 +265,7 @@
 def down0_kernel(
     nx, ny, where_ref, near_ref, far_ref, cnear_ref, cfar_ref,
     ks_own, vs_own, rs_own, cx_own, cy_own, cz_own, wi_own, v1_own, v2_own, rest_own, kc,
-    v0_ref, rs, cx, cy, cz, wi, block_ref, mnear_ref, mfar_ref, meven_ref, modd_ref,
+    v0_ref, rs, cx, cy, cz, wi, block_ref, mnear_ref, mfar_ref,
     ks, vs, v1, v2, pair, fine, coarse,
 ):
     even, outside = edge_flags(where_ref[0], nx)
@@ -327,28 +327,15 @@
         for i in range(2):
             ref[3 + i] = v0_ref[shallow + i]
 
-    def write(low_ref, high_ref):
-        for i in range(3):
-            low_ref[i] = block_ref[i]
-            high_ref[i] = block_ref[i]
-        for x in range(8):
-            at = 2 * (x % 4)
-            low_ref[3 + x // 4, at : at + 2] = v0_ref[x, 0:2]
-            high_ref[3 + x // 4, at : at + 2] = v0_ref[x, 6:8]
-
-    by_parity(where_ref, meven_ref, modd_ref, write)
-
 
 def corner1_message(ny, meven, modd):
-    high, low = both_tiles(ny, meven, modd)
-    rows = [high[4:5, 6:8], low[4:5, 6:8], high[3:4, 0:2], low[3:4, 0:2]]
-    return jnp.concatenate([high[0:3], low[0:3], jnp.concatenate(rows, axis=1)], axis=0)
+    return jnp.concatenate(both_tiles(ny, meven, modd), axis=0)
 
 
 def down1_kernel(
     nx, ny, where_ref, block_ref, v0_ref, near_ref, far_ref, meven_ref, modd_ref,
     cnear_ref, cfar_ref,
-    v0x, v1, f1, w1, cx, cy, cz, send_ref,
+    v0x, v1, f1, w1, cx, cy, cz, send_ref, veven_ref, vodd_ref,
     k1, u1, pair, fine,
 ):
     even, outside = edge_flags(where_ref[0], nx)
@@ -358,9 +345,9 @@
 
     near = [near_ref[i] for i in range(3)]
     far = [inside(far_ref[i]) for i in range(3)]
-    cnear = [cnear_ref[i] for i in range(7)]
-    cfar = [inside(cfar_ref[i]) for i in range(7)]
-    mine = [y_tiles(where_ref, ny, meven_ref, modd_ref, i) for i in range(5)]
+    cnear = [cnear_ref[i] for i in range(6)]
+    cfar = [inside(cfar_ref[i]) for i in range(6)]
+    mine = [y_tiles(where_ref, ny, meven_ref, modd_ref, i) for i in range(3)]
 
     def pick(a, b):
         return [jnp.where(even, p, q) for p, q in zip(a, b)]
@@ -388,19 +375,21 @@
         v0x[p, 8:16] = blank
     for x in range(8):
         v0x[2 + x, 0:8] = v0_ref[x]
-        at = 2 * (x % 4)
-        v0x[2 + x, 8:10] = mine[3 + x // 4][0][at : at + 2]
-        v0x[2 + x, 14:16] = mine[3 + x // 4][1][at : at + 2]
     near_at = jnp.where(even, 10, 0)
     far_at = jnp.where(even, 0, 10)
     for i in range(2):
         v0x[near_at + i, 0:8] = near_ref[3 + i]
         v0x[far_at + i, 0:8] = inside(far_ref[3 + i])
-    low_tile = jnp.where(even, cfar[6], cnear[6])
-    high_tile = jnp.where(even, cnear[6], cfar[6])
-    for at, tile, row in ((1, low_tile, 0), (10, high_tile, 4)):
-        v0x[at, 8:10] = tile[row : row + 2]
-        v0x[at, 14:16] = tile[row + 2 : row + 4]
+
+    def write(low_ref, high_ref):
+        for q in range(10):
+            at = 2 * (q % 4)
+            low_ref[q // 4, at : at + 2] = v0x[q + 1, 0:2]
+            high_ref[q // 4, at : at + 2] = v0x[q + 1, 6:8]
+        for ref in (low_ref, high_ref):
+            ref[2, 4:8] = jnp.zeros((4, 512), F32)
+
+    by_parity(where_ref, veven_ref, vodd_ref, write)
     for p in range(12):
         u1[p] = w1[p] * f1[p]
         if p < 11:
@@ -441,7 +430,8 @@
 
 
 def up_levels(
-    nx, ny, where_ref, columns, rs, cx0, cy0, cz0, w0, v1, f1, w1, cx1, cy1, cz1, v0x, out_ref,
+    nx, ny, where_ref, columns, rs, cx0, cy0, cz0, w0, v1, f1, w1, cx1, cy1, cz1, v0x, veven_ref, vodd_ref,
+    out_ref,
     f2, k2, cx2, cyi, cyo, cz2, w2, d2, u2, v2, e2, f3, k3, cx3, cy3, cz3, w3, edge3, ga, gb,
     small, wide, e1a, e1b, narrow, e0a, e0b,
 ):
@@ -637,6 +627,12 @@
         spread = row_copy(narrow, doubled[8 * i : 8 * i + 8])
         for p in (2 * i, 2 * i + 1):
             e0a[p] = v0x[p] + spread
+    tiles = [y_tiles(where_ref, ny, veven_ref, vodd_ref, i) for i in range(3)]
+    for q in range(10):
+        at = 2 * (q % 4)
+        above, below = (tile[at : at + 2] for tile in tiles[q // 4])
+        e0a[q + 1, 8:10] = e0a[q + 1, 8:10] + above
+        e0a[q + 1, 14:16] = e0a[q + 1, 14:16] + below
     for p in range(1, 11):
         mid = e0a[p]
         total = gathered(
@@ -726,29 +722,31 @@
         [(4, 16, 128), (32, 512)],
         where, kappa, init, rhs, yeven, yodd, cost=early_cost,
     )
-    v0, rs, cx0, cy0, cz0, w0, block, mnear, mfar, meven, modd = run(
+    v0, rs, cx0, cy0, cz0, w0, block, mnear, mfar = run(
         functools.partial(down0_kernel, nx, ny),
         [(8,) + tile0]
         + [(6,) + ring0, (6,) + ring0]
         + [(8,) + ring0] * 3
         + [(3,) + tile0]
-        + [(5,) + tile0] * 4,
+        + [(5,) + tile0] * 2,
         [(6,) + ring0] * 2 + [(8,) + ring0, (10,) + ring0, (4, 16, 128), (32, 512), (32, 256)],
         where, near, far, cnear, cfar,
         ksx, vsx, rsx, cxx, cyx, czx, wix, v1x, v2x, restx, kcx,
     )
-    meven, modd = swap_y(meven, modd)
+    meven, modd = swap_y(block, block)
     mnear, mfar = swap_x(mnear, mfar)
     modd, meven, mfar, mnear = lax.optimization_barrier((modd, meven, mfar, mnear))
     corner = corner1_message(ny, meven, modd)
     cnear, cfar = swap_x(corner, corner)
-    v0x, v1, f1, w1, cx1, cy1, cz1, send = run(
+    v0x, v1, f1, w1, cx1, cy1, cz1, send, veven, vodd = run(
         functools.partial(down1_kernel, nx, ny),
-        [(12,) + ring0] + [(12,) + ring1] * 6 + [(ny, 8, 128)],
+        [(12,) + ring0] + [(12,) + ring1] * 6
+        + [(ny, 8, 128), (3,) + tile0, (3,) + tile0],
         [(12,) + ring1, (12,) + ring1, (4, 16, 128), (8, 256)],
         where, block, v0, mnear, mfar, meven, modd, cnear, cfar,
     )
     column = jnp.transpose(lax.all_to_all(send, "gy", 0, 0), (1, 0, 2))
+    column, veven, vodd = lax.optimization_barrier((column, veven, vodd))
 
     def chips_apart(j):
         return pairs(lambda x, y: (((x // 2) ^ j) * 2 + x % 2, y))
@@ -757,6 +755,8 @@
     for j in sorted(range(1, nx // 2), key=lambda j: j != 2):
         mine[j] = lax.ppermute(column, both, chips_apart(j))
     mine = [mine[j] for j in range(nx // 2)]
+    veven, vodd = swap_y(veven, vodd)
+    mine[-1], veven, vodd = lax.optimization_barrier((mine[-1], veven, vodd))
     other = [lax.ppermute(c, both, pairs(lambda x, y: (x ^ 1, y))) for c in mine]
     n2 = 2 * nx
     pair2 = (n2 + 2, 2, ny, 128)
@@ -768,7 +768,7 @@
         + [one3] * 9
         + [(48, 128), (48, 256), (12,) + ring1, (12,) + ring1, (4, 16, 128), (12,) + ring0, (12,) + ring0],
         where, *mine, *other, rsx, cxx, cyx, czx, wix, rs, cx0, cy0, cz0, w0,
-        v1, f1, w1, cx1, cy1, cz1, v0x,
+        v1, f1, w1, cx1, cy1, cz1, v0x, veven, vodd,
     )
     return out
 

time: 67.1 us -> 68 us (1.013); the launches traced: 67 us -> 66.8 us
  starting transfers between devices: 31.7 us -> 29.2 us
  blocking collectives: 17.1 us -> 18.4 us
  waiting for transfers between devices: 6.97 us -> 7.97 us
    ppermute x4, starting transfers between devices: 9.44 us -> 3.61 us  [body(): lax.ppermute(c, both, pairs(lambda x, y: (x ^ 1, y)))]
    ppermute x4, starting transfers between devices: 2.47 us -> 5.88 us  [swap_x(): lax.ppermute(near, both, pairs(lambda x, y: (x ^ 1, y)))]
    ppermute x4, waiting for transfers between devices: 4.1 us -> 1.1 us  [swap_x(): lax.ppermute(far, both, pairs(far_x))]
    ppermute x2 -> x3, waiting for transfers between devices: 1.86 us -> 4.67 us  [swap_y(): lax.ppermute(near, both, pairs(lambda x, y: (x, y ^ 1)))]
    ppermute x4, starting transfers between devices: 7.68 us -> 6.01 us  [swap_x(): lax.ppermute(far, both, pairs(far_x))]
    ppermute x2 -> x3, starting transfers between devices: 5.16 us -> 6.69 us  [swap_y(): lax.ppermute(far, both, pairs(far_y))]
    all_to_all x1, blocking collectives: 17.1 us -> 18.4 us  [body(): column = jnp.transpose(lax.all_to_all(send, 'gy', 0, 0), (1, 0, 2))]
    ppermute x4, waiting for transfers between devices: 0.01 us -> 0.95 us  [swap_x(): lax.ppermute(near, both, pairs(lambda x, y: (x ^ 1, y)))]
  transfers between devices with their start and end apart: 19 -> 21, of which waited for: 6 -> 8; matrix products, arithmetic and copies ran while one was open for 0% -> 0% of each run, Pallas kernels for 2% -> 2%
where the time goes in v4:
time: 68 us; the launch traced here: 66.8 us
  starting transfers between devices  29.2 us (43%)
  blocking collectives  18.4 us (27%)
  Pallas kernels  11 us (16%)
  waiting for transfers between devices  7.97 us (12%)
    all_to_all x1, blocking collectives, body(): column = jnp.transpose(lax.all_to_all(send, 'gy', 0, 0), (1, 0, 2))  18.4 us
    pallas_call x5, Pallas kernels, run(): pl.pallas_call(kernel, out_shape=[jax.ShapeDtypeStruct(shape, F32) for sh...  11 us
    ppermute x3, starting transfers between devices, swap_y(): lax.ppermute(far, both, pairs(far_y))  6.69 us
    ppermute x4, starting transfers between devices, swap_x(): lax.ppermute(far, both, pairs(far_x))  6.01 us
    ppermute x4, starting transfers between devices, swap_x(): lax.ppermute(near, both, pairs(lambda x, y: (x ^ 1, y)))  5.88 us
    ppermute x3, waiting for transfers between devices, swap_y(): lax.ppermute(near, both, pairs(lambda x, y: (x, y ^ 1)))  4.67 us
    ppermute x3, starting transfers between devices, body(): mine[j] = lax.ppermute(column, both, chips_apart(j))  3.79 us
    ppermute x4, starting transfers between devices, body(): lax.ppermute(c, both, pairs(lambda x, y: (x ^ 1, y)))  3.61 us
  transfers between devices with their start and end apart: 21, of which 8 were waited for; matrix products, arithmetic and copies ran while one was open for 0% of the time, Pallas kernels for 2%

profile of v4, /device:TPU:1, one launch (start us, length us, event | category | flops | bytes accessed | tf_op | source)
XLA Modules:
  0.0 66.8 jit_solution(62940175141438915)
XLA Ops:
  0.0 0.1 pad_add_fusion.where_ref
  0.1 1.7 %shard_map.46 = (f32[8,8,512]{2,1,0:T(8,128)S(1)}, f32[8,8,512]{2,1,0:T(8,128)S(1)}, f32[8,8,512]{2,1,0:T(8,128)S(1)}, f32[8,8,512]{2,1,0:T(8,128)S(1)}, f32[8,8...) custom-call(s32[2]{0:T(128)S(1)} %pad_add_fusion.where_ref, f32[3]{0:T(128)} %table_hbm.1, ...), custom_call_target="tpu_custom_call" | custom-call | tf_op jit(solution)/shard_map/pallas_call | solution.py:651
  1.8 3.3 %collective-permute-start = (f32[8,8,512]{2,1,0:T(8,128)S(1)}, f32[8,8,512]{2,1,0:T(8,128)S(1)}, u32[]{:S(2)}, u32[]{:S(2)}) collective-permute-start(f32[8,8,512]{2,1,0:T(8,128)S(1)} %get-tuple-element.56), channel_id=1, source_target_pairs={{0,32},{1,2},{2,1},{3,4},{4,3},{5,6},{6,5},{7,8},{8,7},{9,10},{10,... | collective-permute-start | bytes 393224 | tf_op jit(solution)/shard_map/ppermute | solution.py:698
  5.1 0.9 %collective-permute-start.1 = (f32[8,8,512]{2,1,0:T(8,128)S(1)}, f32[8,8,512]{2,1,0:T(8,128)S(1)}, u32[]{:S(2)}, u32[]{:S(2)}) collective-permute-start(f32[8,8,512]{2,1,0:T(8,128)S(1)} %get-tuple-element.57), channel_id=1, source_target_pairs={{0,1},{1,0},{2,3},{3,2},{4,5},{5,4},{6,7},{7,6},{8,9},{9,8},{10,11... | collective-permute-start | bytes 393224 | tf_op jit(solution)/shard_map/ppermute | solution.py:697
  6.0 2.3 %collective-permute-start.2 = (f32[8,8,512]{2,1,0:T(8,128)S(1)}, f32[8,8,512]{2,1,0:T(8,128)S(1)}, u32[]{:S(2)}, u32[]{:S(2)}) collective-permute-start(f32[8,8,512]{2,1,0:T(8,128)S(1)} %get-tuple-element.58), channel_id=1, source_target_pairs={{0,1},{1,0},{2,3},{3,2},{4,5},{5,4},{6,7},{7,6},{8,9},{9,8},{10,11... | collective-permute-start | bytes 393224 | tf_op jit(solution)/shard_map/ppermute | solution.py:692
  8.3 0.0 collective-permute-start.3
  8.3 0.0 collective-permute-done.odd_ref
  8.3 1.9 %collective-permute-done.1.even_ref = f32[8,8,512]{2,1,0:T(8,128)S(1)} collective-permute-done((f32[8,8,512]{2,1,0:T(8,128)S(1)}, f32[8,8,512]{2,1,0:T(8,128)S(1)}, u32[]{:S(2)}, u32[]{:S(2)}) %collective-permute-start.1) | collective-permute-done | bytes 131104 | tf_op jit(solution)/shard_map/ppermute | solution.py:697
  10.2 1.1 %collective-permute-done.2.far_ref = f32[8,8,512]{2,1,0:T(8,128)S(1)} collective-permute-done((f32[8,8,512]{2,1,0:T(8,128)S(1)}, f32[8,8,512]{2,1,0:T(8,128)S(1)}, u32[]{:S(2)}, u32[]{:S(2)}) %collective-permute-start.2) | collective-permute-done | bytes 131104 | tf_op jit(solution)/shard_map/ppermute | solution.py:692
  11.3 0.0 collective-permute-done.3.near_ref
  11.4 1.5 %collective-permute-start.5 = (f32[4,8,512]{2,1,0:T(8,128)S(1)}, f32[4,8,512]{2,1,0:T(8,128)S(1)}, u32[]{:S(2)}, u32[]{:S(2)}) collective-permute-start(f32[4,8,512]{2,1,0:T(8,128)S(1)} %get-tuple-element.109), channel_id=1, source_target_pairs={{0,1},{1,0},{2,3},{3,2},{4,5},{5,4},{6,7},{7,6},{8,9},{9,8},{10,11... | collective-permute-start | bytes 196616 | tf_op jit(solution)/shard_map/ppermute | solution.py:692
  12.9 0.9 %collective-permute-start.4 = (f32[4,8,512]{2,1,0:T(8,128)S(1)}, f32[4,8,512]{2,1,0:T(8,128)S(1)}, u32[]{:S(2)}, u32[]{:S(2)}) collective-permute-start(f32[4,8,512]{2,1,0:T(8,128)S(1)} %get-tuple-element.110), channel_id=1, source_target_pairs={{0,32},{1,33},{2,34},{3,35},{4,36},{5,37},{6,38},{7,39},{8,40},{9,... | collective-permute-start | bytes 196616 | tf_op jit(solution)/shard_map/ppermute | solution.py:691
  13.8 1.3 %shard_map.47 = (f32[8,16,512]{2,1,0:T(8,128)S(1)}, f32[8,16,512]{2,1,0:T(8,128)S(1)}, f32[8,16,512]{2,1,0:T(8,128)S(1)}, f32[7,16,512]{2,1,0:T(8,128)S(1)}, f32...) custom-call(s32[2]{0:T(128)S(1)} %pad_add_fusion.where_ref, ...), custom_call_target="tpu_custom_call" | custom-call | flops 20000000 | bytes 4000000 | tf_op jit(solution)/shard_map/pallas_call | solution.py:651
  15.1 0.0 collective-permute-done.5.cfar_ref
  15.1 0.0 collective-permute-done.4.cnear_ref
  15.2 1.6 %shard_map.48 = (f32[8,8,512]{2,1,0:T(8,128)S(1)}, f32[6,16,512]{2,1,0:T(8,128)S(1)}, f32[6,16,512]{2,1,0:T(8,128)S(1)}, f32[8,16,512]{2,1,0:T(8,128)S(1)}, f32[...) custom-call(s32[2]{0:T(128)S(1)} %pad_add_fusion.where_ref, ...), custom_call_target="tpu_custom_call" | custom-call | tf_op jit(solution)/shard_map/pallas_call | solution.py:651
  16.8 1.5 %collective-permute-start.8 = (f32[5,8,512]{2,1,0:T(8,128)S(1)}, f32[5,8,512]{2,1,0:T(8,128)S(1)}, u32[]{:S(2)}, u32[]{:S(2)}) collective-permute-start(f32[5,8,512]{2,1,0:T(8,128)S(1)} %get-tuple-element.80), channel_id=1, source_target_pairs={{0,1},{1,0},{2,3},{3,2},{4,5},{5,4},{6,7},{7,6},{8,9},{9,8},{10,11... | collective-permute-start | bytes 245768 | tf_op jit(solution)/shard_map/ppermute | solution.py:692
  18.3 1.5 %collective-permute-start.9 = (f32[5,8,512]{2,1,0:T(8,128)S(1)}, f32[5,8,512]{2,1,0:T(8,128)S(1)}, u32[]{:S(2)}, u32[]{:S(2)}) collective-permute-start(f32[5,8,512]{2,1,0:T(8,128)S(1)} %get-tuple-element.81), channel_id=1, source_target_pairs={{0,32},{1,33},{2,34},{3,35},{4,36},{5,37},{6,38},{7,39},{8,40},{9,... | collective-permute-start | bytes 245768 | tf_op jit(solution)/shard_map/ppermute | solution.py:691
  19.7 0.6 collective-permute-start.7
  20.3 0.3 collective-permute-start.6
  20.6 2.8 %collective-permute-done.7.meven_ref = f32[3,8,512]{2,1,0:T(8,128)S(1)} collective-permute-done((f32[3,8,512]{2,1,0:T(8,128)S(1)}, f32[3,8,512]{2,1,0:T(8,128)S(1)}, u32[]{:S(2)}, u32[]{:S(2)}) %collective-permute-start.7) | collective-permute-done | bytes 49184 | tf_op jit(solution)/shard_map/ppermute | solution.py:697
  23.4 0.0 collective-permute-done.6.modd_ref
  23.4 0.0 collective-permute-done.8.far_ref
  23.4 0.0 collective-permute-done.9.near_ref
  23.5 0.6 collective-permute-start.11
  24.1 3.5 %collective-permute-start.10 = (f32[6,8,512]{2,1,0:T(8,128)S(1)}, f32[6,8,512]{2,1,0:T(8,128)S(1)}, u32[]{:S(2)}, u32[]{:S(2)}) collective-permute-start(f32[6,8,512]{2,1,0:T(8,128)S(1)} %pad_maximum_fusion), channel_id=1, source_target_pairs={{0,32},{1,33},{2,34},{3,35},{4,36},{5,37},{6,38},{7,39},{8,40},{9,... | collective-permute-start | bytes 294920 | tf_op jit(solution)/shard_map/ppermute | solution.py:691
  27.7 0.0 collective-permute-done.11.cfar_ref
  27.7 0.9 %collective-permute-done.10.cnear_ref = f32[6,8,512]{2,1,0:T(8,128)S(1)} collective-permute-done((f32[6,8,512]{2,1,0:T(8,128)S(1)}, f32[6,8,512]{2,1,0:T(8,128)S(1)}, u32[]{:S(2)}, u32[]{:S(2)}) %collective-permute-start.10) | collective-permute-done | bytes 98336 | tf_op jit(solution)/shard_map/ppermute | solution.py:691
  28.6 1.1 %shard_map.49 = (f32[12,16,512]{2,1,0:T(8,128)S(1)}, f32[12,16,256]{2,1,0:T(8,128)S(1)}, f32[12,16,256]{2,1,0:T(8,128)S(1)}, f32[12,16,256]{2,1,0:T(8,128)S(1)},...) custom-call(s32[2]{0:T(128)S(1)} %pad_add_fusion.where_ref, ...), custom_call_target="tpu_custom_call" | custom-call | tf_op jit(solution)/shard_map/pallas_call | solution.py:651
  29.8 18.4 %all_to_all.5 = f32[32,8,128]{2,1,0:T(8,128)S(1)} all-to-all(f32[32,8,128]{2,1,0:T(8,128)S(1)} %get-tuple-element.86), channel_id=1, replica_groups=mesh['gx'=8,'gy'=32] {'gy'}, dimensions={0} | all-to-all | bytes 262144 | tf_op jit(solution)/shard_map/all_to_all | solution.py:748
  48.1 0.7 %collective-permute-start.14 = (f32[8,32,128]{2,1,0:T(8,128)S(1)}, f32[8,32,128]{2,1,0:T(8,128)S(1)}, u32[]{:S(2)}, u32[]{:S(2)}) collective-permute-start(f32[8,32,128]{2,1,0:T(8,128)S(1)} %bitcast.5), channel_id=1, source_target_pairs={{0,192},{1,193},{2,194},{3,195},{4,196},{5,197},{6,198},{7,199},{8... | collective-permute-start | bytes 393224 | tf_op jit(solution)/shard_map/ppermute | solution.py:756
  48.9 3.1 %collective-permute-start.13 = (f32[8,32,128]{2,1,0:T(8,128)S(1)}, f32[8,32,128]{2,1,0:T(8,128)S(1)}, u32[]{:S(2)}, u32[]{:S(2)}) collective-permute-start(f32[8,32,128]{2,1,0:T(8,128)S(1)} %bitcast.6), channel_id=1, source_target_pairs={{0,128},{1,129},{2,130},{3,131},{4,132},{5,133},{6,134},{7,135},{8... | collective-permute-start | bytes 393224 | tf_op jit(solution)/shard_map/ppermute | solution.py:756
  51.9 0.0 collective-permute-start.12
  51.9 1.7 %collective-permute-start.15 = (f32[3,8,512]{2,1,0:T(8,128)S(1)}, f32[3,8,512]{2,1,0:T(8,128)S(1)}, u32[]{:S(2)}, u32[]{:S(2)}) collective-permute-start(f32[3,8,512]{2,1,0:T(8,128)S(1)} %get-tuple-element.90), channel_id=1, source_target_pairs={{0,1},{1,0},{2,3},{3,2},{4,5},{5,4},{6,7},{7,6},{8,9},{9,8},{10,11... | collective-permute-start | bytes 147464 | tf_op jit(solution)/shard_map/ppermute | solution.py:697
  53.6 3.1 %collective-permute-start.16 = (f32[3,8,512]{2,1,0:T(8,128)S(1)}, f32[3,8,512]{2,1,0:T(8,128)S(1)}, u32[]{:S(2)}, u32[]{:S(2)}) collective-permute-start(f32[3,8,512]{2,1,0:T(8,128)S(1)} %get-tuple-element.91), channel_id=1, source_target_pairs={{0,32},{1,2},{2,1},{3,4},{4,3},{5,6},{6,5},{7,8},{8,7},{9,10},{10,... | collective-permute-start | bytes 147464 | tf_op jit(solution)/shard_map/ppermute | solution.py:698
  56.7 0.0 collective-permute-done.15.refs_25_
  56.7 3.0 %collective-permute-start.17 = (f32[8,32,128]{2,1,0:T(8,128)S(1)}, f32[8,32,128]{2,1,0:T(8,128)S(1)}, u32[]{:S(2)}, u32[]{:S(2)}) collective-permute-start(f32[8,32,128]{2,1,0:T(8,128)S(1)} %bitcast.8), channel_id=1, source_target_pairs={{0,32},{1,33},{2,34},{3,35},{4,36},{5,37},{6,38},{7,39},{8,40},{9,... | collective-permute-start | bytes 393224 | tf_op jit(solution)/shard_map/ppermute | solution.py:760
  59.7 0.0 collective-permute-done.16.refs_26_
  59.7 0.0 collective-permute-done.14.refs_3_
  59.7 0.1 collective-permute-start.20
  59.8 0.0 collective-permute-done.13.refs_2_
  59.8 0.4 collective-permute-start.19
  60.2 0.0 collective-permute-done.12.refs_1_
  60.2 0.1 collective-permute-start.18
  60.3 0.4 collective-permute-done.17.refs_4_
  60.7 0.4 collective-permute-done.20.refs_7_
  61.1 0.2 collective-permute-done.19.refs_6_
  61.3 0.3 collective-permute-done.18.refs_5_
  61.6 5.2 %shard_map.50 = f32[8,8,512]{2,1,0:T(8,128)} custom-call(s32[2]{0:T(128)S(1)} %pad_add_fusion.where_ref, f32[8,32,128]{2,1,0:T(8,128)S(1)} %bitcast.9, f32[8,32,128]{2,1,0:T(8,128)S(1)} %collective-permute-done.12.refs_1_, f32[8,32,128]{2,1,0:T(8,128)S(1)} %collective-permute-done.13.refs_2_, f32[8,32,128]{2,1,0:T(8,128)S(1)} %collective-permute-done.14.refs_3_, ...), custom_call_target="tpu_custom_call" | custom-call | tf_op jit(solution)/shard_map/pallas_call | solution.py:651
  (8 shorter events, 0.1 us)
Async XLA Ops:
  1.8 6.5 %collective-permute-start = (f32[8,8,512]{2,1,0:T(8,128)S(1)}, f32[8,8,512]{2,1,0:T(8,128)S(1)}, u32[]{:S(2)}, u32[]{:S(2)}) collective-permute-start(f32[8,8,512]{2,1,0:T(8,128)S(1)} %get-tuple-element.56), channel_id=1, source_target_pairs={{0,32},{1,2},{2,1},{3,4},{4,3},{5,6},{6,5},{7,8},{8,7},{9,10},{10,... | collective-permute-start | bytes 393224 | tf_op jit(solution)/shard_map/ppermute | solution.py:698
  5.1 5.1 %collective-permute-start.1 = (f32[8,8,512]{2,1,0:T(8,128)S(1)}, f32[8,8,512]{2,1,0:T(8,128)S(1)}, u32[]{:S(2)}, u32[]{:S(2)}) collective-permute-start(f32[8,8,512]{2,1,0:T(8,128)S(1)} %get-tuple-element.57), channel_id=1, source_target_pairs={{0,1},{1,0},{2,3},{3,2},{4,5},{5,4},{6,7},{7,6},{8,9},{9,8},{10,11... | collective-permute-start | bytes 393224 | tf_op jit(solution)/shard_map/ppermute | solution.py:697
  6.0 5.3 %collective-permute-start.2 = (f32[8,8,512]{2,1,0:T(8,128)S(1)}, f32[8,8,512]{2,1,0:T(8,128)S(1)}, u32[]{:S(2)}, u32[]{:S(2)}) collective-permute-start(f32[8,8,512]{2,1,0:T(8,128)S(1)} %get-tuple-element.58), channel_id=1, source_target_pairs={{0,1},{1,0},{2,3},{3,2},{4,5},{5,4},{6,7},{7,6},{8,9},{9,8},{10,11... | collective-permute-start | bytes 393224 | tf_op jit(solution)/shard_map/ppermute | solution.py:692
  8.3 2.9 %collective-permute-start.3 = (f32[8,8,512]{2,1,0:T(8,128)S(1)}, f32[8,8,512]{2,1,0:T(8,128)S(1)}, u32[]{:S(2)}, u32[]{:S(2)}) collective-permute-start(f32[8,8,512]{2,1,0:T(8,128)S(1)} %get-tuple-element.59), channel_id=1, source_target_pairs={{0,32},{1,33},{2,34},{3,35},{4,36},{5,37},{6,38},{7,39},{8,40},{9,... | collective-permute-start | bytes 393224 | tf_op jit(solution)/shard_map/ppermute | solution.py:691
  11.4 3.8 %collective-permute-start.5 = (f32[4,8,512]{2,1,0:T(8,128)S(1)}, f32[4,8,512]{2,1,0:T(8,128)S(1)}, u32[]{:S(2)}, u32[]{:S(2)}) collective-permute-start(f32[4,8,512]{2,1,0:T(8,128)S(1)} %get-tuple-element.109), channel_id=1, source_target_pairs={{0,1},{1,0},{2,3},{3,2},{4,5},{5,4},{6,7},{7,6},{8,9},{9,8},{10,11... | collective-permute-start | bytes 196616 | tf_op jit(solution)/shard_map/ppermute | solution.py:692
  12.9 2.2 %collective-permute-start.4 = (f32[4,8,512]{2,1,0:T(8,128)S(1)}, f32[4,8,512]{2,1,0:T(8,128)S(1)}, u32[]{:S(2)}, u32[]{:S(2)}) collective-permute-start(f32[4,8,512]{2,1,0:T(8,128)S(1)} %get-tuple-element.110), channel_id=1, source_target_pairs={{0,32},{1,33},{2,34},{3,35},{4,36},{5,37},{6,38},{7,39},{8,40},{9,... | collective-permute-start | bytes 196616 | tf_op jit(solution)/shard_map/ppermute | solution.py:691
  16.8 6.7 %collective-permute-start.8 = (f32[5,8,512]{2,1,0:T(8,128)S(1)}, f32[5,8,512]{2,1,0:T(8,128)S(1)}, u32[]{:S(2)}, u32[]{:S(2)}) collective-permute-start(f32[5,8,512]{2,1,0:T(8,128)S(1)} %get-tuple-element.80), channel_id=1, source_target_pairs={{0,1},{1,0},{2,3},{3,2},{4,5},{5,4},{6,7},{7,6},{8,9},{9,8},{10,11... | collective-permute-start | bytes 245768 | tf_op jit(solution)/shard_map/ppermute | solution.py:692
  18.3 5.2 %collective-permute-start.9 = (f32[5,8,512]{2,1,0:T(8,128)S(1)}, f32[5,8,512]{2,1,0:T(8,128)S(1)}, u32[]{:S(2)}, u32[]{:S(2)}) collective-permute-start(f32[5,8,512]{2,1,0:T(8,128)S(1)} %get-tuple-element.81), channel_id=1, source_target_pairs={{0,32},{1,33},{2,34},{3,35},{4,36},{5,37},{6,38},{7,39},{8,40},{9,... | collective-permute-start | bytes 245768 | tf_op jit(solution)/shard_map/ppermute | solution.py:691
  19.7 3.7 %collective-permute-start.7 = (f32[3,8,512]{2,1,0:T(8,128)S(1)}, f32[3,8,512]{2,1,0:T(8,128)S(1)}, u32[]{:S(2)}, u32[]{:S(2)}) collective-permute-start(f32[3,8,512]{2,1,0:T(8,128)S(1)} %get-tuple-element.78.block_ref), channel_id=1, source_target_pairs={{0,1},{1,0},{2,3},{3,2},{4,5},{5,4},{6,7},{7,6},{8,9},{9,8},{10,11... | collective-permute-start | bytes 147464 | tf_op jit(solution)/shard_map/ppermute | solution.py:697
  20.3 3.1 %collective-permute-start.6 = (f32[3,8,512]{2,1,0:T(8,128)S(1)}, f32[3,8,512]{2,1,0:T(8,128)S(1)}, u32[]{:S(2)}, u32[]{:S(2)}) collective-permute-start(f32[3,8,512]{2,1,0:T(8,128)S(1)} %get-tuple-element.78.block_ref), channel_id=1, source_target_pairs={{0,32},{1,2},{2,1},{3,4},{4,3},{5,6},{6,5},{7,8},{8,7},{9,10},{10,... | collective-permute-start | bytes 147464 | tf_op jit(solution)/shard_map/ppermute | solution.py:698
  23.5 4.2 %collective-permute-start.11 = (f32[6,8,512]{2,1,0:T(8,128)S(1)}, f32[6,8,512]{2,1,0:T(8,128)S(1)}, u32[]{:S(2)}, u32[]{:S(2)}) collective-permute-start(f32[6,8,512]{2,1,0:T(8,128)S(1)} %pad_maximum_fusion), channel_id=1, source_target_pairs={{0,1},{1,0},{2,3},{3,2},{4,5},{5,4},{6,7},{7,6},{8,9},{9,8},{10,11... | collective-permute-start | bytes 294920 | tf_op jit(solution)/shard_map/ppermute | solution.py:692
  24.1 4.5 %collective-permute-start.10 = (f32[6,8,512]{2,1,0:T(8,128)S(1)}, f32[6,8,512]{2,1,0:T(8,128)S(1)}, u32[]{:S(2)}, u32[]{:S(2)}) collective-permute-start(f32[6,8,512]{2,1,0:T(8,128)S(1)} %pad_maximum_fusion), channel_id=1, source_target_pairs={{0,32},{1,33},{2,34},{3,35},{4,36},{5,37},{6,38},{7,39},{8,40},{9,... | collective-permute-start | bytes 294920 | tf_op jit(solution)/shard_map/ppermute | solution.py:691
  48.1 11.6 %collective-permute-start.14 = (f32[8,32,128]{2,1,0:T(8,128)S(1)}, f32[8,32,128]{2,1,0:T(8,128)S(1)}, u32[]{:S(2)}, u32[]{:S(2)}) collective-permute-start(f32[8,32,128]{2,1,0:T(8,128)S(1)} %bitcast.5), channel_id=1, source_target_pairs={{0,192},{1,193},{2,194},{3,195},{4,196},{5,197},{6,198},{7,199},{8... | collective-permute-start | bytes 393224 | tf_op jit(solution)/shard_map/ppermute | solution.py:756
  48.9 10.9 %collective-permute-start.13 = (f32[8,32,128]{2,1,0:T(8,128)S(1)}, f32[8,32,128]{2,1,0:T(8,128)S(1)}, u32[]{:S(2)}, u32[]{:S(2)}) collective-permute-start(f32[8,32,128]{2,1,0:T(8,128)S(1)} %bitcast.6), channel_id=1, source_target_pairs={{0,128},{1,129},{2,130},{3,131},{4,132},{5,133},{6,134},{7,135},{8... | collective-permute-start | bytes 393224 | tf_op jit(solution)/shard_map/ppermute | solution.py:756
  51.9 8.3 %collective-permute-start.12 = (f32[8,32,128]{2,1,0:T(8,128)S(1)}, f32[8,32,128]{2,1,0:T(8,128)S(1)}, u32[]{:S(2)}, u32[]{:S(2)}) collective-permute-start(f32[8,32,128]{2,1,0:T(8,128)S(1)} %bitcast.7), channel_id=1, source_target_pairs={{0,64},{1,65},{2,66},{3,67},{4,68},{5,69},{6,70},{7,71},{8,72},{9,... | collective-permute-start | bytes 393224 | tf_op jit(solution)/shard_map/ppermute | solution.py:756
  51.9 4.8 %collective-permute-start.15 = (f32[3,8,512]{2,1,0:T(8,128)S(1)}, f32[3,8,512]{2,1,0:T(8,128)S(1)}, u32[]{:S(2)}, u32[]{:S(2)}) collective-permute-start(f32[3,8,512]{2,1,0:T(8,128)S(1)} %get-tuple-element.90), channel_id=1, source_target_pairs={{0,1},{1,0},{2,3},{3,2},{4,5},{5,4},{6,7},{7,6},{8,9},{9,8},{10,11... | collective-permute-start | bytes 147464 | tf_op jit(solution)/shard_map/ppermute | solution.py:697
  53.6 6.1 %collective-permute-start.16 = (f32[3,8,512]{2,1,0:T(8,128)S(1)}, f32[3,8,512]{2,1,0:T(8,128)S(1)}, u32[]{:S(2)}, u32[]{:S(2)}) collective-permute-start(f32[3,8,512]{2,1,0:T(8,128)S(1)} %get-tuple-element.91), channel_id=1, source_target_pairs={{0,32},{1,2},{2,1},{3,4},{4,3},{5,6},{6,5},{7,8},{8,7},{9,10},{10,... | collective-permute-start | bytes 147464 | tf_op jit(solution)/shard_map/ppermute | solution.py:698
  56.7 4.0 %collective-permute-start.17 = (f32[8,32,128]{2,1,0:T(8,128)S(1)}, f32[8,32,128]{2,1,0:T(8,128)S(1)}, u32[]{:S(2)}, u32[]{:S(2)}) collective-permute-start(f32[8,32,128]{2,1,0:T(8,128)S(1)} %bitcast.8), channel_id=1, source_target_pairs={{0,32},{1,33},{2,34},{3,35},{4,36},{5,37},{6,38},{7,39},{8,40},{9,... | collective-permute-start | bytes 393224 | tf_op jit(solution)/shard_map/ppermute | solution.py:760
  59.7 1.4 %collective-permute-start.20 = (f32[8,32,128]{2,1,0:T(8,128)S(1)}, f32[8,32,128]{2,1,0:T(8,128)S(1)}, u32[]{:S(2)}, u32[]{:S(2)}) collective-permute-start(f32[8,32,128]{2,1,0:T(8,128)S(1)} %collective-permute-done.14.refs_3_), channel_id=1, source_target_pairs={{0,32},{1,33},{2,34},{3,35},{4,36},{5,37},{6,38},{7,39},{8,40},{9,... | collective-permute-start | bytes 393224 | tf_op jit(solution)/shard_map/ppermute | solution.py:760
  59.8 1.4 %collective-permute-start.19 = (f32[8,32,128]{2,1,0:T(8,128)S(1)}, f32[8,32,128]{2,1,0:T(8,128)S(1)}, u32[]{:S(2)}, u32[]{:S(2)}) collective-permute-start(f32[8,32,128]{2,1,0:T(8,128)S(1)} %collective-permute-done.13.refs_2_), channel_id=1, source_target_pairs={{0,32},{1,33},{2,34},{3,35},{4,36},{5,37},{6,38},{7,39},{8,40},{9,... | collective-permute-start | bytes 393224 | tf_op jit(solution)/shard_map/ppermute | solution.py:760
  60.2 1.3 %collective-permute-start.18 = (f32[8,32,128]{2,1,0:T(8,128)S(1)}, f32[8,32,128]{2,1,0:T(8,128)S(1)}, u32[]{:S(2)}, u32[]{:S(2)}) collective-permute-start(f32[8,32,128]{2,1,0:T(8,128)S(1)} %collective-permute-done.12.refs_1_), channel_id=1, source_target_pairs={{0,32},{1,33},{2,34},{3,35},{4,36},{5,37},{6,38},{7,39},{8,40},{9,... | collective-permute-start | bytes 393224 | tf_op jit(solution)/shard_map/ppermute | solution.py:760

commit v5 on v3

--- a/solution.py
+++ b/solution.py
@@ -717,7 +717,7 @@
     )
     yeven, yodd = swap_y(yeven, yodd)
     near, far = swap_x(near, far)
-    yodd, far, yeven, near = lax.optimization_barrier((yodd, far, yeven, near))
+    yeven, yodd, far, near = lax.optimization_barrier((yeven, yodd, far, near))
     cnear, cfar = swap_x(*corner_messages(nx, ny, yeven, yodd))
     ksx, vsx, rsx, cxx, cyx, czx, wix, v1x, v2x, restx, kcx = run(
         functools.partial(early0_kernel, ny),
@@ -739,7 +739,7 @@
     )
     meven, modd = swap_y(meven, modd)
     mnear, mfar = swap_x(mnear, mfar)
-    modd, mfar, meven, mnear = lax.optimization_barrier((modd, mfar, meven, mnear))
+    meven, modd, mfar, mnear = lax.optimization_barrier((meven, modd, mfar, mnear))
     corner = corner1_message(ny, meven, modd)
     cnear, cfar = swap_x(corner, corner)
     v0x, v1, f1, w1, cx1, cy1, cz1, send = run(

time: 68.5 us -> 66.2 us (0.966)
  waiting for transfers between devices: 6.84 us -> 3.87 us
  starting transfers between devices: 32.6 us -> 34.4 us
  blocking collectives: 17.7 us -> 16.6 us
    ppermute x4, starting transfers between devices: 5.85 us -> 13.7 us  [swap_x(): lax.ppermute(near, both, pairs(lambda x, y: (x ^ 1, y)))]
    ppermute x2, starting transfers between devices: 6.52 us -> 3.75 us  [swap_y(): lax.ppermute(near, both, pairs(lambda x, y: (x, y ^ 1)))]
    ppermute x2, waiting for transfers between devices: 2.56 us -> 0.01 us  [swap_y(): lax.ppermute(near, both, pairs(lambda x, y: (x, y ^ 1)))]
    ppermute x2, starting transfers between devices: 4.3 us -> 2.74 us  [swap_y(): lax.ppermute(far, both, pairs(far_y))]
    ppermute x4, starting transfers between devices: 3.15 us -> 1.96 us  [swap_x(): lax.ppermute(far, both, pairs(far_x))]
    all_to_all x1, blocking collectives: 17.7 us -> 16.6 us  [body(): column = jnp.transpose(lax.all_to_all(send, 'gy', 0, 0), (1, 0, 2))]
    ppermute x4, waiting for transfers between devices: 1.95 us -> 1.25 us  [swap_x(): lax.ppermute(far, both, pairs(far_x))]
  transfers between devices with their start and end apart: 19 -> 19, of which waited for: 9 -> 8; matrix products, arithmetic and copies ran while one was open for 0% -> 0% of each run, Pallas kernels for 2% -> 2%
where the time goes in v5:
time: 66.2 us; the launch traced here: 66.1 us
  starting transfers between devices  34.4 us (52%)
  blocking collectives  16.6 us (25%)
  Pallas kernels  10.9 us (16%)
  waiting for transfers between devices  3.87 us (6%)
    all_to_all x1, blocking collectives, body(): column = jnp.transpose(lax.all_to_all(send, 'gy', 0, 0), (1, 0, 2))  16.6 us
    ppermute x4, starting transfers between devices, swap_x(): lax.ppermute(near, both, pairs(lambda x, y: (x ^ 1, y)))  13.7 us
    pallas_call x5, Pallas kernels, run(): pl.pallas_call(kernel, out_shape=[jax.ShapeDtypeStruct(shape, F32) for sh...  10.9 us
    ppermute x4, starting transfers between devices, body(): lax.ppermute(c, both, pairs(lambda x, y: (x ^ 1, y)))  8.87 us
    ppermute x2, starting transfers between devices, swap_y(): lax.ppermute(near, both, pairs(lambda x, y: (x, y ^ 1)))  3.75 us
    ppermute x3, starting transfers between devices, body(): mine[j] = lax.ppermute(column, both, chips_apart(j))  3.33 us
    ppermute x2, starting transfers between devices, swap_y(): lax.ppermute(far, both, pairs(far_y))  2.74 us
    ppermute x4, starting transfers between devices, swap_x(): lax.ppermute(far, both, pairs(far_x))  1.96 us
  transfers between devices with their start and end apart: 19, of which 8 were waited for; matrix products, arithmetic and copies ran while one was open for 0% of the time, Pallas kernels for 2%

profile of v5, /device:TPU:1, one launch (start us, length us, event | category | flops | bytes accessed | tf_op | source)
XLA Modules:
  0.0 66.1 jit_solution(14290879154707667233)
XLA Ops:
  0.0 0.1 pad_add_fusion.where_ref
  0.1 1.7 %shard_map.46 = (f32[8,8,512]{2,1,0:T(8,128)S(1)}, f32[8,8,512]{2,1,0:T(8,128)S(1)}, f32[8,8,512]{2,1,0:T(8,128)S(1)}, f32[8,8,512]{2,1,0:T(8,128)S(1)}, f32[8,8...) custom-call(s32[2]{0:T(128)S(1)} %pad_add_fusion.where_ref, f32[3]{0:T(128)} %table_hbm.1, ...), custom_call_target="tpu_custom_call" | custom-call | tf_op jit(solution)/shard_map/pallas_call | solution.py:655
  1.8 2.6 %collective-permute-start = (f32[8,8,512]{2,1,0:T(8,128)S(1)}, f32[8,8,512]{2,1,0:T(8,128)S(1)}, u32[]{:S(2)}, u32[]{:S(2)}) collective-permute-start(f32[8,8,512]{2,1,0:T(8,128)S(1)} %get-tuple-element.50), channel_id=1, source_target_pairs={{0,1},{1,0},{2,3},{3,2},{4,5},{5,4},{6,7},{7,6},{8,9},{9,8},{10,11... | collective-permute-start | bytes 393224 | tf_op jit(solution)/shard_map/ppermute | solution.py:701
  4.4 1.0 %collective-permute-start.1 = (f32[8,8,512]{2,1,0:T(8,128)S(1)}, f32[8,8,512]{2,1,0:T(8,128)S(1)}, u32[]{:S(2)}, u32[]{:S(2)}) collective-permute-start(f32[8,8,512]{2,1,0:T(8,128)S(1)} %get-tuple-element.51), channel_id=1, source_target_pairs={{0,32},{1,2},{2,1},{3,4},{4,3},{5,6},{6,5},{7,8},{8,7},{9,10},{10,... | collective-permute-start | bytes 393224 | tf_op jit(solution)/shard_map/ppermute | solution.py:702
  5.3 1.1 %collective-permute-start.2 = (f32[8,8,512]{2,1,0:T(8,128)S(1)}, f32[8,8,512]{2,1,0:T(8,128)S(1)}, u32[]{:S(2)}, u32[]{:S(2)}) collective-permute-start(f32[8,8,512]{2,1,0:T(8,128)S(1)} %get-tuple-element.52), channel_id=1, source_target_pairs={{0,1},{1,0},{2,3},{3,2},{4,5},{5,4},{6,7},{7,6},{8,9},{9,8},{10,11... | collective-permute-start | bytes 393224 | tf_op jit(solution)/shard_map/ppermute | solution.py:696
  6.4 2.7 %collective-permute-start.3 = (f32[8,8,512]{2,1,0:T(8,128)S(1)}, f32[8,8,512]{2,1,0:T(8,128)S(1)}, u32[]{:S(2)}, u32[]{:S(2)}) collective-permute-start(f32[8,8,512]{2,1,0:T(8,128)S(1)} %get-tuple-element.53), channel_id=1, source_target_pairs={{0,32},{1,33},{2,34},{3,35},{4,36},{5,37},{6,38},{7,39},{8,40},{9,... | collective-permute-start | bytes 393224 | tf_op jit(solution)/shard_map/ppermute | solution.py:695
  9.1 0.0 collective-permute-done.even_ref
  9.2 0.0 collective-permute-done.1.odd_ref
  9.2 0.6 collective-permute-done.2.far_ref
  9.7 0.4 collective-permute-done.3.near_ref
  10.2 0.8 %collective-permute-start.5 = (f32[4,8,512]{2,1,0:T(8,128)S(1)}, f32[4,8,512]{2,1,0:T(8,128)S(1)}, u32[]{:S(2)}, u32[]{:S(2)}) collective-permute-start(f32[4,8,512]{2,1,0:T(8,128)S(1)} %get-tuple-element.99), channel_id=1, source_target_pairs={{0,1},{1,0},{2,3},{3,2},{4,5},{5,4},{6,7},{7,6},{8,9},{9,8},{10,11... | collective-permute-start | bytes 196616 | tf_op jit(solution)/shard_map/ppermute | solution.py:696
  11.0 3.3 %collective-permute-start.4 = (f32[4,8,512]{2,1,0:T(8,128)S(1)}, f32[4,8,512]{2,1,0:T(8,128)S(1)}, u32[]{:S(2)}, u32[]{:S(2)}) collective-permute-start(f32[4,8,512]{2,1,0:T(8,128)S(1)} %get-tuple-element.100), channel_id=1, source_target_pairs={{0,32},{1,33},{2,34},{3,35},{4,36},{5,37},{6,38},{7,39},{8,40},{9,... | collective-permute-start | bytes 196616 | tf_op jit(solution)/shard_map/ppermute | solution.py:695
  14.3 1.3 %shard_map.47 = (f32[8,16,512]{2,1,0:T(8,128)S(1)}, f32[8,16,512]{2,1,0:T(8,128)S(1)}, f32[8,16,512]{2,1,0:T(8,128)S(1)}, f32[7,16,512]{2,1,0:T(8,128)S(1)}, f32...) custom-call(s32[2]{0:T(128)S(1)} %pad_add_fusion.where_ref, ...), custom_call_target="tpu_custom_call" | custom-call | flops 20000000 | bytes 4000000 | tf_op jit(solution)/shard_map/pallas_call | solution.py:655
  15.6 0.0 collective-permute-done.5.cfar_ref
  15.7 0.0 collective-permute-done.4.cnear_ref
  15.7 1.6 %shard_map.48 = (f32[8,8,512]{2,1,0:T(8,128)S(1)}, f32[6,16,512]{2,1,0:T(8,128)S(1)}, f32[6,16,512]{2,1,0:T(8,128)S(1)}, f32[8,16,512]{2,1,0:T(8,128)S(1)}, f32[...) custom-call(s32[2]{0:T(128)S(1)} %pad_add_fusion.where_ref, ...), custom_call_target="tpu_custom_call" | custom-call | tf_op jit(solution)/shard_map/pallas_call | solution.py:655
  17.3 1.2 %collective-permute-start.6 = (f32[5,8,512]{2,1,0:T(8,128)S(1)}, f32[5,8,512]{2,1,0:T(8,128)S(1)}, u32[]{:S(2)}, u32[]{:S(2)}) collective-permute-start(f32[5,8,512]{2,1,0:T(8,128)S(1)} %get-tuple-element.74), channel_id=1, source_target_pairs={{0,1},{1,0},{2,3},{3,2},{4,5},{5,4},{6,7},{7,6},{8,9},{9,8},{10,11... | collective-permute-start | bytes 245768 | tf_op jit(solution)/shard_map/ppermute | solution.py:701
  18.5 1.8 %collective-permute-start.7 = (f32[5,8,512]{2,1,0:T(8,128)S(1)}, f32[5,8,512]{2,1,0:T(8,128)S(1)}, u32[]{:S(2)}, u32[]{:S(2)}) collective-permute-start(f32[5,8,512]{2,1,0:T(8,128)S(1)} %get-tuple-element.75), channel_id=1, source_target_pairs={{0,32},{1,2},{2,1},{3,4},{4,3},{5,6},{6,5},{7,8},{8,7},{9,10},{10,... | collective-permute-start | bytes 245768 | tf_op jit(solution)/shard_map/ppermute | solution.py:702
  20.3 0.0 collective-permute-start.8
  20.3 4.1 %collective-permute-start.9 = (f32[5,8,512]{2,1,0:T(8,128)S(1)}, f32[5,8,512]{2,1,0:T(8,128)S(1)}, u32[]{:S(2)}, u32[]{:S(2)}) collective-permute-start(f32[5,8,512]{2,1,0:T(8,128)S(1)} %get-tuple-element.77), channel_id=1, source_target_pairs={{0,32},{1,33},{2,34},{3,35},{4,36},{5,37},{6,38},{7,39},{8,40},{9,... | collective-permute-start | bytes 245768 | tf_op jit(solution)/shard_map/ppermute | solution.py:695
  24.4 0.0 collective-permute-done.6.meven_ref
  24.4 0.0 collective-permute-done.7.modd_ref
  24.4 0.0 collective-permute-done.8.far_ref
  24.5 0.9 %collective-permute-done.9.near_ref = f32[5,8,512]{2,1,0:T(8,128)S(1)} collective-permute-done((f32[5,8,512]{2,1,0:T(8,128)S(1)}, f32[5,8,512]{2,1,0:T(8,128)S(1)}, u32[]{:S(2)}, u32[]{:S(2)}) %collective-permute-start.9) | collective-permute-done | bytes 81952 | tf_op jit(solution)/shard_map/ppermute | solution.py:695
  25.5 0.1 collective-permute-start.11
  25.6 3.5 %collective-permute-start.10 = (f32[7,8,512]{2,1,0:T(8,128)S(1)}, f32[7,8,512]{2,1,0:T(8,128)S(1)}, u32[]{:S(2)}, u32[]{:S(2)}) collective-permute-start(f32[7,8,512]{2,1,0:T(8,128)S(1)} %maximum_maximum_fusion), channel_id=1, source_target_pairs={{0,32},{1,33},{2,34},{3,35},{4,36},{5,37},{6,38},{7,39},{8,40},{9,... | collective-permute-start | bytes 344072 | tf_op jit(solution)/shard_map/ppermute | solution.py:695
  29.1 0.7 %collective-permute-done.11.cfar_ref = f32[7,8,512]{2,1,0:T(8,128)S(1)} collective-permute-done((f32[7,8,512]{2,1,0:T(8,128)S(1)}, f32[7,8,512]{2,1,0:T(8,128)S(1)}, u32[]{:S(2)}, u32[]{:S(2)}) %collective-permute-start.11) | collective-permute-done | bytes 114720 | tf_op jit(solution)/shard_map/ppermute | solution.py:696
  29.8 0.3 collective-permute-done.10.cnear_ref
  30.0 1.1 %shard_map.49 = (f32[12,16,512]{2,1,0:T(8,128)S(1)}, f32[12,16,256]{2,1,0:T(8,128)S(1)}, f32[12,16,256]{2,1,0:T(8,128)S(1)}, f32[12,16,256]{2,1,0:T(8,128)S(1)},...) custom-call(s32[2]{0:T(128)S(1)} %pad_add_fusion.where_ref, ...), custom_call_target="tpu_custom_call" | custom-call | tf_op jit(solution)/shard_map/pallas_call | solution.py:655
  31.2 16.6 %all_to_all.5 = f32[32,8,128]{2,1,0:T(8,128)S(1)} all-to-all(f32[32,8,128]{2,1,0:T(8,128)S(1)} %get-tuple-element.82), channel_id=1, replica_groups=mesh['gx'=8,'gy'=32] {'gy'}, dimensions={0} | all-to-all | bytes 262144 | tf_op jit(solution)/shard_map/all_to_all | solution.py:751
  47.8 0.1 collective-permute-start.14
  47.9 3.0 %collective-permute-start.13 = (f32[8,32,128]{2,1,0:T(8,128)S(1)}, f32[8,32,128]{2,1,0:T(8,128)S(1)}, u32[]{:S(2)}, u32[]{:S(2)}) collective-permute-start(f32[8,32,128]{2,1,0:T(8,128)S(1)} %bitcast.6), channel_id=1, source_target_pairs={{0,128},{1,129},{2,130},{3,131},{4,132},{5,133},{6,134},{7,135},{8... | collective-permute-start | bytes 393224 | tf_op jit(solution)/shard_map/ppermute | solution.py:758
  51.0 0.2 collective-permute-start.12
  51.2 4.5 %collective-permute-start.15 = (f32[8,32,128]{2,1,0:T(8,128)S(1)}, f32[8,32,128]{2,1,0:T(8,128)S(1)}, u32[]{:S(2)}, u32[]{:S(2)}) collective-permute-start(f32[8,32,128]{2,1,0:T(8,128)S(1)} %bitcast.8), channel_id=1, source_target_pairs={{0,32},{1,33},{2,34},{3,35},{4,36},{5,37},{6,38},{7,39},{8,40},{9,... | collective-permute-start | bytes 393224 | tf_op jit(solution)/shard_map/ppermute | solution.py:760
  55.7 0.0 collective-permute-done.14.refs_3_
  55.7 3.5 %collective-permute-start.18 = (f32[8,32,128]{2,1,0:T(8,128)S(1)}, f32[8,32,128]{2,1,0:T(8,128)S(1)}, u32[]{:S(2)}, u32[]{:S(2)}) collective-permute-start(f32[8,32,128]{2,1,0:T(8,128)S(1)} %collective-permute-done.14.refs_3_), channel_id=1, source_target_pairs={{0,32},{1,33},{2,34},{3,35},{4,36},{5,37},{6,38},{7,39},{8,40},{9,... | collective-permute-start | bytes 393224 | tf_op jit(solution)/shard_map/ppermute | solution.py:760
  59.2 0.0 collective-permute-done.13.refs_2_
  59.2 0.0 collective-permute-start.17
  59.2 0.0 collective-permute-done.12.refs_1_
  59.2 0.8 %collective-permute-start.16 = (f32[8,32,128]{2,1,0:T(8,128)S(1)}, f32[8,32,128]{2,1,0:T(8,128)S(1)}, u32[]{:S(2)}, u32[]{:S(2)}) collective-permute-start(f32[8,32,128]{2,1,0:T(8,128)S(1)} %collective-permute-done.12.refs_1_), channel_id=1, source_target_pairs={{0,32},{1,33},{2,34},{3,35},{4,36},{5,37},{6,38},{7,39},{8,40},{9,... | collective-permute-start | bytes 393224 | tf_op jit(solution)/shard_map/ppermute | solution.py:760
  60.0 0.0 collective-permute-done.15.refs_4_
  60.0 0.1 collective-permute-done.18.refs_7_
  60.2 0.4 collective-permute-done.17.refs_6_
  60.5 0.5 collective-permute-done.16.refs_5_
  61.0 5.1 %shard_map.50 = f32[8,8,512]{2,1,0:T(8,128)} custom-call(s32[2]{0:T(128)S(1)} %pad_add_fusion.where_ref, f32[8,32,128]{2,1,0:T(8,128)S(1)} %bitcast.9, f32[8,32,128]{2,1,0:T(8,128)S(1)} %collective-permute-done.12.refs_1_, f32[8,32,128]{2,1,0:T(8,128)S(1)} %collective-permute-done.13.refs_2_, f32[8,32,128]{2,1,0:T(8,128)S(1)} %collective-permute-done.14.refs_3_, ...), custom_call_target="tpu_custom_call" | custom-call | tf_op jit(solution)/shard_map/pallas_call | solution.py:655
  (12 shorter events, 0.1 us)
Async XLA Ops:
  1.8 7.4 %collective-permute-start = (f32[8,8,512]{2,1,0:T(8,128)S(1)}, f32[8,8,512]{2,1,0:T(8,128)S(1)}, u32[]{:S(2)}, u32[]{:S(2)}) collective-permute-start(f32[8,8,512]{2,1,0:T(8,128)S(1)} %get-tuple-element.50), channel_id=1, source_target_pairs={{0,1},{1,0},{2,3},{3,2},{4,5},{5,4},{6,7},{7,6},{8,9},{9,8},{10,11... | collective-permute-start | bytes 393224 | tf_op jit(solution)/shard_map/ppermute | solution.py:701
  4.4 4.8 %collective-permute-start.1 = (f32[8,8,512]{2,1,0:T(8,128)S(1)}, f32[8,8,512]{2,1,0:T(8,128)S(1)}, u32[]{:S(2)}, u32[]{:S(2)}) collective-permute-start(f32[8,8,512]{2,1,0:T(8,128)S(1)} %get-tuple-element.51), channel_id=1, source_target_pairs={{0,32},{1,2},{2,1},{3,4},{4,3},{5,6},{6,5},{7,8},{8,7},{9,10},{10,... | collective-permute-start | bytes 393224 | tf_op jit(solution)/shard_map/ppermute | solution.py:702
  5.3 4.4 %collective-permute-start.2 = (f32[8,8,512]{2,1,0:T(8,128)S(1)}, f32[8,8,512]{2,1,0:T(8,128)S(1)}, u32[]{:S(2)}, u32[]{:S(2)}) collective-permute-start(f32[8,8,512]{2,1,0:T(8,128)S(1)} %get-tuple-element.52), channel_id=1, source_target_pairs={{0,1},{1,0},{2,3},{3,2},{4,5},{5,4},{6,7},{7,6},{8,9},{9,8},{10,11... | collective-permute-start | bytes 393224 | tf_op jit(solution)/shard_map/ppermute | solution.py:696
  6.4 3.7 %collective-permute-start.3 = (f32[8,8,512]{2,1,0:T(8,128)S(1)}, f32[8,8,512]{2,1,0:T(8,128)S(1)}, u32[]{:S(2)}, u32[]{:S(2)}) collective-permute-start(f32[8,8,512]{2,1,0:T(8,128)S(1)} %get-tuple-element.53), channel_id=1, source_target_pairs={{0,32},{1,33},{2,34},{3,35},{4,36},{5,37},{6,38},{7,39},{8,40},{9,... | collective-permute-start | bytes 393224 | tf_op jit(solution)/shard_map/ppermute | solution.py:695
  10.2 5.4 %collective-permute-start.5 = (f32[4,8,512]{2,1,0:T(8,128)S(1)}, f32[4,8,512]{2,1,0:T(8,128)S(1)}, u32[]{:S(2)}, u32[]{:S(2)}) collective-permute-start(f32[4,8,512]{2,1,0:T(8,128)S(1)} %get-tuple-element.99), channel_id=1, source_target_pairs={{0,1},{1,0},{2,3},{3,2},{4,5},{5,4},{6,7},{7,6},{8,9},{9,8},{10,11... | collective-permute-start | bytes 196616 | tf_op jit(solution)/shard_map/ppermute | solution.py:696
  11.0 4.7 %collective-permute-start.4 = (f32[4,8,512]{2,1,0:T(8,128)S(1)}, f32[4,8,512]{2,1,0:T(8,128)S(1)}, u32[]{:S(2)}, u32[]{:S(2)}) collective-permute-start(f32[4,8,512]{2,1,0:T(8,128)S(1)} %get-tuple-element.100), channel_id=1, source_target_pairs={{0,32},{1,33},{2,34},{3,35},{4,36},{5,37},{6,38},{7,39},{8,40},{9,... | collective-permute-start | bytes 196616 | tf_op jit(solution)/shard_map/ppermute | solution.py:695
  17.3 7.1 %collective-permute-start.6 = (f32[5,8,512]{2,1,0:T(8,128)S(1)}, f32[5,8,512]{2,1,0:T(8,128)S(1)}, u32[]{:S(2)}, u32[]{:S(2)}) collective-permute-start(f32[5,8,512]{2,1,0:T(8,128)S(1)} %get-tuple-element.74), channel_id=1, source_target_pairs={{0,1},{1,0},{2,3},{3,2},{4,5},{5,4},{6,7},{7,6},{8,9},{9,8},{10,11... | collective-permute-start | bytes 245768 | tf_op jit(solution)/shard_map/ppermute | solution.py:701
  18.5 5.9 %collective-permute-start.7 = (f32[5,8,512]{2,1,0:T(8,128)S(1)}, f32[5,8,512]{2,1,0:T(8,128)S(1)}, u32[]{:S(2)}, u32[]{:S(2)}) collective-permute-start(f32[5,8,512]{2,1,0:T(8,128)S(1)} %get-tuple-element.75), channel_id=1, source_target_pairs={{0,32},{1,2},{2,1},{3,4},{4,3},{5,6},{6,5},{7,8},{8,7},{9,10},{10,... | collective-permute-start | bytes 245768 | tf_op jit(solution)/shard_map/ppermute | solution.py:702
  20.3 4.2 %collective-permute-start.8 = (f32[5,8,512]{2,1,0:T(8,128)S(1)}, f32[5,8,512]{2,1,0:T(8,128)S(1)}, u32[]{:S(2)}, u32[]{:S(2)}) collective-permute-start(f32[5,8,512]{2,1,0:T(8,128)S(1)} %get-tuple-element.76), channel_id=1, source_target_pairs={{0,1},{1,0},{2,3},{3,2},{4,5},{5,4},{6,7},{7,6},{8,9},{9,8},{10,11... | collective-permute-start | bytes 245768 | tf_op jit(solution)/shard_map/ppermute | solution.py:696
  20.3 5.1 %collective-permute-start.9 = (f32[5,8,512]{2,1,0:T(8,128)S(1)}, f32[5,8,512]{2,1,0:T(8,128)S(1)}, u32[]{:S(2)}, u32[]{:S(2)}) collective-permute-start(f32[5,8,512]{2,1,0:T(8,128)S(1)} %get-tuple-element.77), channel_id=1, source_target_pairs={{0,32},{1,33},{2,34},{3,35},{4,36},{5,37},{6,38},{7,39},{8,40},{9,... | collective-permute-start | bytes 245768 | tf_op jit(solution)/shard_map/ppermute | solution.py:695
  25.5 4.3 %collective-permute-start.11 = (f32[7,8,512]{2,1,0:T(8,128)S(1)}, f32[7,8,512]{2,1,0:T(8,128)S(1)}, u32[]{:S(2)}, u32[]{:S(2)}) collective-permute-start(f32[7,8,512]{2,1,0:T(8,128)S(1)} %maximum_maximum_fusion), channel_id=1, source_target_pairs={{0,1},{1,0},{2,3},{3,2},{4,5},{5,4},{6,7},{7,6},{8,9},{9,8},{10,11... | collective-permute-start | bytes 344072 | tf_op jit(solution)/shard_map/ppermute | solution.py:696
  25.6 4.5 %collective-permute-start.10 = (f32[7,8,512]{2,1,0:T(8,128)S(1)}, f32[7,8,512]{2,1,0:T(8,128)S(1)}, u32[]{:S(2)}, u32[]{:S(2)}) collective-permute-start(f32[7,8,512]{2,1,0:T(8,128)S(1)} %maximum_maximum_fusion), channel_id=1, source_target_pairs={{0,32},{1,33},{2,34},{3,35},{4,36},{5,37},{6,38},{7,39},{8,40},{9,... | collective-permute-start | bytes 344072 | tf_op jit(solution)/shard_map/ppermute | solution.py:695
  47.8 7.9 %collective-permute-start.14 = (f32[8,32,128]{2,1,0:T(8,128)S(1)}, f32[8,32,128]{2,1,0:T(8,128)S(1)}, u32[]{:S(2)}, u32[]{:S(2)}) collective-permute-start(f32[8,32,128]{2,1,0:T(8,128)S(1)} %bitcast.5), channel_id=1, source_target_pairs={{0,192},{1,193},{2,194},{3,195},{4,196},{5,197},{6,198},{7,199},{8... | collective-permute-start | bytes 393224 | tf_op jit(solution)/shard_map/ppermute | solution.py:758
  47.9 11.3 %collective-permute-start.13 = (f32[8,32,128]{2,1,0:T(8,128)S(1)}, f32[8,32,128]{2,1,0:T(8,128)S(1)}, u32[]{:S(2)}, u32[]{:S(2)}) collective-permute-start(f32[8,32,128]{2,1,0:T(8,128)S(1)} %bitcast.6), channel_id=1, source_target_pairs={{0,128},{1,129},{2,130},{3,131},{4,132},{5,133},{6,134},{7,135},{8... | collective-permute-start | bytes 393224 | tf_op jit(solution)/shard_map/ppermute | solution.py:758
  51.0 8.2 %collective-permute-start.12 = (f32[8,32,128]{2,1,0:T(8,128)S(1)}, f32[8,32,128]{2,1,0:T(8,128)S(1)}, u32[]{:S(2)}, u32[]{:S(2)}) collective-permute-start(f32[8,32,128]{2,1,0:T(8,128)S(1)} %bitcast.7), channel_id=1, source_target_pairs={{0,64},{1,65},{2,66},{3,67},{4,68},{5,69},{6,70},{7,71},{8,72},{9,... | collective-permute-start | bytes 393224 | tf_op jit(solution)/shard_map/ppermute | solution.py:758
  51.2 8.9 %collective-permute-start.15 = (f32[8,32,128]{2,1,0:T(8,128)S(1)}, f32[8,32,128]{2,1,0:T(8,128)S(1)}, u32[]{:S(2)}, u32[]{:S(2)}) collective-permute-start(f32[8,32,128]{2,1,0:T(8,128)S(1)} %bitcast.8), channel_id=1, source_target_pairs={{0,32},{1,33},{2,34},{3,35},{4,36},{5,37},{6,38},{7,39},{8,40},{9,... | collective-permute-start | bytes 393224 | tf_op jit(solution)/shard_map/ppermute | solution.py:760
  55.7 4.5 %collective-permute-start.18 = (f32[8,32,128]{2,1,0:T(8,128)S(1)}, f32[8,32,128]{2,1,0:T(8,128)S(1)}, u32[]{:S(2)}, u32[]{:S(2)}) collective-permute-start(f32[8,32,128]{2,1,0:T(8,128)S(1)} %collective-permute-done.14.refs_3_), channel_id=1, source_target_pairs={{0,32},{1,33},{2,34},{3,35},{4,36},{5,37},{6,38},{7,39},{8,40},{9,... | collective-permute-start | bytes 393224 | tf_op jit(solution)/shard_map/ppermute | solution.py:760
  59.2 1.3 %collective-permute-start.17 = (f32[8,32,128]{2,1,0:T(8,128)S(1)}, f32[8,32,128]{2,1,0:T(8,128)S(1)}, u32[]{:S(2)}, u32[]{:S(2)}) collective-permute-start(f32[8,32,128]{2,1,0:T(8,128)S(1)} %collective-permute-done.13.refs_2_), channel_id=1, source_target_pairs={{0,32},{1,33},{2,34},{3,35},{4,36},{5,37},{6,38},{7,39},{8,40},{9,... | collective-permute-start | bytes 393224 | tf_op jit(solution)/shard_map/ppermute | solution.py:760
  59.2 1.8 %collective-permute-start.16 = (f32[8,32,128]{2,1,0:T(8,128)S(1)}, f32[8,32,128]{2,1,0:T(8,128)S(1)}, u32[]{:S(2)}, u32[]{:S(2)}) collective-permute-start(f32[8,32,128]{2,1,0:T(8,128)S(1)} %collective-permute-done.12.refs_1_), channel_id=1, source_target_pairs={{0,32},{1,33},{2,34},{3,35},{4,36},{5,37},{6,38},{7,39},{8,40},{9,... | collective-permute-start | bytes 393224 | tf_op jit(solution)/shard_map/ppermute | solution.py:760
